TPU v7x, 32 devices: a whole 2x2x4 slice. The times are simulated.
32 devices in a mesh: row: 4 (over y, x), col: 2 (over core), layer: 4 (over z).
Axes of the slice: x: 2, y: 2, z: 4, core: 2. Of those that a mesh axis runs over, the one named last changes fastest.
Arguments:
- values: float32 [2048, 2048], P('row', ('layer', 'col')), may hold values from 0 to 2
- a_pattern: int32 [16, 16], P('row', ('layer', 'col')), may hold values from 0 to 1, as said below
- c_pattern: int32 [16, 16], P('row', ('layer', 'col')), may hold values 0 or 1
- prune_mask: int32 [2048, 2048], P('row', ('layer', 'col')), may hold values 0 or 1
Outputs:
- inflated: float32 [2048, 2048], P('row', ('layer', 'col'))
Inputs may be any that keep to these rules, and one draw needn't show every extreme that they name: `a_pattern`: 1 marks a present tile, 0 an absent one. `c_pattern`: 1 marks a kept tile. `prune_mask`: 1 marks a surviving entry.
All inputs are finite; a program needn't handle non-finite values. No bound on the sum of `c_pattern` or of `prune_mask` on one device may be relied on, other than what follows from the above.
Results may differ from a plain program's by a relative error of at most 0.001.
Values may be sent and summed in bfloat16 or wider, within the bound.
No kernel may reach another device: no remote copies, remote signals or barrier semaphores. Data moves between devices by JAX's collectives and lax.ppermute only.
A program may use at most 64 MiB of HBM per device.

v0:
```python
import jax
import jax.numpy as jnp
from jax import lax
from jax.sharding import PartitionSpec as P

TILE = 128


epsilon = 1e-09


def spread_tiles(pattern):
    tile_rows, tile_cols = pattern.shape
    blocked = jnp.broadcast_to(
        pattern.astype(jnp.float32)[:, None, :, None], (tile_rows, TILE, tile_cols, TILE)
    )
    return blocked.reshape(tile_rows * TILE, tile_cols * TILE)


def on_device(values, a_pattern, c_pattern, prune_mask):
    local_rows = values.shape[0]
    local_cols = values.shape[1]
    layer_count = lax.axis_size("layer")
    total_rows = local_rows * lax.axis_size("row")
    sparse = (values * spread_tiles(a_pattern)).astype(jnp.bfloat16)
    left_panel = lax.all_gather(sparse, "col", axis=1, tiled=True)
    all_rows = lax.all_gather(sparse, "row", axis=0, tiled=True)
    stacked = all_rows.reshape(layer_count, total_rows // layer_count, local_cols)
    regrouped = lax.all_to_all(stacked, "layer", split_axis=0, concat_axis=2, tiled=True)
    partial_value = jnp.dot(left_panel, regrouped[0], preferred_element_type=jnp.float32)
    summed = lax.psum_scatter(partial_value, "layer", scatter_dimension=1, tiled=True)
    kept_tiles = summed * spread_tiles(c_pattern)
    squares = kept_tiles * kept_tiles * prune_mask.astype(jnp.float32)
    column_sums = lax.psum(jnp.sum(squares, axis=0), "row")
    return total_rows * squares / (column_sums[None, :] + epsilon)


def solution(mesh):
    placed = (
        P("row", ("layer", "col")),
        P("row", ("layer", "col")),
        P("row", ("layer", "col")),
        P("row", ("layer", "col")),
    )
    return jax.shard_map(
        on_device, mesh=mesh, in_specs=placed, out_specs=P("row", ("layer", "col")), check_vma=False
    )
```

profile of v0, /device:TPU:0, one launch (start us, length us, event | category | flops | bytes accessed | tf_op | source)
XLA Modules:
  0.0 133.0 jit_solution(17889375073066092072)
XLA Ops:
  6.5 0.0 all-gather.2.cloned.1.call-start
  6.5 0.7 convert_element_type.12
  7.2 0.1 copy.9
  7.3 0.2 broadcast_in_dim.4
  7.5 1.8 %fusion.2 = bf16[512,256]{1,0:T(8,128)(2,1)} fusion(f32[512,256]{1,0:T(8,128)} %param.4, f32[64,8,2,128]{3,2,1,0:T(2,128)S(1)} %bitcast.29), kind=kLoop, calls=%fused_computation.4 | loop fusion | flops 262144 | bytes 1310720 | tf_op jit(solution)/shard_map/convert_element_type | solution.py:25
  9.3 0.0 all-gather.2.cloned.1.call-update
  9.4 29.5 %all-gather.2.cloned.1.call-done = bf16[2048,256]{1,0:T(8,128)(2,1)} async-done(((bf16[512,256]{1,0:T(8,128)(2,1)}), bf16[2048,256]{1,0:T(8,128)(2,1)}) %all-gather.2.cloned.1.call-update) | async-done | bytes 1048592 | tf_op jit(solution)/shard_map/all_gather | solution.py:27
  38.8 4.6 %all-to-all-start = ((bf16[4,512,256]{2,1,0:T(8,128)(2,1)}), bf16[4,512,256]{2,1,0:T(8,128)(2,1)S(1)}, u32[]{:S(2)}, u32[]{:S(2)}) async-start(bf16[4,512,256]{2,1,0:T(8,128)(2,1)} %bitcast.30), calls=%async_computation | async-start | bytes 2097152 | tf_op jit(solution)/shard_map/all_to_all | solution.py:29
  43.4 0.0 reduce-scatter.2.cloned.1.call-start
  43.4 0.0 copy-done
  43.4 2.2 %all_gather.6 = bf16[512,512]{1,0:T(8,128)(2,1)S(1)} all-gather(bf16[512,256]{1,0:T(8,128)(2,1)S(1)} %copy-done), channel_id=1, replica_groups=mesh['row'=4,'col'=2,'layer'=4] {'col'}, dimensions={1}, use_global_device_ids=true | all-gather | bytes 786432 | tf_op jit(solution)/shard_map/all_gather | solution.py:26
  45.6 23.5 %all-to-all-done = bf16[4,512,256]{2,1,0:T(8,128)(2,1)S(1)} async-done(((bf16[4,512,256]{2,1,0:T(8,128)(2,1)}), bf16[4,512,256]{2,1,0:T(8,128)(2,1)S(1)}, u32[]{:S(2)}, u32[]{:S(2)}) %all-to-all-start) | async-done | bytes 1048608 | tf_op jit(solution)/shard_map/all_to_all | solution.py:29
  69.2 0.5 copy.10
  69.7 0.0 copy-start.3
  69.7 2.1 %fusion.4 = f32[512,1024]{1,0:T(8,128)} fusion(bf16[512,512]{1,0:T(8,128)(2,1)S(1)} %all_gather.6, bf16[512,1024]{0,1:T(8,128)(2,1)S(1)} %bitcast.27), kind=kOutput, calls=%fused_computation.8 | convolution fusion | flops 536870912 | bytes 3670016 | tf_op jit(solution)/shard_map/dot_general | solution.py:30
  71.8 0.0 reduce-scatter.2.cloned.1.call-update
  71.8 0.0 copy-done.3
  71.8 0.1 copy.11
  71.9 42.0 %reduce-scatter.2.cloned.1.call-done = f32[512,256]{1,0:T(8,128)} async-done(((f32[512,1024]{1,0:T(8,128)}), f32[512,256]{1,0:T(8,128)}) %reduce-scatter.2.cloned.1.call-update) | async-done | bytes 524304 | tf_op jit(solution)/shard_map/reduce_scatter | solution.py:31
  114.0 0.2 broadcast_in_dim.5
  114.2 0.0 copy-done.1
  114.2 1.2 fusion.3
  115.3 9.9 %psum.7 = f32[256]{0:T(256)S(1)} all-reduce(f32[256]{0:T(256)S(1)} %fusion.3), channel_id=1, replica_groups=mesh['row'=4,'col'=2,'layer'=4] {'row'}, use_global_device_ids=true, to_apply=%region_2.0 | all-reduce | flops 256 | bytes 2048 | tf_op jit(solution)/shard_map/psum | solution.py:34
  125.2 0.9 multiply_divide_fusion
  (6 shorter events, 0.0 us)
Async XLA Ops:
  6.5 32.3 %all-gather.2.cloned.1.call-start = ((), (), s32[]{:S(2)}) async-start(), calls=%async_computation.2 | async-start | bytes 1310720 | tf_op jit(solution)/shard_map/all_gather | solution.py:27
  9.3 34.1 %copy-start = (bf16[512,256]{1,0:T(8,128)(2,1)S(1)}, bf16[512,256]{1,0:T(8,128)(2,1)}, u32[]{:S(2)}) copy-start(bf16[512,256]{1,0:T(8,128)(2,1)} %fusion.2) | copy-start | bytes 786436
  38.8 30.3 %all-to-all-start = ((bf16[4,512,256]{2,1,0:T(8,128)(2,1)}), bf16[4,512,256]{2,1,0:T(8,128)(2,1)S(1)}, u32[]{:S(2)}, u32[]{:S(2)}) async-start(bf16[4,512,256]{2,1,0:T(8,128)(2,1)} %bitcast.30), calls=%async_computation | async-start | bytes 2097152 | tf_op jit(solution)/shard_map/all_to_all | solution.py:29
  43.4 70.5 %reduce-scatter.2.cloned.1.call-start = ((), (), s32[]{:S(2)}) async-start(), calls=%async_computation.3 | async-start | bytes 2621440 | tf_op jit(solution)/shard_map/reduce_scatter | solution.py:31
  69.7 2.1 %copy-start.3 = (s32[4,2]{0,1:T(2,128)S(1)}, s32[4,2]{0,1:T(2,128)}, u32[]{:S(2)}) copy-start(s32[4,2]{0,1:T(2,128)} %param.6) | copy-start | bytes 100
  71.8 42.4 %copy-start.1 = (s32[512,256]{1,0:T(8,128)S(1)}, s32[512,256]{1,0:T(8,128)}, u32[]{:S(2)}) copy-start(s32[512,256]{1,0:T(8,128)} %param.7) | copy-start | bytes 1572868
  114.0 11.3 %copy-start.2 = (f32[512,256]{1,0:T(8,128)S(1)}, f32[512,256]{1,0:T(8,128)}, u32[]{:S(2)}) copy-start(f32[512,256]{1,0:T(8,128)} %reduce-scatter.2.cloned.1.call-done) | copy-start | bytes 1572868
Sparse Core Ops, SparseCore 0:
  9.5 29.3 all-gather.1
  71.9 41.9 reduce-scatter.1
where the time goes:
time: 133 us
  waiting for transfers between devices  95.1 us (72%)
  between operations  13.4 us (10%)
  blocking collectives  12.1 us (9%)
  starting transfers between devices  4.6 us (3%)
  other arithmetic  4.56 us (3%)
  matrix products  2.07 us (2%)
    reduce_scatter x1, waiting for transfers between devices, on_device(): lax.psum_scatter(partial_value, 'layer', scatter_dimension=1, tiled=True)  42 us
    all_gather x1, waiting for transfers between devices, on_device(): all_rows = lax.all_gather(sparse, 'row', axis=0, tiled=True)  29.5 us
    all_to_all x1, waiting for transfers between devices, on_device(): lax.all_to_all(stacked, 'layer', split_axis=0, concat_axis=2, tiled=True)  23.5 us
    psum x1, blocking collectives, on_device(): column_sums = lax.psum(jnp.sum(squares, axis=0), 'row')  9.89 us
    all_to_all x1, starting transfers between devices, on_device(): lax.all_to_all(stacked, 'layer', split_axis=0, concat_axis=2, tiled=True)  4.6 us
  transfers between devices with their start and end apart: 3, of which 3 were waited for; matrix products, arithmetic and copies ran while one was open for 0% of the time, Pallas kernels for 0%

commit v1 on v0

v1 whole, which is shorter than its diff:
```python
import functools

import jax
import jax.numpy as jnp
from jax import lax
from jax.experimental import pallas as pl
from jax.experimental.pallas import tpu as pltpu
from jax.sharding import PartitionSpec as P

TILE = 128


epsilon = 1e-09

VMEM = pl.BlockSpec(memory_space=pltpu.VMEM)
SMEM = pl.BlockSpec(memory_space=pltpu.SMEM)


def spread_tiles(pattern):
    tile_rows, tile_cols = pattern.shape
    blocked = jnp.broadcast_to(
        pattern.astype(jnp.float32)[:, None, :, None], (tile_rows, TILE, tile_cols, TILE)
    )
    return blocked.reshape(tile_rows * TILE, tile_cols * TILE)


def tile_slices(shape):
    for i in range(shape[0] // TILE):
        for j in range(shape[1] // TILE):
            yield i, j, (slice(i * TILE, (i + 1) * TILE), slice(j * TILE, (j + 1) * TILE))


def sparse_kernel(values_ref, pattern_ref, out_ref):
    for i, j, at in tile_slices(values_ref.shape):
        present = pattern_ref[i, j].astype(jnp.float32)
        out_ref[at] = (values_ref[at] * present).astype(jnp.bfloat16)


def most_kernel(place_ref, *refs):
    left, right = refs[:6], refs[6:10]
    total_ref, own_ref, other_ref, panel_ref = refs[10:]
    lead, parity = place_ref[0], place_ref[1]
    half = left[0].shape[1]
    for s in range(4):
        panel_ref[s ^ lead] = right[s][...]
    total = None
    for s in range(3):
        for side in range(2):
            rows = pl.ds(pl.multiple_of((parity ^ side) * half, half), half)
            part = jnp.dot(left[2 * s + side][...], panel_ref[s, rows, :], preferred_element_type=jnp.float32)
            total = part if total is None else total + part
    total_ref[...] = total
    own_ref[...] = panel_ref[3, pl.ds(pl.multiple_of(parity * half, half), half), :]
    other_ref[...] = panel_ref[3, pl.ds(pl.multiple_of((1 - parity) * half, half), half), :]


def squares_kernel(pattern_ref, total_ref, left_own_ref, left_other_ref, own_ref, other_ref, mask_ref, squares_ref, sums_ref):
    product = total_ref[...] + jnp.dot(left_own_ref[...], own_ref[...], preferred_element_type=jnp.float32)
    product = product + jnp.dot(left_other_ref[...], other_ref[...], preferred_element_type=jnp.float32)
    columns = [None] * (product.shape[1] // TILE)
    for i, j, at in tile_slices(product.shape):
        kept = product[at] * pattern_ref[i, j].astype(jnp.float32)
        squares = kept * kept * mask_ref[at].astype(jnp.float32)
        squares_ref[at] = squares
        part = jnp.sum(squares.reshape(TILE // 8, 8, TILE), axis=0)
        columns[j] = part if columns[j] is None else columns[j] + part
    for j, part in enumerate(columns):
        sums_ref[:, j * TILE:(j + 1) * TILE] = part


def scale_kernel(total_rows, squares_ref, *refs):
    sums, out_ref = refs[:-1], refs[-1]
    column = sums[0][...]
    for other in sums[1:]:
        column = column + other[...]
    column = jnp.sum(column, axis=0, keepdims=True) + epsilon
    out_ref[...] = total_rows * squares_ref[...] / column


def swap(x, axis, size, s):
    return lax.ppermute(x, axis, [(i, i ^ s) for i in range(size)])


def after(x, *others):
    return lax.optimization_barrier((x,) + others)[0]


def call(kernel, out_shape, in_specs, flops=0, size=0, **options):
    return pl.pallas_call(
        kernel,
        out_shape=out_shape,
        in_specs=in_specs,
        out_specs=jax.tree.map(lambda _: VMEM, out_shape),
        compiler_params=pltpu.CompilerParams(vmem_limit_bytes=16 * 2**20),
        cost_estimate=pl.CostEstimate(flops=flops, bytes_accessed=size, transcendentals=0),
        **options,
    )


def on_small_mesh(values, a_pattern, c_pattern, prune_mask):
    rows, cols = values.shape
    row, col, layer = lax.axis_index("row"), lax.axis_index("col"), lax.axis_index("layer")
    total_rows = rows * 4
    block = jax.ShapeDtypeStruct((rows, cols), jnp.bfloat16)
    full = jax.ShapeDtypeStruct((rows, cols), jnp.float32)

    own = call(sparse_kernel, block, [VMEM, SMEM], size=6 * rows * cols)(values, a_pattern)
    near2 = swap(own, "layer", 4, 2)
    near1 = swap(own, "layer", 4, 1)
    right = [own] + [swap(own, "row", 4, s) for s in (1, 2, 3)]
    own_late = after(own, near2)
    ends = lax.ppermute(near2, "layer", [(2, 3), (1, 0)])
    middle = lax.ppermute(own_late, "layer", [(1, 2), (2, 1)])
    left = []
    for x in (own, near1, near2):
        left += [x, swap(x, "col", 2, 1)]
    place = jnp.stack([row ^ layer, col]).astype(jnp.int32)
    total, last_own, last_other = call(
        most_kernel,
        [full, jax.ShapeDtypeStruct((cols, cols), jnp.bfloat16), jax.ShapeDtypeStruct((cols, cols), jnp.bfloat16)],
        [SMEM] + [VMEM] * 10,
        flops=2 * rows * cols * 3 * rows,
        size=2 * 10 * rows * cols,
        scratch_shapes=[pltpu.VMEM((4, rows, cols), jnp.bfloat16)],
    )(place, *left, *right)
    far = ends + middle
    far_other = swap(far, "col", 2, 1)
    squares, sums = call(
        squares_kernel,
        [full, jax.ShapeDtypeStruct((8, cols), jnp.float32)],
        [SMEM] + [VMEM] * 6,
        flops=2 * rows * cols * rows,
        size=16 * rows * cols,
    )(c_pattern, total, far, far_other, last_own, last_other, prune_mask)
    others = [swap(sums, "row", 4, s) for s in (1, 2, 3)]
    return call(
        functools.partial(scale_kernel, total_rows), full, [VMEM] * 5, flops=4 * rows * cols, size=8 * rows * cols
    )(squares, sums, *others)


def on_any_mesh(values, a_pattern, c_pattern, prune_mask):
    total_rows = values.shape[0] * lax.axis_size("row")
    sparse = (values * spread_tiles(a_pattern)).astype(jnp.bfloat16)
    left = lax.all_gather(sparse, ("layer", "col"), axis=1, tiled=True)
    right = lax.all_gather(sparse, "row", axis=0, tiled=True)
    kept = jnp.dot(left, right, preferred_element_type=jnp.float32) * spread_tiles(c_pattern)
    squares = kept * kept * prune_mask.astype(jnp.float32)
    column_sums = lax.psum(jnp.sum(squares, axis=0), "row")
    return total_rows * squares / (column_sums[None, :] + epsilon)


def solution(mesh):
    spec = P("row", ("layer", "col"))
    sizes = tuple(mesh.shape[name] for name in ("row", "col", "layer"))
    on_device = on_small_mesh if sizes == (4, 2, 4) else on_any_mesh
    return jax.shard_map(on_device, mesh=mesh, in_specs=(spec,) * 4, out_specs=spec, check_vma=False)
```

time: 133 us -> 45.8 us (0.34)
  the two profiles are of different devices: /device:TPU:0 before, /device:TPU:18 now
where the time goes in v1:
time: 45.8 us; the launch traced here: 45.6 us
  waiting for transfers between devices  23.1 us (50%)
  starting transfers between devices  16.1 us (35%)
  Pallas kernels  3.52 us (8%)
  local copies, waits for them, and re-layouts  2.58 us (6%)
    ppermute x12, waiting for transfers between devices, swap(): return lax.ppermute(x, axis, [(i, i ^ s) for i in range(size)])  21 us
    ppermute x12, starting transfers between devices, swap(): return lax.ppermute(x, axis, [(i, i ^ s) for i in range(size)])  9.1 us
    ppermute x1, starting transfers between devices, on_small_mesh(): middle = lax.ppermute(own_late, 'layer', [(1, 2), (2, 1)])  4.44 us
    ppermute x1, starting transfers between devices, on_small_mesh(): ends = lax.ppermute(near2, 'layer', [(2, 3), (1, 0)])  2.61 us
    unnamed x8, local copies, waits for them, and re-layouts  2.58 us
    ppermute x1, waiting for transfers between devices, on_small_mesh(): ends = lax.ppermute(near2, 'layer', [(2, 3), (1, 0)])  1.85 us
    pallas_call x1, Pallas kernels, on_small_mesh(): call(most_kernel, [full, jax.ShapeDtypeStruct((cols, cols), jnp.bfloat16)...  1.19 us
  transfers between devices with their start and end apart: 14, of which 9 were waited for; matrix products, arithmetic and copies ran while one was open for 1% of the time, Pallas kernels for 3%

profile of v1, /device:TPU:18, one launch (start us, length us, event | category | flops | bytes accessed | tf_op | source)
XLA Modules:
  0.0 45.6 jit_solution(5008809942381575561)
XLA Ops:
  0.0 0.8 %copy.5.pattern_ref = s32[4,2]{1,0:T(4,128)S(1)} copy(s32[4,2]{0,1:T(2,128)} %param.5) | data formatting | bytes 64 | tf_op args[1]
  0.8 1.0 %copy-done = f32[512,256]{1,0:T(8,128)S(1)} copy-done((f32[512,256]{1,0:T(8,128)S(1)}, f32[512,256]{1,0:T(8,128)}, u32[]{:S(2)}) %copy-start) | copy-done | bytes 524312
  1.8 0.6 %shard_map.46.refs_0_.refs_6_ = bf16[512,256]{1,0:T(8,128)(2,1)S(1)} custom-call(f32[512,256]{1,0:T(8,128)S(1)} %copy-done, s32[4,2]{1,0:T(4,128)S(1)} %copy.5.pattern_ref), custom_call_target="tpu_custom_call" | custom-call | bytes 786432 | tf_op jit(solution)/shard_map/pallas_call | solution.py:107
  2.4 0.4 collective-permute-start.3
  2.8 1.6 %collective-permute-start.1 = (bf16[512,256]{1,0:T(8,128)(2,1)S(1)}, bf16[512,256]{1,0:T(8,128)(2,1)S(1)}, u32[]{:S(2)}, u32[]{:S(2)}) collective-permute-start(bf16[512,256]{1,0:T(8,128)(2,1)S(1)} %shard_map.46.refs_0_.refs_6_), channel_id=1, source_target_pairs={{0,1},{1,0},{2,3},{3,2},{4,5},{5,4},{6,7},{7,6},{8,9},{9,8},{10,11... | collective-permute-start | bytes 786440 | tf_op jit(solution)/shard_map/ppermute | solution.py:81
  4.4 9.6 %collective-permute-done.3.refs_4_ = bf16[512,256]{1,0:T(8,128)(2,1)S(1)} collective-permute-done((bf16[512,256]{1,0:T(8,128)(2,1)S(1)}, bf16[512,256]{1,0:T(8,128)(2,1)S(1)}, u32[]{:S(2)}, u32[]{:S(2)}) %collective-permute-start.3) | collective-permute-done | bytes 262176 | tf_op jit(solution)/shard_map/ppermute | solution.py:81
  14.1 4.4 %collective-permute-start.9 = (bf16[512,256]{1,0:T(8,128)(2,1)S(1)}, bf16[512,256]{1,0:T(8,128)(2,1)S(1)}, u32[]{:S(2)}, u32[]{:S(2)}) collective-permute-start(bf16[512,256]{1,0:T(8,128)(2,1)S(1)} %shard_map.46.refs_0_.refs_6_), channel_id=1, source_target_pairs={{1,2},{2,1},{5,6},{6,5},{9,10},{10,9},{13,14},{14,13},{17,18},{18,... | collective-permute-start | bytes 786440 | tf_op jit(solution)/shard_map/ppermute | solution.py:113
  18.5 2.6 %collective-permute-start.8 = (bf16[512,256]{1,0:T(8,128)(2,1)S(1)}, bf16[512,256]{1,0:T(8,128)(2,1)S(1)}, u32[]{:S(2)}, u32[]{:S(2)}) collective-permute-start(bf16[512,256]{1,0:T(8,128)(2,1)S(1)} %collective-permute-done.3.refs_4_), channel_id=1, source_target_pairs={{2,3},{1,0},{6,7},{5,4},{10,11},{9,8},{14,15},{13,12},{18,19},{17,... | collective-permute-start | bytes 786440 | tf_op jit(solution)/shard_map/ppermute | solution.py:112
  21.1 0.6 %collective-permute-start.5 = (bf16[512,256]{1,0:T(8,128)(2,1)S(1)}, bf16[512,256]{1,0:T(8,128)(2,1)S(1)}, u32[]{:S(2)}, u32[]{:S(2)}) collective-permute-start(bf16[512,256]{1,0:T(8,128)(2,1)S(1)} %shard_map.46.refs_0_.refs_6_), channel_id=1, source_target_pairs={{0,8},{8,0},{16,24},{24,16},{1,9},{9,1},{17,25},{25,17},{2,10},{10... | collective-permute-start | bytes 786440 | tf_op jit(solution)/shard_map/ppermute | solution.py:81
  21.7 1.5 %collective-permute-start.6 = (bf16[512,256]{1,0:T(8,128)(2,1)S(1)}, bf16[512,256]{1,0:T(8,128)(2,1)S(1)}, u32[]{:S(2)}, u32[]{:S(2)}) collective-permute-start(bf16[512,256]{1,0:T(8,128)(2,1)S(1)} %shard_map.46.refs_0_.refs_6_), channel_id=1, source_target_pairs={{0,16},{8,24},{16,0},{24,8},{1,17},{9,25},{17,1},{25,9},{2,18},{10... | collective-permute-start | bytes 786440 | tf_op jit(solution)/shard_map/ppermute | solution.py:81
  23.2 1.4 %collective-permute-start.7 = (bf16[512,256]{1,0:T(8,128)(2,1)S(1)}, bf16[512,256]{1,0:T(8,128)(2,1)S(1)}, u32[]{:S(2)}, u32[]{:S(2)}) collective-permute-start(bf16[512,256]{1,0:T(8,128)(2,1)S(1)} %shard_map.46.refs_0_.refs_6_), channel_id=1, source_target_pairs={{0,24},{8,16},{16,8},{24,0},{1,25},{9,17},{17,9},{25,1},{2,26},{10... | collective-permute-start | bytes 786440 | tf_op jit(solution)/shard_map/ppermute | solution.py:81
  25.0 1.9 %collective-permute-done.8 = bf16[512,256]{1,0:T(8,128)(2,1)S(1)} collective-permute-done((bf16[512,256]{1,0:T(8,128)(2,1)S(1)}, bf16[512,256]{1,0:T(8,128)(2,1)S(1)}, u32[]{:S(2)}, u32[]{:S(2)}) %collective-permute-start.8) | collective-permute-done | bytes 262176 | tf_op jit(solution)/shard_map/ppermute | solution.py:112
  26.9 3.5 %collective-permute-done.5.refs_7_ = bf16[512,256]{1,0:T(8,128)(2,1)S(1)} collective-permute-done((bf16[512,256]{1,0:T(8,128)(2,1)S(1)}, bf16[512,256]{1,0:T(8,128)(2,1)S(1)}, u32[]{:S(2)}, u32[]{:S(2)}) %collective-permute-start.5) | collective-permute-done | bytes 262176 | tf_op jit(solution)/shard_map/ppermute | solution.py:81
  30.4 0.7 %copy-done.2 = s32[4,2]{0,1:T(2,128)S(1)} copy-done((s32[4,2]{0,1:T(2,128)S(1)}, s32[4,2]{0,1:T(2,128)}, u32[]{:S(2)}) %copy-start.2) | copy-done | bytes 56
  31.2 2.8 %collective-permute-done.6.refs_8_ = bf16[512,256]{1,0:T(8,128)(2,1)S(1)} collective-permute-done((bf16[512,256]{1,0:T(8,128)(2,1)S(1)}, bf16[512,256]{1,0:T(8,128)(2,1)S(1)}, u32[]{:S(2)}, u32[]{:S(2)}) %collective-permute-start.6) | collective-permute-done | bytes 262176 | tf_op jit(solution)/shard_map/ppermute | solution.py:81
  34.1 1.6 %collective-permute-done.7.refs_9_ = bf16[512,256]{1,0:T(8,128)(2,1)S(1)} collective-permute-done((bf16[512,256]{1,0:T(8,128)(2,1)S(1)}, bf16[512,256]{1,0:T(8,128)(2,1)S(1)}, u32[]{:S(2)}, u32[]{:S(2)}) %collective-permute-start.7) | collective-permute-done | bytes 262176 | tf_op jit(solution)/shard_map/ppermute | solution.py:81
  35.7 1.2 %shard_map.47 = (f32[512,256]{1,0:T(8,128)S(1)}, bf16[256,256]{1,0:T(8,128)(2,1)S(1)}, bf16[256,256]{1,0:T(8,128)(2,1)S(1)}) custom-call(s32[2]{0:T(128)S(1)} %pad_add_fusion.place_ref, bf16[512,256]{1,0:T(8,128)(2,1)S(1)} %shard_map.46.refs_0_.refs_6_, bf16[512,256]{1,0:T(8,128)(2,1)S(1)} %collective-permute-done.refs_1_, ...), custom_call_target="tpu_custom_call" | custom-call | flops 402653184 | bytes 2621440 | tf_op jit(solution)/shard_map/pallas_call | solution.py:118
  36.9 0.9 %shard_map.48 = (f32[512,256]{1,0:T(8,128)S(1)}, f32[8,256]{1,0:T(8,128)S(1)}) custom-call(s32[4,2]{1,0:T(4,128)S(1)} %copy.6.pattern_ref, f32[512,256]{1,0:T(8,128)S(1)} %get-tuple-element.11.total_ref, bf16[512,256]{1,0:T(8,128)(2,1)S(1)} %add.3.left_own_ref, bf16[512,256]{1,0:T(8,128)(2,1)S(1)} %collective-permute-done.10.left_other_ref, ...), custom_call_target="tpu_custom_call" | custom-call | flops 134217728 | bytes 2097152 | tf_op jit(solution)/shard_map/pallas_call | solution.py:128
  37.8 0.9 %collective-permute-start.11 = (f32[8,256]{1,0:T(8,128)S(1)}, f32[8,256]{1,0:T(8,128)S(1)}, u32[]{:S(2)}, u32[]{:S(2)}) collective-permute-start(f32[8,256]{1,0:T(8,128)S(1)} %get-tuple-element.16.refs_0_), channel_id=1, source_target_pairs={{0,8},{8,0},{16,24},{24,16},{1,9},{9,1},{17,25},{25,17},{2,10},{10... | collective-permute-start | bytes 24584 | tf_op jit(solution)/shard_map/ppermute | solution.py:81
  38.7 1.5 %collective-permute-start.12 = (f32[8,256]{1,0:T(8,128)S(1)}, f32[8,256]{1,0:T(8,128)S(1)}, u32[]{:S(2)}, u32[]{:S(2)}) collective-permute-start(f32[8,256]{1,0:T(8,128)S(1)} %get-tuple-element.16.refs_0_), channel_id=1, source_target_pairs={{0,16},{8,24},{16,0},{24,8},{1,17},{9,25},{17,1},{25,9},{2,18},{10... | collective-permute-start | bytes 24584 | tf_op jit(solution)/shard_map/ppermute | solution.py:81
  40.2 1.2 %collective-permute-start.13 = (f32[8,256]{1,0:T(8,128)S(1)}, f32[8,256]{1,0:T(8,128)S(1)}, u32[]{:S(2)}, u32[]{:S(2)}) collective-permute-start(f32[8,256]{1,0:T(8,128)S(1)} %get-tuple-element.16.refs_0_), channel_id=1, source_target_pairs={{0,24},{8,16},{16,8},{24,0},{1,25},{9,17},{17,9},{25,1},{2,26},{10... | collective-permute-start | bytes 24584 | tf_op jit(solution)/shard_map/ppermute | solution.py:81
  41.5 0.8 %collective-permute-done.12.refs_2_ = f32[8,256]{1,0:T(8,128)S(1)} collective-permute-done((f32[8,256]{1,0:T(8,128)S(1)}, f32[8,256]{1,0:T(8,128)S(1)}, u32[]{:S(2)}, u32[]{:S(2)}) %collective-permute-start.12) | collective-permute-done | bytes 8224 | tf_op jit(solution)/shard_map/ppermute | solution.py:81
  42.3 2.4 %collective-permute-done.13.refs_3_ = f32[8,256]{1,0:T(8,128)S(1)} collective-permute-done((f32[8,256]{1,0:T(8,128)S(1)}, f32[8,256]{1,0:T(8,128)S(1)}, u32[]{:S(2)}, u32[]{:S(2)}) %collective-permute-start.13) | collective-permute-done | bytes 8224 | tf_op jit(solution)/shard_map/ppermute | solution.py:81
  44.8 0.8 %shard_map.49 = f32[512,256]{1,0:T(8,128)} custom-call(f32[512,256]{1,0:T(8,128)S(1)} %get-tuple-element.15.squares_ref, f32[8,256]{1,0:T(8,128)S(1)} %get-tuple-element.16.refs_0_, f32[8,256]{1,0:T(8,128)S(1)} %collective-permute-done.11.refs_1_, f32[8,256]{1,0:T(8,128)S(1)} %collective-permute-done.12.refs_2_, f32[8,256]{1,0:T(8,128)S(1)} %collective-permute-done.13.refs_3_), custom_call_target="tpu_custom_call" | custom-call | flops 524288 | bytes 1048576 | tf_op jit(solution)/shard_map/pallas_call | solution.py:136
  (18 shorter events, 0.7 us)
Async XLA Ops:
  0.8 1.0 %copy-start = (f32[512,256]{1,0:T(8,128)S(1)}, f32[512,256]{1,0:T(8,128)}, u32[]{:S(2)}) copy-start(f32[512,256]{1,0:T(8,128)} %values_ref.1) | copy-start | bytes 1572868
  2.4 11.6 %collective-permute-start.3 = (bf16[512,256]{1,0:T(8,128)(2,1)S(1)}, bf16[512,256]{1,0:T(8,128)(2,1)S(1)}, u32[]{:S(2)}, u32[]{:S(2)}) collective-permute-start(bf16[512,256]{1,0:T(8,128)(2,1)S(1)} %shard_map.46.refs_0_.refs_6_), channel_id=1, source_target_pairs={{0,2},{1,3},{2,0},{3,1},{4,6},{5,7},{6,4},{7,5},{8,10},{9,11},{10,... | collective-permute-start | bytes 786440 | tf_op jit(solution)/shard_map/ppermute | solution.py:81
  2.8 18.9 %collective-permute-start.1 = (bf16[512,256]{1,0:T(8,128)(2,1)S(1)}, bf16[512,256]{1,0:T(8,128)(2,1)S(1)}, u32[]{:S(2)}, u32[]{:S(2)}) collective-permute-start(bf16[512,256]{1,0:T(8,128)(2,1)S(1)} %shard_map.46.refs_0_.refs_6_), channel_id=1, source_target_pairs={{0,1},{1,0},{2,3},{3,2},{4,5},{5,4},{6,7},{7,6},{8,9},{9,8},{10,11... | collective-permute-start | bytes 786440 | tf_op jit(solution)/shard_map/ppermute | solution.py:81
  4.4 18.8 %collective-permute-start = (bf16[512,256]{1,0:T(8,128)(2,1)S(1)}, bf16[512,256]{1,0:T(8,128)(2,1)S(1)}, u32[]{:S(2)}, u32[]{:S(2)}) collective-permute-start(bf16[512,256]{1,0:T(8,128)(2,1)S(1)} %shard_map.46.refs_0_.refs_6_), channel_id=1, source_target_pairs={{0,4},{4,0},{1,5},{5,1},{2,6},{6,2},{3,7},{7,3},{8,12},{12,8},{9,1... | collective-permute-start | bytes 786440 | tf_op jit(solution)/shard_map/ppermute | solution.py:81
  14.1 10.9 %collective-permute-start.9 = (bf16[512,256]{1,0:T(8,128)(2,1)S(1)}, bf16[512,256]{1,0:T(8,128)(2,1)S(1)}, u32[]{:S(2)}, u32[]{:S(2)}) collective-permute-start(bf16[512,256]{1,0:T(8,128)(2,1)S(1)} %shard_map.46.refs_0_.refs_6_), channel_id=1, source_target_pairs={{1,2},{2,1},{5,6},{6,5},{9,10},{10,9},{13,14},{14,13},{17,18},{18,... | collective-permute-start | bytes 786440 | tf_op jit(solution)/shard_map/ppermute | solution.py:113
  18.5 8.3 %collective-permute-start.8 = (bf16[512,256]{1,0:T(8,128)(2,1)S(1)}, bf16[512,256]{1,0:T(8,128)(2,1)S(1)}, u32[]{:S(2)}, u32[]{:S(2)}) collective-permute-start(bf16[512,256]{1,0:T(8,128)(2,1)S(1)} %collective-permute-done.3.refs_4_), channel_id=1, source_target_pairs={{2,3},{1,0},{6,7},{5,4},{10,11},{9,8},{14,15},{13,12},{18,19},{17,... | collective-permute-start | bytes 786440 | tf_op jit(solution)/shard_map/ppermute | solution.py:112
  21.1 9.3 %collective-permute-start.5 = (bf16[512,256]{1,0:T(8,128)(2,1)S(1)}, bf16[512,256]{1,0:T(8,128)(2,1)S(1)}, u32[]{:S(2)}, u32[]{:S(2)}) collective-permute-start(bf16[512,256]{1,0:T(8,128)(2,1)S(1)} %shard_map.46.refs_0_.refs_6_), channel_id=1, source_target_pairs={{0,8},{8,0},{16,24},{24,16},{1,9},{9,1},{17,25},{25,17},{2,10},{10... | collective-permute-start | bytes 786440 | tf_op jit(solution)/shard_map/ppermute | solution.py:81
  21.7 12.4 %collective-permute-start.6 = (bf16[512,256]{1,0:T(8,128)(2,1)S(1)}, bf16[512,256]{1,0:T(8,128)(2,1)S(1)}, u32[]{:S(2)}, u32[]{:S(2)}) collective-permute-start(bf16[512,256]{1,0:T(8,128)(2,1)S(1)} %shard_map.46.refs_0_.refs_6_), channel_id=1, source_target_pairs={{0,16},{8,24},{16,0},{24,8},{1,17},{9,25},{17,1},{25,9},{2,18},{10... | collective-permute-start | bytes 786440 | tf_op jit(solution)/shard_map/ppermute | solution.py:81
  23.2 12.5 %collective-permute-start.7 = (bf16[512,256]{1,0:T(8,128)(2,1)S(1)}, bf16[512,256]{1,0:T(8,128)(2,1)S(1)}, u32[]{:S(2)}, u32[]{:S(2)}) collective-permute-start(bf16[512,256]{1,0:T(8,128)(2,1)S(1)} %shard_map.46.refs_0_.refs_6_), channel_id=1, source_target_pairs={{0,24},{8,16},{16,8},{24,0},{1,25},{9,17},{17,9},{25,1},{2,26},{10... | collective-permute-start | bytes 786440 | tf_op jit(solution)/shard_map/ppermute | solution.py:81
  25.0 10.7 %collective-permute-start.4 = (bf16[512,256]{1,0:T(8,128)(2,1)S(1)}, bf16[512,256]{1,0:T(8,128)(2,1)S(1)}, u32[]{:S(2)}, u32[]{:S(2)}) collective-permute-start(bf16[512,256]{1,0:T(8,128)(2,1)S(1)} %collective-permute-done.3.refs_4_), channel_id=1, source_target_pairs={{0,4},{4,0},{1,5},{5,1},{2,6},{6,2},{3,7},{7,3},{8,12},{12,8},{9,1... | collective-permute-start | bytes 786440 | tf_op jit(solution)/shard_map/ppermute | solution.py:81
  26.8 8.9 %collective-permute-start.2 = (bf16[512,256]{1,0:T(8,128)(2,1)S(1)}, bf16[512,256]{1,0:T(8,128)(2,1)S(1)}, u32[]{:S(2)}, u32[]{:S(2)}) collective-permute-start(bf16[512,256]{1,0:T(8,128)(2,1)S(1)} %collective-permute-done.1.refs_2_), channel_id=1, source_target_pairs={{0,4},{4,0},{1,5},{5,1},{2,6},{6,2},{3,7},{7,3},{8,12},{12,8},{9,1... | collective-permute-start | bytes 786440 | tf_op jit(solution)/shard_map/ppermute | solution.py:81
  30.4 6.5 %collective-permute-start.10 = (bf16[512,256]{1,0:T(8,128)(2,1)S(1)}, bf16[512,256]{1,0:T(8,128)(2,1)S(1)}, u32[]{:S(2)}, u32[]{:S(2)}) collective-permute-start(bf16[512,256]{1,0:T(8,128)(2,1)S(1)} %add.3.left_own_ref), channel_id=1, source_target_pairs={{0,4},{4,0},{1,5},{5,1},{2,6},{6,2},{3,7},{7,3},{8,12},{12,8},{9,1... | collective-permute-start | bytes 786440 | tf_op jit(solution)/shard_map/ppermute | solution.py:81
  30.4 0.7 %copy-start.2 = (s32[4,2]{0,1:T(2,128)S(1)}, s32[4,2]{0,1:T(2,128)}, u32[]{:S(2)}) copy-start(s32[4,2]{0,1:T(2,128)} %param.6) | copy-start | bytes 100
  31.2 5.7 %copy-start.1 = (s32[512,256]{1,0:T(8,128)S(1)}, s32[512,256]{1,0:T(8,128)}, u32[]{:S(2)}) copy-start(s32[512,256]{1,0:T(8,128)} %mask_ref.1) | copy-start | bytes 1572868
  37.8 3.7 %collective-permute-start.11 = (f32[8,256]{1,0:T(8,128)S(1)}, f32[8,256]{1,0:T(8,128)S(1)}, u32[]{:S(2)}, u32[]{:S(2)}) collective-permute-start(f32[8,256]{1,0:T(8,128)S(1)} %get-tuple-element.16.refs_0_), channel_id=1, source_target_pairs={{0,8},{8,0},{16,24},{24,16},{1,9},{9,1},{17,25},{25,17},{2,10},{10... | collective-permute-start | bytes 24584 | tf_op jit(solution)/shard_map/ppermute | solution.py:81
  38.7 3.7 %collective-permute-start.12 = (f32[8,256]{1,0:T(8,128)S(1)}, f32[8,256]{1,0:T(8,128)S(1)}, u32[]{:S(2)}, u32[]{:S(2)}) collective-permute-start(f32[8,256]{1,0:T(8,128)S(1)} %get-tuple-element.16.refs_0_), channel_id=1, source_target_pairs={{0,16},{8,24},{16,0},{24,8},{1,17},{9,25},{17,1},{25,9},{2,18},{10... | collective-permute-start | bytes 24584 | tf_op jit(solution)/shard_map/ppermute | solution.py:81
  40.2 4.5 %collective-permute-start.13 = (f32[8,256]{1,0:T(8,128)S(1)}, f32[8,256]{1,0:T(8,128)S(1)}, u32[]{:S(2)}, u32[]{:S(2)}) collective-permute-start(f32[8,256]{1,0:T(8,128)S(1)} %get-tuple-element.16.refs_0_), channel_id=1, source_target_pairs={{0,24},{8,16},{16,8},{24,0},{1,25},{9,17},{17,9},{25,1},{2,26},{10... | collective-permute-start | bytes 24584 | tf_op jit(solution)/shard_map/ppermute | solution.py:81

commit v2 on v1

v2 whole, which is shorter than its diff:
```python
import functools

import jax
import jax.numpy as jnp
from jax import lax
from jax.experimental import pallas as pl
from jax.experimental.pallas import tpu as pltpu
from jax.sharding import PartitionSpec as P

TILE = 128


epsilon = 1e-09

VMEM = pl.BlockSpec(memory_space=pltpu.VMEM)


def spread_tiles(pattern):
    tile_rows, tile_cols = pattern.shape
    blocked = jnp.broadcast_to(
        pattern.astype(jnp.float32)[:, None, :, None], (tile_rows, TILE, tile_cols, TILE)
    )
    return blocked.reshape(tile_rows * TILE, tile_cols * TILE)


def times_tiles(x, pattern):
    tile_rows, tile_cols = pattern.shape
    tiles = x.reshape(tile_rows, TILE, tile_cols, TILE) * pattern[:, None, :, None]
    return tiles.reshape(x.shape)


def most_kernel(*refs):
    here, there, right = refs[:3], refs[3:6], refs[6:10]
    total_ref, own_ref, other_ref, panel_ref = refs[10:]
    parity = lax.axis_index("col")
    lead = lax.axis_index("row") ^ lax.axis_index("layer")
    half = here[0].shape[1]
    for s in range(4):
        panel_ref[s ^ lead] = right[s][...]
    total = None
    for s in range(3):
        for side, block in enumerate((here[s], there[s])):
            rows = pl.ds(pl.multiple_of((parity ^ side) * half, half), half)
            part = jnp.dot(block[...], panel_ref[s, rows, :], preferred_element_type=jnp.float32)
            total = part if total is None else total + part
    total_ref[...] = total
    own_ref[...] = panel_ref[3, pl.ds(pl.multiple_of(parity * half, half), half), :]
    other_ref[...] = panel_ref[3, pl.ds(pl.multiple_of((1 - parity) * half, half), half), :]


def squares_kernel(total_ref, left_own_ref, left_other_ref, own_ref, other_ref, weight_ref, squares_ref, sums_ref):
    product = total_ref[...] + jnp.dot(left_own_ref[...], own_ref[...], preferred_element_type=jnp.float32)
    product = product + jnp.dot(left_other_ref[...], other_ref[...], preferred_element_type=jnp.float32)
    squares = product * product * weight_ref[...]
    squares_ref[...] = squares
    rows, cols = squares.shape
    sums_ref[...] = jnp.sum(squares.reshape(rows // 8, 8, cols), axis=0)


def scale_kernel(total_rows, squares_ref, *refs):
    sums, out_ref = refs[:-1], refs[-1]
    column = sums[0][...]
    for other in sums[1:]:
        column = column + other[...]
    column = jnp.sum(column, axis=0, keepdims=True) + epsilon
    out_ref[...] = total_rows * squares_ref[...] / column


def swap(x, axis, size, s):
    return lax.ppermute(x, axis, [(i, i ^ s) for i in range(size)])


def call(kernel, out_shape, in_specs, flops=0, size=0, **options):
    return pl.pallas_call(
        kernel,
        out_shape=out_shape,
        in_specs=in_specs,
        out_specs=jax.tree.map(lambda _: VMEM, out_shape),
        compiler_params=pltpu.CompilerParams(vmem_limit_bytes=16 * 2**20),
        cost_estimate=pl.CostEstimate(flops=flops, bytes_accessed=size, transcendentals=0),
        **options,
    )


def on_small_mesh(values, a_pattern, c_pattern, prune_mask):
    rows, cols = values.shape
    total_rows = rows * 4
    full = jax.ShapeDtypeStruct((rows, cols), jnp.float32)

    own = times_tiles(values, a_pattern.astype(jnp.float32)).astype(jnp.bfloat16)
    near2 = swap(own, "layer", 4, 2)
    near1 = swap(own, "layer", 4, 1)
    right = [own] + [swap(own, "row", 4, s) for s in (1, 2, 3)]
    weight = times_tiles(prune_mask.astype(jnp.float32), c_pattern.astype(jnp.float32))
    near2, *right, near1, weight = lax.optimization_barrier((near2, *right, near1, weight))
    ends = lax.ppermute(near2, "layer", [(2, 3), (1, 0)])
    far = lax.ppermute(right[0], "layer", [(1, 2), (2, 1)])
    here = [own, near1, near2]
    there = [swap(x, "col", 2, 1) for x in here]
    ends, far = lax.optimization_barrier((ends, far))
    far = ends + far
    far_other = swap(far, "col", 2, 1)
    total, last_own, last_other = call(
        most_kernel,
        [full, jax.ShapeDtypeStruct((cols, cols), jnp.bfloat16), jax.ShapeDtypeStruct((cols, cols), jnp.bfloat16)],
        [VMEM] * 10,
        flops=2 * rows * cols * 3 * rows,
        size=2 * 10 * rows * cols,
        scratch_shapes=[pltpu.VMEM((4, rows, cols), jnp.bfloat16)],
    )(*here, *there, *right)
    squares, sums = call(
        squares_kernel,
        [full, jax.ShapeDtypeStruct((8, cols), jnp.float32)],
        [VMEM] * 6,
        flops=2 * rows * cols * rows,
        size=16 * rows * cols,
    )(total, far, far_other, last_own, last_other, weight)
    others = [swap(sums, "row", 4, s) for s in (1, 2, 3)]
    return call(
        functools.partial(scale_kernel, total_rows), full, [VMEM] * 5, flops=4 * rows * cols, size=8 * rows * cols
    )(squares, sums, *others)


def on_any_mesh(values, a_pattern, c_pattern, prune_mask):
    total_rows = values.shape[0] * lax.axis_size("row")
    sparse = (values * spread_tiles(a_pattern)).astype(jnp.bfloat16)
    left = lax.all_gather(sparse, ("layer", "col"), axis=1, tiled=True)
    right = lax.all_gather(sparse, "row", axis=0, tiled=True)
    kept = jnp.dot(left, right, preferred_element_type=jnp.float32) * spread_tiles(c_pattern)
    squares = kept * kept * prune_mask.astype(jnp.float32)
    column_sums = lax.psum(jnp.sum(squares, axis=0), "row")
    return total_rows * squares / (column_sums[None, :] + epsilon)


def solution(mesh):
    spec = P("row", ("layer", "col"))
    sizes = tuple(mesh.shape[name] for name in ("row", "col", "layer"))
    on_device = on_small_mesh if sizes == (4, 2, 4) else on_any_mesh
    return jax.shard_map(on_device, mesh=mesh, in_specs=(spec,) * 4, out_specs=spec, check_vma=False)
```

time: 45.8 us -> 40 us (0.87)
  the two profiles are of different devices: /device:TPU:18 before, /device:TPU:8 now
where the time goes in v2:
time: 40 us; the launch traced here: 39.8 us
  waiting for transfers between devices  19.4 us (48%)
  starting transfers between devices  16.9 us (42%)
  Pallas kernels  1.81 us (5%)
  other arithmetic  0.95 us (2%)
  local copies, waits for them, and re-layouts  0.63 us (2%)
    ppermute x12, waiting for transfers between devices, swap(): return lax.ppermute(x, axis, [(i, i ^ s) for i in range(size)])  15.2 us
    ppermute x12, starting transfers between devices, swap(): return lax.ppermute(x, axis, [(i, i ^ s) for i in range(size)])  10.9 us
    ppermute x1, waiting for transfers between devices, on_small_mesh(): far = lax.ppermute(right[0], 'layer', [(1, 2), (2, 1)])  4.15 us
    ppermute x1, starting transfers between devices, on_small_mesh(): far = lax.ppermute(right[0], 'layer', [(1, 2), (2, 1)])  3.45 us
    ppermute x1, starting transfers between devices, on_small_mesh(): ends = lax.ppermute(near2, 'layer', [(2, 3), (1, 0)])  2.63 us
    pallas_call x1, Pallas kernels, on_small_mesh(): call(functools.partial(scale_kernel, total_rows), full, [VMEM] * 5, flops...  0.85 us
  transfers between devices with their start and end apart: 14, of which 7 were waited for; matrix products, arithmetic and copies ran while one was open for 1% of the time, Pallas kernels for 2%

profile of v2, /device:TPU:8, one launch (start us, length us, event | category | flops | bytes accessed | tf_op | source)
XLA Modules:
  0.0 39.8 jit_solution(13013776412158856010)
XLA Ops:
  0.0 0.7 %convert_element_type.12 = f32[4,2]{0,1:T(2,128)S(1)} convert(s32[4,2]{0,1:T(2,128)} %param.5) | non-fusion elementwise | flops 8 | bytes 64 | tf_op jit(solution)/shard_map/convert_element_type | solution.py:90
  0.8 0.2 mul.22
  1.2 2.7 %collective-permute-start = (bf16[512,256]{1,0:T(8,128)(2,1)S(1)}, bf16[512,256]{1,0:T(8,128)(2,1)S(1)}, u32[]{:S(2)}, u32[]{:S(2)}) collective-permute-start(bf16[512,256]{1,0:T(8,128)(2,1)S(1)} %fusion.refs_0_.refs_6_), channel_id=1, source_target_pairs={{0,2},{1,3},{2,0},{3,1},{4,6},{5,7},{6,4},{7,5},{8,10},{9,11},{10,... | collective-permute-start | bytes 786440 | tf_op jit(solution)/shard_map/ppermute | solution.py:70
  3.8 1.5 %collective-permute-start.1 = (bf16[512,256]{1,0:T(8,128)(2,1)S(1)}, bf16[512,256]{1,0:T(8,128)(2,1)S(1)}, u32[]{:S(2)}, u32[]{:S(2)}) collective-permute-start(bf16[512,256]{1,0:T(8,128)(2,1)S(1)} %fusion.refs_0_.refs_6_), channel_id=1, source_target_pairs={{0,8},{8,0},{16,24},{24,16},{1,9},{9,1},{17,25},{25,17},{2,10},{10... | collective-permute-start | bytes 786440 | tf_op jit(solution)/shard_map/ppermute | solution.py:70
  5.3 1.5 %collective-permute-start.2 = (bf16[512,256]{1,0:T(8,128)(2,1)S(1)}, bf16[512,256]{1,0:T(8,128)(2,1)S(1)}, u32[]{:S(2)}, u32[]{:S(2)}) collective-permute-start(bf16[512,256]{1,0:T(8,128)(2,1)S(1)} %fusion.refs_0_.refs_6_), channel_id=1, source_target_pairs={{0,16},{8,24},{16,0},{24,8},{1,17},{9,25},{17,1},{25,9},{2,18},{10... | collective-permute-start | bytes 786440 | tf_op jit(solution)/shard_map/ppermute | solution.py:70
  6.8 0.5 %collective-permute-start.3 = (bf16[512,256]{1,0:T(8,128)(2,1)S(1)}, bf16[512,256]{1,0:T(8,128)(2,1)S(1)}, u32[]{:S(2)}, u32[]{:S(2)}) collective-permute-start(bf16[512,256]{1,0:T(8,128)(2,1)S(1)} %fusion.refs_0_.refs_6_), channel_id=1, source_target_pairs={{0,24},{8,16},{16,8},{24,0},{1,25},{9,17},{17,9},{25,1},{2,26},{10... | collective-permute-start | bytes 786440 | tf_op jit(solution)/shard_map/ppermute | solution.py:70
  7.3 0.4 %collective-permute-start.4 = (bf16[512,256]{1,0:T(8,128)(2,1)S(1)}, bf16[512,256]{1,0:T(8,128)(2,1)S(1)}, u32[]{:S(2)}, u32[]{:S(2)}) collective-permute-start(bf16[512,256]{1,0:T(8,128)(2,1)S(1)} %fusion.refs_0_.refs_6_), channel_id=1, source_target_pairs={{0,1},{1,0},{2,3},{3,2},{4,5},{5,4},{6,7},{7,6},{8,9},{9,8},{10,11... | collective-permute-start | bytes 786440 | tf_op jit(solution)/shard_map/ppermute | solution.py:70
  7.9 0.2 mul.25
  8.2 6.8 %collective-permute-done.refs_2_ = bf16[512,256]{1,0:T(8,128)(2,1)S(1)} collective-permute-done((bf16[512,256]{1,0:T(8,128)(2,1)S(1)}, bf16[512,256]{1,0:T(8,128)(2,1)S(1)}, u32[]{:S(2)}, u32[]{:S(2)}) %collective-permute-start) | collective-permute-done | bytes 262176 | tf_op jit(solution)/shard_map/ppermute | solution.py:70
  14.9 3.5 %collective-permute-done.2.refs_8_ = bf16[512,256]{1,0:T(8,128)(2,1)S(1)} collective-permute-done((bf16[512,256]{1,0:T(8,128)(2,1)S(1)}, bf16[512,256]{1,0:T(8,128)(2,1)S(1)}, u32[]{:S(2)}, u32[]{:S(2)}) %collective-permute-start.2) | collective-permute-done | bytes 262176 | tf_op jit(solution)/shard_map/ppermute | solution.py:70
  18.4 2.6 %collective-permute-start.8 = (bf16[512,256]{1,0:T(8,128)(2,1)S(1)}, bf16[512,256]{1,0:T(8,128)(2,1)S(1)}, u32[]{:S(2)}, u32[]{:S(2)}) collective-permute-start(bf16[512,256]{1,0:T(8,128)(2,1)S(1)} %collective-permute-done.refs_2_), channel_id=1, source_target_pairs={{2,3},{1,0},{6,7},{5,4},{10,11},{9,8},{14,15},{13,12},{18,19},{17,... | collective-permute-start | bytes 786440 | tf_op jit(solution)/shard_map/ppermute | solution.py:96
  21.1 3.4 %collective-permute-start.9 = (bf16[512,256]{1,0:T(8,128)(2,1)S(1)}, bf16[512,256]{1,0:T(8,128)(2,1)S(1)}, u32[]{:S(2)}, u32[]{:S(2)}) collective-permute-start(bf16[512,256]{1,0:T(8,128)(2,1)S(1)} %fusion.refs_0_.refs_6_), channel_id=1, source_target_pairs={{1,2},{2,1},{5,6},{6,5},{9,10},{10,9},{13,14},{14,13},{17,18},{18,... | collective-permute-start | bytes 786440 | tf_op jit(solution)/shard_map/ppermute | solution.py:97
  24.6 0.5 %collective-permute-start.6 = (bf16[512,256]{1,0:T(8,128)(2,1)S(1)}, bf16[512,256]{1,0:T(8,128)(2,1)S(1)}, u32[]{:S(2)}, u32[]{:S(2)}) collective-permute-start(bf16[512,256]{1,0:T(8,128)(2,1)S(1)} %collective-permute-done.4.refs_1_), channel_id=1, source_target_pairs={{0,4},{4,0},{1,5},{5,1},{2,6},{6,2},{3,7},{7,3},{8,12},{12,8},{9,1... | collective-permute-start | bytes 786440 | tf_op jit(solution)/shard_map/ppermute | solution.py:70
  25.2 4.2 %collective-permute-done.9 = bf16[512,256]{1,0:T(8,128)(2,1)S(1)} collective-permute-done((bf16[512,256]{1,0:T(8,128)(2,1)S(1)}, bf16[512,256]{1,0:T(8,128)(2,1)S(1)}, u32[]{:S(2)}, u32[]{:S(2)}) %collective-permute-start.9) | collective-permute-done | bytes 262176 | tf_op jit(solution)/shard_map/ppermute | solution.py:97
  29.5 0.7 %shard_map.46 = (f32[512,256]{1,0:T(8,128)S(1)}, bf16[256,256]{1,0:T(8,128)(2,1)S(1)}, bf16[256,256]{1,0:T(8,128)(2,1)S(1)}) custom-call(bf16[512,256]{1,0:T(8,128)(2,1)S(1)} %fusion.refs_0_.refs_6_, bf16[512,256]{1,0:T(8,128)(2,1)S(1)} %collective-permute-done.4.refs_1_, bf16[512,256]{1,0:T(8,128)(2,1)S(1)} %collective-permute-done.refs_2_, ...), custom_call_target="tpu_custom_call" | custom-call | flops 402653184 | bytes 2621440 | tf_op jit(solution)/shard_map/pallas_call | solution.py:103
  30.2 0.8 %collective-permute-done.10.left_other_ref = bf16[512,256]{1,0:T(8,128)(2,1)S(1)} collective-permute-done((bf16[512,256]{1,0:T(8,128)(2,1)S(1)}, bf16[512,256]{1,0:T(8,128)(2,1)S(1)}, u32[]{:S(2)}, u32[]{:S(2)}) %collective-permute-start.10) | collective-permute-done | bytes 262176 | tf_op jit(solution)/shard_map/ppermute | solution.py:70
  31.0 0.3 shard_map.47
  31.3 1.6 %collective-permute-start.11 = (f32[8,256]{1,0:T(8,128)S(1)}, f32[8,256]{1,0:T(8,128)S(1)}, u32[]{:S(2)}, u32[]{:S(2)}) collective-permute-start(f32[8,256]{1,0:T(8,128)S(1)} %get-tuple-element.32.refs_0_), channel_id=1, source_target_pairs={{0,8},{8,0},{16,24},{24,16},{1,9},{9,1},{17,25},{25,17},{2,10},{10... | collective-permute-start | bytes 24584 | tf_op jit(solution)/shard_map/ppermute | solution.py:70
  32.9 1.5 %collective-permute-start.12 = (f32[8,256]{1,0:T(8,128)S(1)}, f32[8,256]{1,0:T(8,128)S(1)}, u32[]{:S(2)}, u32[]{:S(2)}) collective-permute-start(f32[8,256]{1,0:T(8,128)S(1)} %get-tuple-element.32.refs_0_), channel_id=1, source_target_pairs={{0,16},{8,24},{16,0},{24,8},{1,17},{9,25},{17,1},{25,9},{2,18},{10... | collective-permute-start | bytes 24584 | tf_op jit(solution)/shard_map/ppermute | solution.py:70
  34.4 0.4 %collective-permute-start.13 = (f32[8,256]{1,0:T(8,128)S(1)}, f32[8,256]{1,0:T(8,128)S(1)}, u32[]{:S(2)}, u32[]{:S(2)}) collective-permute-start(f32[8,256]{1,0:T(8,128)S(1)} %get-tuple-element.32.refs_0_), channel_id=1, source_target_pairs={{0,24},{8,16},{16,8},{24,0},{1,25},{9,17},{17,9},{25,1},{2,26},{10... | collective-permute-start | bytes 24584 | tf_op jit(solution)/shard_map/ppermute | solution.py:70
  34.8 0.2 collective-permute-done.11.refs_1_
  35.0 1.5 %collective-permute-done.12.refs_2_ = f32[8,256]{1,0:T(8,128)S(1)} collective-permute-done((f32[8,256]{1,0:T(8,128)S(1)}, f32[8,256]{1,0:T(8,128)S(1)}, u32[]{:S(2)}, u32[]{:S(2)}) %collective-permute-start.12) | collective-permute-done | bytes 8224 | tf_op jit(solution)/shard_map/ppermute | solution.py:70
  36.6 2.4 %collective-permute-done.13.refs_3_ = f32[8,256]{1,0:T(8,128)S(1)} collective-permute-done((f32[8,256]{1,0:T(8,128)S(1)}, f32[8,256]{1,0:T(8,128)S(1)}, u32[]{:S(2)}, u32[]{:S(2)}) %collective-permute-start.13) | collective-permute-done | bytes 8224 | tf_op jit(solution)/shard_map/ppermute | solution.py:70
  39.0 0.8 %shard_map.48 = f32[512,256]{1,0:T(8,128)} custom-call(f32[512,256]{1,0:T(8,128)S(1)} %get-tuple-element.31.squares_ref, f32[8,256]{1,0:T(8,128)S(1)} %get-tuple-element.32.refs_0_, f32[8,256]{1,0:T(8,128)S(1)} %collective-permute-done.11.refs_1_, f32[8,256]{1,0:T(8,128)S(1)} %collective-permute-done.12.refs_2_, f32[8,256]{1,0:T(8,128)S(1)} %collective-permute-done.13.refs_3_), custom_call_target="tpu_custom_call" | custom-call | flops 524288 | bytes 1048576 | tf_op jit(solution)/shard_map/pallas_call | solution.py:119
  (22 shorter events, 0.7 us)
Async XLA Ops:
  0.0 1.1 %copy-start.1 = (f32[512,256]{1,0:T(8,128)S(1)}, f32[512,256]{1,0:T(8,128)}, u32[]{:S(2)}) copy-start(f32[512,256]{1,0:T(8,128)} %param.4) | copy-start | bytes 1572868
  1.1 6.7 %copy-start.2 = (s32[4,2]{0,1:T(2,128)S(1)}, s32[4,2]{0,1:T(2,128)}, u32[]{:S(2)}) copy-start(s32[4,2]{0,1:T(2,128)} %param.6) | copy-start | bytes 100
  1.2 6.9 %copy-start = (s32[512,256]{1,0:T(8,128)S(1)}, s32[512,256]{1,0:T(8,128)}, u32[]{:S(2)}) copy-start(s32[512,256]{1,0:T(8,128)} %param.7) | copy-start | bytes 1572868
  1.2 13.8 %collective-permute-start = (bf16[512,256]{1,0:T(8,128)(2,1)S(1)}, bf16[512,256]{1,0:T(8,128)(2,1)S(1)}, u32[]{:S(2)}, u32[]{:S(2)}) collective-permute-start(bf16[512,256]{1,0:T(8,128)(2,1)S(1)} %fusion.refs_0_.refs_6_), channel_id=1, source_target_pairs={{0,2},{1,3},{2,0},{3,1},{4,6},{5,7},{6,4},{7,5},{8,10},{9,11},{10,... | collective-permute-start | bytes 786440 | tf_op jit(solution)/shard_map/ppermute | solution.py:70
  3.8 11.1 %collective-permute-start.1 = (bf16[512,256]{1,0:T(8,128)(2,1)S(1)}, bf16[512,256]{1,0:T(8,128)(2,1)S(1)}, u32[]{:S(2)}, u32[]{:S(2)}) collective-permute-start(bf16[512,256]{1,0:T(8,128)(2,1)S(1)} %fusion.refs_0_.refs_6_), channel_id=1, source_target_pairs={{0,8},{8,0},{16,24},{24,16},{1,9},{9,1},{17,25},{25,17},{2,10},{10... | collective-permute-start | bytes 786440 | tf_op jit(solution)/shard_map/ppermute | solution.py:70
  5.3 13.1 %collective-permute-start.2 = (bf16[512,256]{1,0:T(8,128)(2,1)S(1)}, bf16[512,256]{1,0:T(8,128)(2,1)S(1)}, u32[]{:S(2)}, u32[]{:S(2)}) collective-permute-start(bf16[512,256]{1,0:T(8,128)(2,1)S(1)} %fusion.refs_0_.refs_6_), channel_id=1, source_target_pairs={{0,16},{8,24},{16,0},{24,8},{1,17},{9,25},{17,1},{25,9},{2,18},{10... | collective-permute-start | bytes 786440 | tf_op jit(solution)/shard_map/ppermute | solution.py:70
  6.8 11.6 %collective-permute-start.3 = (bf16[512,256]{1,0:T(8,128)(2,1)S(1)}, bf16[512,256]{1,0:T(8,128)(2,1)S(1)}, u32[]{:S(2)}, u32[]{:S(2)}) collective-permute-start(bf16[512,256]{1,0:T(8,128)(2,1)S(1)} %fusion.refs_0_.refs_6_), channel_id=1, source_target_pairs={{0,24},{8,16},{16,8},{24,0},{1,25},{9,17},{17,9},{25,1},{2,26},{10... | collective-permute-start | bytes 786440 | tf_op jit(solution)/shard_map/ppermute | solution.py:70
  7.3 11.1 %collective-permute-start.4 = (bf16[512,256]{1,0:T(8,128)(2,1)S(1)}, bf16[512,256]{1,0:T(8,128)(2,1)S(1)}, u32[]{:S(2)}, u32[]{:S(2)}) collective-permute-start(bf16[512,256]{1,0:T(8,128)(2,1)S(1)} %fusion.refs_0_.refs_6_), channel_id=1, source_target_pairs={{0,1},{1,0},{2,3},{3,2},{4,5},{5,4},{6,7},{7,6},{8,9},{9,8},{10,11... | collective-permute-start | bytes 786440 | tf_op jit(solution)/shard_map/ppermute | solution.py:70
  18.4 6.7 %collective-permute-start.8 = (bf16[512,256]{1,0:T(8,128)(2,1)S(1)}, bf16[512,256]{1,0:T(8,128)(2,1)S(1)}, u32[]{:S(2)}, u32[]{:S(2)}) collective-permute-start(bf16[512,256]{1,0:T(8,128)(2,1)S(1)} %collective-permute-done.refs_2_), channel_id=1, source_target_pairs={{2,3},{1,0},{6,7},{5,4},{10,11},{9,8},{14,15},{13,12},{18,19},{17,... | collective-permute-start | bytes 786440 | tf_op jit(solution)/shard_map/ppermute | solution.py:96
  21.1 8.3 %collective-permute-start.9 = (bf16[512,256]{1,0:T(8,128)(2,1)S(1)}, bf16[512,256]{1,0:T(8,128)(2,1)S(1)}, u32[]{:S(2)}, u32[]{:S(2)}) collective-permute-start(bf16[512,256]{1,0:T(8,128)(2,1)S(1)} %fusion.refs_0_.refs_6_), channel_id=1, source_target_pairs={{1,2},{2,1},{5,6},{6,5},{9,10},{10,9},{13,14},{14,13},{17,18},{18,... | collective-permute-start | bytes 786440 | tf_op jit(solution)/shard_map/ppermute | solution.py:97
  24.5 5.0 %collective-permute-start.5 = (bf16[512,256]{1,0:T(8,128)(2,1)S(1)}, bf16[512,256]{1,0:T(8,128)(2,1)S(1)}, u32[]{:S(2)}, u32[]{:S(2)}) collective-permute-start(bf16[512,256]{1,0:T(8,128)(2,1)S(1)} %fusion.refs_0_.refs_6_), channel_id=1, source_target_pairs={{0,4},{4,0},{1,5},{5,1},{2,6},{6,2},{3,7},{7,3},{8,12},{12,8},{9,1... | collective-permute-start | bytes 786440 | tf_op jit(solution)/shard_map/ppermute | solution.py:70
  24.6 4.9 %collective-permute-start.6 = (bf16[512,256]{1,0:T(8,128)(2,1)S(1)}, bf16[512,256]{1,0:T(8,128)(2,1)S(1)}, u32[]{:S(2)}, u32[]{:S(2)}) collective-permute-start(bf16[512,256]{1,0:T(8,128)(2,1)S(1)} %collective-permute-done.4.refs_1_), channel_id=1, source_target_pairs={{0,4},{4,0},{1,5},{5,1},{2,6},{6,2},{3,7},{7,3},{8,12},{12,8},{9,1... | collective-permute-start | bytes 786440 | tf_op jit(solution)/shard_map/ppermute | solution.py:70
  25.1 4.4 %collective-permute-start.7 = (bf16[512,256]{1,0:T(8,128)(2,1)S(1)}, bf16[512,256]{1,0:T(8,128)(2,1)S(1)}, u32[]{:S(2)}, u32[]{:S(2)}) collective-permute-start(bf16[512,256]{1,0:T(8,128)(2,1)S(1)} %collective-permute-done.refs_2_), channel_id=1, source_target_pairs={{0,4},{4,0},{1,5},{5,1},{2,6},{6,2},{3,7},{7,3},{8,12},{12,8},{9,1... | collective-permute-start | bytes 786440 | tf_op jit(solution)/shard_map/ppermute | solution.py:70
  29.4 1.6 %collective-permute-start.10 = (bf16[512,256]{1,0:T(8,128)(2,1)S(1)}, bf16[512,256]{1,0:T(8,128)(2,1)S(1)}, u32[]{:S(2)}, u32[]{:S(2)}) collective-permute-start(bf16[512,256]{1,0:T(8,128)(2,1)S(1)} %add.3.left_own_ref), channel_id=1, source_target_pairs={{0,4},{4,0},{1,5},{5,1},{2,6},{6,2},{3,7},{7,3},{8,12},{12,8},{9,1... | collective-permute-start | bytes 786440 | tf_op jit(solution)/shard_map/ppermute | solution.py:70
  31.3 3.7 %collective-permute-start.11 = (f32[8,256]{1,0:T(8,128)S(1)}, f32[8,256]{1,0:T(8,128)S(1)}, u32[]{:S(2)}, u32[]{:S(2)}) collective-permute-start(f32[8,256]{1,0:T(8,128)S(1)} %get-tuple-element.32.refs_0_), channel_id=1, source_target_pairs={{0,8},{8,0},{16,24},{24,16},{1,9},{9,1},{17,25},{25,17},{2,10},{10... | collective-permute-start | bytes 24584 | tf_op jit(solution)/shard_map/ppermute | solution.py:70
  32.9 3.7 %collective-permute-start.12 = (f32[8,256]{1,0:T(8,128)S(1)}, f32[8,256]{1,0:T(8,128)S(1)}, u32[]{:S(2)}, u32[]{:S(2)}) collective-permute-start(f32[8,256]{1,0:T(8,128)S(1)} %get-tuple-element.32.refs_0_), channel_id=1, source_target_pairs={{0,16},{8,24},{16,0},{24,8},{1,17},{9,25},{17,1},{25,9},{2,18},{10... | collective-permute-start | bytes 24584 | tf_op jit(solution)/shard_map/ppermute | solution.py:70
  34.4 4.5 %collective-permute-start.13 = (f32[8,256]{1,0:T(8,128)S(1)}, f32[8,256]{1,0:T(8,128)S(1)}, u32[]{:S(2)}, u32[]{:S(2)}) collective-permute-start(f32[8,256]{1,0:T(8,128)S(1)} %get-tuple-element.32.refs_0_), channel_id=1, source_target_pairs={{0,24},{8,16},{16,8},{24,0},{1,25},{9,17},{17,9},{25,1},{2,26},{10... | collective-permute-start | bytes 24584 | tf_op jit(solution)/shard_map/ppermute | solution.py:70

commit v3 on v2

--- a/solution.py
+++ b/solution.py
@@ -30,7 +30,7 @@
 
 
 def most_kernel(*refs):
-    here, there, right = refs[:3], refs[3:6], refs[6:10]
+    right, here, there = refs[:4], refs[4:7], refs[7:10]
     total_ref, own_ref, other_ref, panel_ref = refs[10:]
     parity = lax.axis_index("col")
     lead = lax.axis_index("row") ^ lax.axis_index("layer")
@@ -90,13 +90,17 @@
     own = times_tiles(values, a_pattern.astype(jnp.float32)).astype(jnp.bfloat16)
     near2 = swap(own, "layer", 4, 2)
     near1 = swap(own, "layer", 4, 1)
-    right = [own] + [swap(own, "row", 4, s) for s in (1, 2, 3)]
+    right = [own] + [swap(own, "row", 4, s) for s in (1, 2)]
     weight = times_tiles(prune_mask.astype(jnp.float32), c_pattern.astype(jnp.float32))
-    near2, *right, near1, weight = lax.optimization_barrier((near2, *right, near1, weight))
+    own_there = swap(own, "col", 2, 1)
+    near2, near1, right[1], right[2], own_there, start, weight = lax.optimization_barrier(
+        (near2, near1, right[1], right[2], own_there, own, weight)
+    )
     ends = lax.ppermute(near2, "layer", [(2, 3), (1, 0)])
-    far = lax.ppermute(right[0], "layer", [(1, 2), (2, 1)])
+    far = lax.ppermute(start, "layer", [(1, 2), (2, 1)])
+    right.append(swap(start, "row", 4, 3))
     here = [own, near1, near2]
-    there = [swap(x, "col", 2, 1) for x in here]
+    there = [own_there] + [swap(x, "col", 2, 1) for x in here[1:]]
     ends, far = lax.optimization_barrier((ends, far))
     far = ends + far
     far_other = swap(far, "col", 2, 1)
@@ -107,7 +111,7 @@
         flops=2 * rows * cols * 3 * rows,
         size=2 * 10 * rows * cols,
         scratch_shapes=[pltpu.VMEM((4, rows, cols), jnp.bfloat16)],
-    )(*here, *there, *right)
+    )(*right, *here, *there)
     squares, sums = call(
         squares_kernel,
         [full, jax.ShapeDtypeStruct((8, cols), jnp.float32)],

time: 40 us -> 41 us (1.025)
  starting transfers between devices: 16.9 us -> 19.5 us
  waiting for transfers between devices: 19.4 us -> 17.8 us
    ppermute x12, starting transfers between devices: 10.9 us -> 12.8 us  [swap(): return lax.ppermute(x, axis, [(i, i ^ s) for i in range(size)])]
    ppermute x1, waiting for transfers between devices: 4.15 us -> 3.16 us  [on_small_mesh(): far = lax.ppermute(start, 'layer', [(1, 2), (2, 1)])]
    ppermute x1, starting transfers between devices: 3.45 us -> 4.26 us  [on_small_mesh(): far = lax.ppermute(start, 'layer', [(1, 2), (2, 1)])]
    ppermute x12, waiting for transfers between devices: 15.2 us -> 14.6 us  [swap(): return lax.ppermute(x, axis, [(i, i ^ s) for i in range(size)])]
where the time goes in v3:
time: 41 us; the launch traced here: 40.8 us
  starting transfers between devices  19.5 us (48%)
  waiting for transfers between devices  17.8 us (43%)
  Pallas kernels  1.81 us (4%)
  other arithmetic  0.95 us (2%)
  local copies, waits for them, and re-layouts  0.62 us (2%)
    ppermute x12, waiting for transfers between devices, swap(): return lax.ppermute(x, axis, [(i, i ^ s) for i in range(size)])  14.6 us
    ppermute x12, starting transfers between devices, swap(): return lax.ppermute(x, axis, [(i, i ^ s) for i in range(size)])  12.8 us
    ppermute x1, starting transfers between devices, on_small_mesh(): far = lax.ppermute(start, 'layer', [(1, 2), (2, 1)])  4.26 us
    ppermute x1, waiting for transfers between devices, on_small_mesh(): far = lax.ppermute(start, 'layer', [(1, 2), (2, 1)])  3.16 us
    ppermute x1, starting transfers between devices, on_small_mesh(): ends = lax.ppermute(near2, 'layer', [(2, 3), (1, 0)])  2.46 us
    pallas_call x1, Pallas kernels, on_small_mesh(): call(functools.partial(scale_kernel, total_rows), full, [VMEM] * 5, flops...  0.85 us
  transfers between devices with their start and end apart: 14, of which 7 were waited for; matrix products, arithmetic and copies ran while one was open for 1% of the time, Pallas kernels for 2%

profile of v3, /device:TPU:8, one launch (start us, length us, event | category | flops | bytes accessed | tf_op | source)
XLA Modules:
  0.0 40.8 jit_solution(5025763043357466485)
XLA Ops:
  0.0 0.7 %convert_element_type.12 = f32[4,2]{0,1:T(2,128)S(1)} convert(s32[4,2]{0,1:T(2,128)} %param.5) | non-fusion elementwise | flops 8 | bytes 64 | tf_op jit(solution)/shard_map/convert_element_type | solution.py:90
  0.8 0.2 mul.22
  1.2 2.7 %collective-permute-start = (bf16[512,256]{1,0:T(8,128)(2,1)S(1)}, bf16[512,256]{1,0:T(8,128)(2,1)S(1)}, u32[]{:S(2)}, u32[]{:S(2)}) collective-permute-start(bf16[512,256]{1,0:T(8,128)(2,1)S(1)} %fusion.refs_0_.refs_4_), channel_id=1, source_target_pairs={{0,2},{1,3},{2,0},{3,1},{4,6},{5,7},{6,4},{7,5},{8,10},{9,11},{10,... | collective-permute-start | bytes 786440 | tf_op jit(solution)/shard_map/ppermute | solution.py:70
  3.8 0.4 %collective-permute-start.1 = (bf16[512,256]{1,0:T(8,128)(2,1)S(1)}, bf16[512,256]{1,0:T(8,128)(2,1)S(1)}, u32[]{:S(2)}, u32[]{:S(2)}) collective-permute-start(bf16[512,256]{1,0:T(8,128)(2,1)S(1)} %fusion.refs_0_.refs_4_), channel_id=1, source_target_pairs={{0,1},{1,0},{2,3},{3,2},{4,5},{5,4},{6,7},{7,6},{8,9},{9,8},{10,11... | collective-permute-start | bytes 786440 | tf_op jit(solution)/shard_map/ppermute | solution.py:70
  4.3 1.5 %collective-permute-start.2 = (bf16[512,256]{1,0:T(8,128)(2,1)S(1)}, bf16[512,256]{1,0:T(8,128)(2,1)S(1)}, u32[]{:S(2)}, u32[]{:S(2)}) collective-permute-start(bf16[512,256]{1,0:T(8,128)(2,1)S(1)} %fusion.refs_0_.refs_4_), channel_id=1, source_target_pairs={{0,8},{8,0},{16,24},{24,16},{1,9},{9,1},{17,25},{25,17},{2,10},{10... | collective-permute-start | bytes 786440 | tf_op jit(solution)/shard_map/ppermute | solution.py:70
  5.8 1.5 %collective-permute-start.3 = (bf16[512,256]{1,0:T(8,128)(2,1)S(1)}, bf16[512,256]{1,0:T(8,128)(2,1)S(1)}, u32[]{:S(2)}, u32[]{:S(2)}) collective-permute-start(bf16[512,256]{1,0:T(8,128)(2,1)S(1)} %fusion.refs_0_.refs_4_), channel_id=1, source_target_pairs={{0,16},{8,24},{16,0},{24,8},{1,17},{9,25},{17,1},{25,9},{2,18},{10... | collective-permute-start | bytes 786440 | tf_op jit(solution)/shard_map/ppermute | solution.py:70
  7.4 0.2 mul.25
  7.7 7.2 %collective-permute-done.refs_6_ = bf16[512,256]{1,0:T(8,128)(2,1)S(1)} collective-permute-done((bf16[512,256]{1,0:T(8,128)(2,1)S(1)}, bf16[512,256]{1,0:T(8,128)(2,1)S(1)}, u32[]{:S(2)}, u32[]{:S(2)}) %collective-permute-start) | collective-permute-done | bytes 262176 | tf_op jit(solution)/shard_map/ppermute | solution.py:70
  14.9 1.1 %collective-permute-done.1.refs_5_ = bf16[512,256]{1,0:T(8,128)(2,1)S(1)} collective-permute-done((bf16[512,256]{1,0:T(8,128)(2,1)S(1)}, bf16[512,256]{1,0:T(8,128)(2,1)S(1)}, u32[]{:S(2)}, u32[]{:S(2)}) %collective-permute-start.1) | collective-permute-done | bytes 262176 | tf_op jit(solution)/shard_map/ppermute | solution.py:70
  16.0 2.5 %collective-permute-start.8 = (bf16[512,256]{1,0:T(8,128)(2,1)S(1)}, bf16[512,256]{1,0:T(8,128)(2,1)S(1)}, u32[]{:S(2)}, u32[]{:S(2)}) collective-permute-start(bf16[512,256]{1,0:T(8,128)(2,1)S(1)} %collective-permute-done.refs_6_), channel_id=1, source_target_pairs={{2,3},{1,0},{6,7},{5,4},{10,11},{9,8},{14,15},{13,12},{18,19},{17,... | collective-permute-start | bytes 786440 | tf_op jit(solution)/shard_map/ppermute | solution.py:99
  18.4 4.3 %collective-permute-start.9 = (bf16[512,256]{1,0:T(8,128)(2,1)S(1)}, bf16[512,256]{1,0:T(8,128)(2,1)S(1)}, u32[]{:S(2)}, u32[]{:S(2)}) collective-permute-start(bf16[512,256]{1,0:T(8,128)(2,1)S(1)} %fusion.refs_0_.refs_4_), channel_id=1, source_target_pairs={{1,2},{2,1},{5,6},{6,5},{9,10},{10,9},{13,14},{14,13},{17,18},{18,... | collective-permute-start | bytes 786440 | tf_op jit(solution)/shard_map/ppermute | solution.py:100
  22.7 2.5 %collective-permute-start.5 = (bf16[512,256]{1,0:T(8,128)(2,1)S(1)}, bf16[512,256]{1,0:T(8,128)(2,1)S(1)}, u32[]{:S(2)}, u32[]{:S(2)}) collective-permute-start(bf16[512,256]{1,0:T(8,128)(2,1)S(1)} %fusion.refs_0_.refs_4_), channel_id=1, source_target_pairs={{0,24},{8,16},{16,8},{24,0},{1,25},{9,17},{17,9},{25,1},{2,26},{10... | collective-permute-start | bytes 786440 | tf_op jit(solution)/shard_map/ppermute | solution.py:70
  25.2 0.5 %collective-permute-start.7 = (bf16[512,256]{1,0:T(8,128)(2,1)S(1)}, bf16[512,256]{1,0:T(8,128)(2,1)S(1)}, u32[]{:S(2)}, u32[]{:S(2)}) collective-permute-start(bf16[512,256]{1,0:T(8,128)(2,1)S(1)} %collective-permute-done.refs_6_), channel_id=1, source_target_pairs={{0,4},{4,0},{1,5},{5,1},{2,6},{6,2},{3,7},{7,3},{8,12},{12,8},{9,1... | collective-permute-start | bytes 786440 | tf_op jit(solution)/shard_map/ppermute | solution.py:70
  25.7 3.2 %collective-permute-done.9 = bf16[512,256]{1,0:T(8,128)(2,1)S(1)} collective-permute-done((bf16[512,256]{1,0:T(8,128)(2,1)S(1)}, bf16[512,256]{1,0:T(8,128)(2,1)S(1)}, u32[]{:S(2)}, u32[]{:S(2)}) %collective-permute-start.9) | collective-permute-done | bytes 262176 | tf_op jit(solution)/shard_map/ppermute | solution.py:100
  29.0 2.3 %collective-permute-done.5.refs_3_ = bf16[512,256]{1,0:T(8,128)(2,1)S(1)} collective-permute-done((bf16[512,256]{1,0:T(8,128)(2,1)S(1)}, bf16[512,256]{1,0:T(8,128)(2,1)S(1)}, u32[]{:S(2)}, u32[]{:S(2)}) %collective-permute-start.5) | collective-permute-done | bytes 262176 | tf_op jit(solution)/shard_map/ppermute | solution.py:70
  31.3 0.7 %shard_map.46 = (f32[512,256]{1,0:T(8,128)S(1)}, bf16[256,256]{1,0:T(8,128)(2,1)S(1)}, bf16[256,256]{1,0:T(8,128)(2,1)S(1)}) custom-call(bf16[512,256]{1,0:T(8,128)(2,1)S(1)} %fusion.refs_0_.refs_4_, bf16[512,256]{1,0:T(8,128)(2,1)S(1)} %collective-permute-done.2.refs_1_, bf16[512,256]{1,0:T(8,128)(2,1)S(1)} %collective-permute-done.3.refs_2_, ...), custom_call_target="tpu_custom_call" | custom-call | flops 402653184 | bytes 2621440 | tf_op jit(solution)/shard_map/pallas_call | solution.py:107
  32.0 0.3 shard_map.47
  32.3 1.6 %collective-permute-start.11 = (f32[8,256]{1,0:T(8,128)S(1)}, f32[8,256]{1,0:T(8,128)S(1)}, u32[]{:S(2)}, u32[]{:S(2)}) collective-permute-start(f32[8,256]{1,0:T(8,128)S(1)} %get-tuple-element.32.refs_0_), channel_id=1, source_target_pairs={{0,8},{8,0},{16,24},{24,16},{1,9},{9,1},{17,25},{25,17},{2,10},{10... | collective-permute-start | bytes 24584 | tf_op jit(solution)/shard_map/ppermute | solution.py:70
  33.9 1.5 %collective-permute-start.12 = (f32[8,256]{1,0:T(8,128)S(1)}, f32[8,256]{1,0:T(8,128)S(1)}, u32[]{:S(2)}, u32[]{:S(2)}) collective-permute-start(f32[8,256]{1,0:T(8,128)S(1)} %get-tuple-element.32.refs_0_), channel_id=1, source_target_pairs={{0,16},{8,24},{16,0},{24,8},{1,17},{9,25},{17,1},{25,9},{2,18},{10... | collective-permute-start | bytes 24584 | tf_op jit(solution)/shard_map/ppermute | solution.py:70
  35.4 0.5 %collective-permute-start.13 = (f32[8,256]{1,0:T(8,128)S(1)}, f32[8,256]{1,0:T(8,128)S(1)}, u32[]{:S(2)}, u32[]{:S(2)}) collective-permute-start(f32[8,256]{1,0:T(8,128)S(1)} %get-tuple-element.32.refs_0_), channel_id=1, source_target_pairs={{0,24},{8,16},{16,8},{24,0},{1,25},{9,17},{17,9},{25,1},{2,26},{10... | collective-permute-start | bytes 24584 | tf_op jit(solution)/shard_map/ppermute | solution.py:70
  35.9 0.2 collective-permute-done.11.refs_1_
  36.0 1.5 %collective-permute-done.12.refs_2_ = f32[8,256]{1,0:T(8,128)S(1)} collective-permute-done((f32[8,256]{1,0:T(8,128)S(1)}, f32[8,256]{1,0:T(8,128)S(1)}, u32[]{:S(2)}, u32[]{:S(2)}) %collective-permute-start.12) | collective-permute-done | bytes 8224 | tf_op jit(solution)/shard_map/ppermute | solution.py:70
  37.5 2.4 %collective-permute-done.13.refs_3_ = f32[8,256]{1,0:T(8,128)S(1)} collective-permute-done((f32[8,256]{1,0:T(8,128)S(1)}, f32[8,256]{1,0:T(8,128)S(1)}, u32[]{:S(2)}, u32[]{:S(2)}) %collective-permute-start.13) | collective-permute-done | bytes 8224 | tf_op jit(solution)/shard_map/ppermute | solution.py:70
  39.9 0.8 %shard_map.48 = f32[512,256]{1,0:T(8,128)} custom-call(f32[512,256]{1,0:T(8,128)S(1)} %get-tuple-element.31.squares_ref, f32[8,256]{1,0:T(8,128)S(1)} %get-tuple-element.32.refs_0_, f32[8,256]{1,0:T(8,128)S(1)} %collective-permute-done.11.refs_1_, f32[8,256]{1,0:T(8,128)S(1)} %collective-permute-done.12.refs_2_, f32[8,256]{1,0:T(8,128)S(1)} %collective-permute-done.13.refs_3_), custom_call_target="tpu_custom_call" | custom-call | flops 524288 | bytes 1048576 | tf_op jit(solution)/shard_map/pallas_call | solution.py:123
  (22 shorter events, 0.5 us)
Async XLA Ops:
  0.0 1.1 %copy-start.1 = (f32[512,256]{1,0:T(8,128)S(1)}, f32[512,256]{1,0:T(8,128)}, u32[]{:S(2)}) copy-start(f32[512,256]{1,0:T(8,128)} %param.4) | copy-start | bytes 1572868
  1.1 6.2 %copy-start.2 = (s32[4,2]{0,1:T(2,128)S(1)}, s32[4,2]{0,1:T(2,128)}, u32[]{:S(2)}) copy-start(s32[4,2]{0,1:T(2,128)} %param.6) | copy-start | bytes 100
  1.2 6.4 %copy-start = (s32[512,256]{1,0:T(8,128)S(1)}, s32[512,256]{1,0:T(8,128)}, u32[]{:S(2)}) copy-start(s32[512,256]{1,0:T(8,128)} %param.7) | copy-start | bytes 1572868
  1.2 13.7 %collective-permute-start = (bf16[512,256]{1,0:T(8,128)(2,1)S(1)}, bf16[512,256]{1,0:T(8,128)(2,1)S(1)}, u32[]{:S(2)}, u32[]{:S(2)}) collective-permute-start(bf16[512,256]{1,0:T(8,128)(2,1)S(1)} %fusion.refs_0_.refs_4_), channel_id=1, source_target_pairs={{0,2},{1,3},{2,0},{3,1},{4,6},{5,7},{6,4},{7,5},{8,10},{9,11},{10,... | collective-permute-start | bytes 786440 | tf_op jit(solution)/shard_map/ppermute | solution.py:70
  3.8 12.1 %collective-permute-start.1 = (bf16[512,256]{1,0:T(8,128)(2,1)S(1)}, bf16[512,256]{1,0:T(8,128)(2,1)S(1)}, u32[]{:S(2)}, u32[]{:S(2)}) collective-permute-start(bf16[512,256]{1,0:T(8,128)(2,1)S(1)} %fusion.refs_0_.refs_4_), channel_id=1, source_target_pairs={{0,1},{1,0},{2,3},{3,2},{4,5},{5,4},{6,7},{7,6},{8,9},{9,8},{10,11... | collective-permute-start | bytes 786440 | tf_op jit(solution)/shard_map/ppermute | solution.py:70
  4.3 11.7 %collective-permute-start.2 = (bf16[512,256]{1,0:T(8,128)(2,1)S(1)}, bf16[512,256]{1,0:T(8,128)(2,1)S(1)}, u32[]{:S(2)}, u32[]{:S(2)}) collective-permute-start(bf16[512,256]{1,0:T(8,128)(2,1)S(1)} %fusion.refs_0_.refs_4_), channel_id=1, source_target_pairs={{0,8},{8,0},{16,24},{24,16},{1,9},{9,1},{17,25},{25,17},{2,10},{10... | collective-permute-start | bytes 786440 | tf_op jit(solution)/shard_map/ppermute | solution.py:70
  5.8 10.2 %collective-permute-start.3 = (bf16[512,256]{1,0:T(8,128)(2,1)S(1)}, bf16[512,256]{1,0:T(8,128)(2,1)S(1)}, u32[]{:S(2)}, u32[]{:S(2)}) collective-permute-start(bf16[512,256]{1,0:T(8,128)(2,1)S(1)} %fusion.refs_0_.refs_4_), channel_id=1, source_target_pairs={{0,16},{8,24},{16,0},{24,8},{1,17},{9,25},{17,1},{25,9},{2,18},{10... | collective-permute-start | bytes 786440 | tf_op jit(solution)/shard_map/ppermute | solution.py:70
  7.3 8.7 %collective-permute-start.4 = (bf16[512,256]{1,0:T(8,128)(2,1)S(1)}, bf16[512,256]{1,0:T(8,128)(2,1)S(1)}, u32[]{:S(2)}, u32[]{:S(2)}) collective-permute-start(bf16[512,256]{1,0:T(8,128)(2,1)S(1)} %fusion.refs_0_.refs_4_), channel_id=1, source_target_pairs={{0,4},{4,0},{1,5},{5,1},{2,6},{6,2},{3,7},{7,3},{8,12},{12,8},{9,1... | collective-permute-start | bytes 786440 | tf_op jit(solution)/shard_map/ppermute | solution.py:70
  16.0 9.8 %collective-permute-start.8 = (bf16[512,256]{1,0:T(8,128)(2,1)S(1)}, bf16[512,256]{1,0:T(8,128)(2,1)S(1)}, u32[]{:S(2)}, u32[]{:S(2)}) collective-permute-start(bf16[512,256]{1,0:T(8,128)(2,1)S(1)} %collective-permute-done.refs_6_), channel_id=1, source_target_pairs={{2,3},{1,0},{6,7},{5,4},{10,11},{9,8},{14,15},{13,12},{18,19},{17,... | collective-permute-start | bytes 786440 | tf_op jit(solution)/shard_map/ppermute | solution.py:99
  18.4 10.5 %collective-permute-start.9 = (bf16[512,256]{1,0:T(8,128)(2,1)S(1)}, bf16[512,256]{1,0:T(8,128)(2,1)S(1)}, u32[]{:S(2)}, u32[]{:S(2)}) collective-permute-start(bf16[512,256]{1,0:T(8,128)(2,1)S(1)} %fusion.refs_0_.refs_4_), channel_id=1, source_target_pairs={{1,2},{2,1},{5,6},{6,5},{9,10},{10,9},{13,14},{14,13},{17,18},{18,... | collective-permute-start | bytes 786440 | tf_op jit(solution)/shard_map/ppermute | solution.py:100
  22.7 8.6 %collective-permute-start.5 = (bf16[512,256]{1,0:T(8,128)(2,1)S(1)}, bf16[512,256]{1,0:T(8,128)(2,1)S(1)}, u32[]{:S(2)}, u32[]{:S(2)}) collective-permute-start(bf16[512,256]{1,0:T(8,128)(2,1)S(1)} %fusion.refs_0_.refs_4_), channel_id=1, source_target_pairs={{0,24},{8,16},{16,8},{24,0},{1,25},{9,17},{17,9},{25,1},{2,26},{10... | collective-permute-start | bytes 786440 | tf_op jit(solution)/shard_map/ppermute | solution.py:70
  25.2 6.1 %collective-permute-start.6 = (bf16[512,256]{1,0:T(8,128)(2,1)S(1)}, bf16[512,256]{1,0:T(8,128)(2,1)S(1)}, u32[]{:S(2)}, u32[]{:S(2)}) collective-permute-start(bf16[512,256]{1,0:T(8,128)(2,1)S(1)} %collective-permute-done.1.refs_5_), channel_id=1, source_target_pairs={{0,4},{4,0},{1,5},{5,1},{2,6},{6,2},{3,7},{7,3},{8,12},{12,8},{9,1... | collective-permute-start | bytes 786440 | tf_op jit(solution)/shard_map/ppermute | solution.py:70
  25.2 6.1 %collective-permute-start.7 = (bf16[512,256]{1,0:T(8,128)(2,1)S(1)}, bf16[512,256]{1,0:T(8,128)(2,1)S(1)}, u32[]{:S(2)}, u32[]{:S(2)}) collective-permute-start(bf16[512,256]{1,0:T(8,128)(2,1)S(1)} %collective-permute-done.refs_6_), channel_id=1, source_target_pairs={{0,4},{4,0},{1,5},{5,1},{2,6},{6,2},{3,7},{7,3},{8,12},{12,8},{9,1... | collective-permute-start | bytes 786440 | tf_op jit(solution)/shard_map/ppermute | solution.py:70
  29.0 3.1 %collective-permute-start.10 = (bf16[512,256]{1,0:T(8,128)(2,1)S(1)}, bf16[512,256]{1,0:T(8,128)(2,1)S(1)}, u32[]{:S(2)}, u32[]{:S(2)}) collective-permute-start(bf16[512,256]{1,0:T(8,128)(2,1)S(1)} %add.3.left_own_ref), channel_id=1, source_target_pairs={{0,4},{4,0},{1,5},{5,1},{2,6},{6,2},{3,7},{7,3},{8,12},{12,8},{9,1... | collective-permute-start | bytes 786440 | tf_op jit(solution)/shard_map/ppermute | solution.py:70
  32.3 3.7 %collective-permute-start.11 = (f32[8,256]{1,0:T(8,128)S(1)}, f32[8,256]{1,0:T(8,128)S(1)}, u32[]{:S(2)}, u32[]{:S(2)}) collective-permute-start(f32[8,256]{1,0:T(8,128)S(1)} %get-tuple-element.32.refs_0_), channel_id=1, source_target_pairs={{0,8},{8,0},{16,24},{24,16},{1,9},{9,1},{17,25},{25,17},{2,10},{10... | collective-permute-start | bytes 24584 | tf_op jit(solution)/shard_map/ppermute | solution.py:70
  33.9 3.7 %collective-permute-start.12 = (f32[8,256]{1,0:T(8,128)S(1)}, f32[8,256]{1,0:T(8,128)S(1)}, u32[]{:S(2)}, u32[]{:S(2)}) collective-permute-start(f32[8,256]{1,0:T(8,128)S(1)} %get-tuple-element.32.refs_0_), channel_id=1, source_target_pairs={{0,16},{8,24},{16,0},{24,8},{1,17},{9,25},{17,1},{25,9},{2,18},{10... | collective-permute-start | bytes 24584 | tf_op jit(solution)/shard_map/ppermute | solution.py:70
  35.4 4.5 %collective-permute-start.13 = (f32[8,256]{1,0:T(8,128)S(1)}, f32[8,256]{1,0:T(8,128)S(1)}, u32[]{:S(2)}, u32[]{:S(2)}) collective-permute-start(f32[8,256]{1,0:T(8,128)S(1)} %get-tuple-element.32.refs_0_), channel_id=1, source_target_pairs={{0,24},{8,16},{16,8},{24,0},{1,25},{9,17},{17,9},{25,1},{2,26},{10... | collective-permute-start | bytes 24584 | tf_op jit(solution)/shard_map/ppermute | solution.py:70

commit v4 on v2

--- a/solution.py
+++ b/solution.py
@@ -30,18 +30,20 @@
 
 
 def most_kernel(*refs):
-    here, there, right = refs[:3], refs[3:6], refs[6:10]
+    right, here, there = refs[:4], refs[4:7], refs[7:10]
     total_ref, own_ref, other_ref, panel_ref = refs[10:]
     parity = lax.axis_index("col")
-    lead = lax.axis_index("row") ^ lax.axis_index("layer")
+    layer = lax.axis_index("layer")
+    lead = lax.axis_index("row") ^ layer
+    middle = (layer ^ (layer >> 1)) & 1
     half = here[0].shape[1]
     for s in range(4):
         panel_ref[s ^ lead] = right[s][...]
     total = None
-    for s in range(3):
+    for s, distance in enumerate((0, 1 + middle, 2 - middle)):
         for side, block in enumerate((here[s], there[s])):
             rows = pl.ds(pl.multiple_of((parity ^ side) * half, half), half)
-            part = jnp.dot(block[...], panel_ref[s, rows, :], preferred_element_type=jnp.float32)
+            part = jnp.dot(block[...], panel_ref[distance, rows, :], preferred_element_type=jnp.float32)
             total = part if total is None else total + part
     total_ref[...] = total
     own_ref[...] = panel_ref[3, pl.ds(pl.multiple_of(parity * half, half), half), :]
@@ -88,16 +90,17 @@
     full = jax.ShapeDtypeStruct((rows, cols), jnp.float32)
 
     own = times_tiles(values, a_pattern.astype(jnp.float32)).astype(jnp.bfloat16)
-    near2 = swap(own, "layer", 4, 2)
-    near1 = swap(own, "layer", 4, 1)
+    first = lax.ppermute(own, "layer", [(0, 2), (3, 1), (1, 0), (2, 3)])
+    second = lax.ppermute(own, "layer", [(0, 1), (3, 2), (1, 3), (2, 0)])
     right = [own] + [swap(own, "row", 4, s) for s in (1, 2, 3)]
     weight = times_tiles(prune_mask.astype(jnp.float32), c_pattern.astype(jnp.float32))
-    near2, *right, near1, weight = lax.optimization_barrier((near2, *right, near1, weight))
-    ends = lax.ppermute(near2, "layer", [(2, 3), (1, 0)])
-    far = lax.ppermute(right[0], "layer", [(1, 2), (2, 1)])
-    here = [own, near1, near2]
+    first, start, weight = lax.optimization_barrier((first, own, weight))
+    far = lax.ppermute(start, "layer", [(1, 2), (2, 1)])
+    ends = lax.ppermute(first, "layer", [(1, 0), (2, 3)])
+    second, right[3], right[2], right[1], first, start = lax.optimization_barrier((second, right[3], right[2], right[1], first, start))
+    here = [start, first, second]
     there = [swap(x, "col", 2, 1) for x in here]
-    ends, far = lax.optimization_barrier((ends, far))
+    far, ends, *there = lax.optimization_barrier((far, ends, *there))
     far = ends + far
     far_other = swap(far, "col", 2, 1)
     total, last_own, last_other = call(
@@ -107,7 +110,7 @@
         flops=2 * rows * cols * 3 * rows,
         size=2 * 10 * rows * cols,
         scratch_shapes=[pltpu.VMEM((4, rows, cols), jnp.bfloat16)],
-    )(*here, *there, *right)
+    )(*right, *here, *there)
     squares, sums = call(
         squares_kernel,
         [full, jax.ShapeDtypeStruct((8, cols), jnp.float32)],

time: 40 us -> 33.6 us (0.84)
  the two profiles are of different devices: /device:TPU:8 before, /device:TPU:0 now
where the time goes in v4:
time: 33.6 us; the launch traced here: 33.4 us
  waiting for transfers between devices  16.1 us (48%)
  starting transfers between devices  13.7 us (41%)
  Pallas kernels  1.8 us (5%)
  other arithmetic  0.95 us (3%)
  local copies, waits for them, and re-layouts  0.62 us (2%)
    ppermute x10, waiting for transfers between devices, swap(): return lax.ppermute(x, axis, [(i, i ^ s) for i in range(size)])  9.88 us
    ppermute x10, starting transfers between devices, swap(): return lax.ppermute(x, axis, [(i, i ^ s) for i in range(size)])  7.7 us
    ppermute x1, starting transfers between devices, on_small_mesh(): first = lax.ppermute(own, 'layer', [(0, 2), (3, 1), (1, 0), (2, 3)])  4.09 us
    ppermute x1, waiting for transfers between devices, on_small_mesh(): ends = lax.ppermute(first, 'layer', [(1, 0), (2, 3)])  3.42 us
    ppermute x1, waiting for transfers between devices, on_small_mesh(): first = lax.ppermute(own, 'layer', [(0, 2), (3, 1), (1, 0), (2, 3)])  2.83 us
    ppermute x1, starting transfers between devices, on_small_mesh(): ends = lax.ppermute(first, 'layer', [(1, 0), (2, 3)])  1.28 us
    pallas_call x1, Pallas kernels, on_small_mesh(): call(functools.partial(scale_kernel, total_rows), full, [VMEM] * 5, flops...  0.85 us
    convert_element_type x1, other arithmetic, on_small_mesh(): a_pattern.astype(jnp.float32)  0.74 us
  transfers between devices with their start and end apart: 14, of which 8 were waited for; matrix products, arithmetic and copies ran while one was open for 1% of the time, Pallas kernels for 2%

profile of v4, /device:TPU:0, one launch (start us, length us, event | category | flops | bytes accessed | tf_op | source)
XLA Modules:
  0.0 33.4 jit_solution(2026382741677974715)
XLA Ops:
  0.0 0.7 %convert_element_type.12 = f32[4,2]{0,1:T(2,128)S(1)} convert(s32[4,2]{0,1:T(2,128)} %param.5) | non-fusion elementwise | flops 8 | bytes 64 | tf_op jit(solution)/shard_map/convert_element_type | solution.py:92
  0.8 0.2 mul.22
  1.2 4.1 %collective-permute-start.4 = (bf16[512,256]{1,0:T(8,128)(2,1)S(1)}, bf16[512,256]{1,0:T(8,128)(2,1)S(1)}, u32[]{:S(2)}, u32[]{:S(2)}) collective-permute-start(bf16[512,256]{1,0:T(8,128)(2,1)S(1)} %fusion.refs_0_.refs_4_), channel_id=1, source_target_pairs={{0,2},{3,1},{1,0},{2,3},{4,6},{7,5},{5,4},{6,7},{8,10},{11,9},{9,8... | collective-permute-start | bytes 786440 | tf_op jit(solution)/shard_map/ppermute | solution.py:93
  5.3 1.5 %collective-permute-start.3 = (bf16[512,256]{1,0:T(8,128)(2,1)S(1)}, bf16[512,256]{1,0:T(8,128)(2,1)S(1)}, u32[]{:S(2)}, u32[]{:S(2)}) collective-permute-start(bf16[512,256]{1,0:T(8,128)(2,1)S(1)} %fusion.refs_0_.refs_4_), channel_id=1, source_target_pairs={{0,8},{8,0},{16,24},{24,16},{1,9},{9,1},{17,25},{25,17},{2,10},{10... | collective-permute-start | bytes 786440 | tf_op jit(solution)/shard_map/ppermute | solution.py:72
  6.7 1.5 %collective-permute-start.2 = (bf16[512,256]{1,0:T(8,128)(2,1)S(1)}, bf16[512,256]{1,0:T(8,128)(2,1)S(1)}, u32[]{:S(2)}, u32[]{:S(2)}) collective-permute-start(bf16[512,256]{1,0:T(8,128)(2,1)S(1)} %fusion.refs_0_.refs_4_), channel_id=1, source_target_pairs={{0,16},{8,24},{16,0},{24,8},{1,17},{9,25},{17,1},{25,9},{2,18},{10... | collective-permute-start | bytes 786440 | tf_op jit(solution)/shard_map/ppermute | solution.py:72
  8.3 0.5 %collective-permute-start.1 = (bf16[512,256]{1,0:T(8,128)(2,1)S(1)}, bf16[512,256]{1,0:T(8,128)(2,1)S(1)}, u32[]{:S(2)}, u32[]{:S(2)}) collective-permute-start(bf16[512,256]{1,0:T(8,128)(2,1)S(1)} %fusion.refs_0_.refs_4_), channel_id=1, source_target_pairs={{0,24},{8,16},{16,8},{24,0},{1,25},{9,17},{17,9},{25,1},{2,26},{10... | collective-permute-start | bytes 786440 | tf_op jit(solution)/shard_map/ppermute | solution.py:72
  8.8 0.2 mul.25
  9.1 2.8 %collective-permute-done.4.refs_5_ = bf16[512,256]{1,0:T(8,128)(2,1)S(1)} collective-permute-done((bf16[512,256]{1,0:T(8,128)(2,1)S(1)}, bf16[512,256]{1,0:T(8,128)(2,1)S(1)}, u32[]{:S(2)}, u32[]{:S(2)}) %collective-permute-start.4) | collective-permute-done | bytes 262176 | tf_op jit(solution)/shard_map/ppermute | solution.py:93
  12.0 1.3 %collective-permute-start.6 = (bf16[512,256]{1,0:T(8,128)(2,1)S(1)}, bf16[512,256]{1,0:T(8,128)(2,1)S(1)}, u32[]{:S(2)}, u32[]{:S(2)}) collective-permute-start(bf16[512,256]{1,0:T(8,128)(2,1)S(1)} %collective-permute-done.4.refs_5_), channel_id=1, source_target_pairs={{1,0},{2,3},{5,4},{6,7},{9,8},{10,11},{13,12},{14,15},{17,16},{18,... | collective-permute-start | bytes 786440 | tf_op jit(solution)/shard_map/ppermute | solution.py:99
  13.3 1.2 %collective-permute-done.3.refs_1_ = bf16[512,256]{1,0:T(8,128)(2,1)S(1)} collective-permute-done((bf16[512,256]{1,0:T(8,128)(2,1)S(1)}, bf16[512,256]{1,0:T(8,128)(2,1)S(1)}, u32[]{:S(2)}, u32[]{:S(2)}) %collective-permute-start.3) | collective-permute-done | bytes 262176 | tf_op jit(solution)/shard_map/ppermute | solution.py:72
  14.5 0.7 %collective-permute-start.5 = (bf16[512,256]{1,0:T(8,128)(2,1)S(1)}, bf16[512,256]{1,0:T(8,128)(2,1)S(1)}, u32[]{:S(2)}, u32[]{:S(2)}) collective-permute-start(bf16[512,256]{1,0:T(8,128)(2,1)S(1)} %fusion.refs_0_.refs_4_), channel_id=1, source_target_pairs={{1,2},{2,1},{5,6},{6,5},{9,10},{10,9},{13,14},{14,13},{17,18},{18,... | collective-permute-start | bytes 786440 | tf_op jit(solution)/shard_map/ppermute | solution.py:98
  15.2 4.7 %collective-permute-done.2.refs_2_ = bf16[512,256]{1,0:T(8,128)(2,1)S(1)} collective-permute-done((bf16[512,256]{1,0:T(8,128)(2,1)S(1)}, bf16[512,256]{1,0:T(8,128)(2,1)S(1)}, u32[]{:S(2)}, u32[]{:S(2)}) %collective-permute-start.2) | collective-permute-done | bytes 262176 | tf_op jit(solution)/shard_map/ppermute | solution.py:72
  19.9 0.5 %collective-permute-start.8 = (bf16[512,256]{1,0:T(8,128)(2,1)S(1)}, bf16[512,256]{1,0:T(8,128)(2,1)S(1)}, u32[]{:S(2)}, u32[]{:S(2)}) collective-permute-start(bf16[512,256]{1,0:T(8,128)(2,1)S(1)} %collective-permute-done.4.refs_5_), channel_id=1, source_target_pairs={{0,4},{4,0},{1,5},{5,1},{2,6},{6,2},{3,7},{7,3},{8,12},{12,8},{9,1... | collective-permute-start | bytes 786440 | tf_op jit(solution)/shard_map/ppermute | solution.py:72
  20.4 3.4 %collective-permute-done.6 = bf16[512,256]{1,0:T(8,128)(2,1)S(1)} collective-permute-done((bf16[512,256]{1,0:T(8,128)(2,1)S(1)}, bf16[512,256]{1,0:T(8,128)(2,1)S(1)}, u32[]{:S(2)}, u32[]{:S(2)}) %collective-permute-start.6) | collective-permute-done | bytes 262176 | tf_op jit(solution)/shard_map/ppermute | solution.py:99
  24.0 0.7 %shard_map.46 = (f32[512,256]{1,0:T(8,128)S(1)}, bf16[256,256]{1,0:T(8,128)(2,1)S(1)}, bf16[256,256]{1,0:T(8,128)(2,1)S(1)}) custom-call(bf16[512,256]{1,0:T(8,128)(2,1)S(1)} %fusion.refs_0_.refs_4_, bf16[512,256]{1,0:T(8,128)(2,1)S(1)} %collective-permute-done.3.refs_1_, bf16[512,256]{1,0:T(8,128)(2,1)S(1)} %collective-permute-done.2.refs_2_, ...), custom_call_target="tpu_custom_call" | custom-call | flops 402653184 | bytes 2621440 | tf_op jit(solution)/shard_map/pallas_call | solution.py:106
  24.7 0.8 %collective-permute-done.10.left_other_ref = bf16[512,256]{1,0:T(8,128)(2,1)S(1)} collective-permute-done((bf16[512,256]{1,0:T(8,128)(2,1)S(1)}, bf16[512,256]{1,0:T(8,128)(2,1)S(1)}, u32[]{:S(2)}, u32[]{:S(2)}) %collective-permute-start.10) | collective-permute-done | bytes 262176 | tf_op jit(solution)/shard_map/ppermute | solution.py:72
  25.6 0.3 shard_map.47
  25.9 2.5 %collective-permute-start.13 = (f32[8,256]{1,0:T(8,128)S(1)}, f32[8,256]{1,0:T(8,128)S(1)}, u32[]{:S(2)}, u32[]{:S(2)}) collective-permute-start(f32[8,256]{1,0:T(8,128)S(1)} %get-tuple-element.42.refs_0_), channel_id=1, source_target_pairs={{0,24},{8,16},{16,8},{24,0},{1,25},{9,17},{17,9},{25,1},{2,26},{10... | collective-permute-start | bytes 24584 | tf_op jit(solution)/shard_map/ppermute | solution.py:72
  28.4 0.5 %collective-permute-start.12 = (f32[8,256]{1,0:T(8,128)S(1)}, f32[8,256]{1,0:T(8,128)S(1)}, u32[]{:S(2)}, u32[]{:S(2)}) collective-permute-start(f32[8,256]{1,0:T(8,128)S(1)} %get-tuple-element.42.refs_0_), channel_id=1, source_target_pairs={{0,16},{8,24},{16,0},{24,8},{1,17},{9,25},{17,1},{25,9},{2,18},{10... | collective-permute-start | bytes 24584 | tf_op jit(solution)/shard_map/ppermute | solution.py:72
  28.9 0.5 %collective-permute-start.11 = (f32[8,256]{1,0:T(8,128)S(1)}, f32[8,256]{1,0:T(8,128)S(1)}, u32[]{:S(2)}, u32[]{:S(2)}) collective-permute-start(f32[8,256]{1,0:T(8,128)S(1)} %get-tuple-element.42.refs_0_), channel_id=1, source_target_pairs={{0,8},{8,0},{16,24},{24,16},{1,9},{9,1},{17,25},{25,17},{2,10},{10... | collective-permute-start | bytes 24584 | tf_op jit(solution)/shard_map/ppermute | solution.py:72
  29.4 1.1 %collective-permute-done.13.refs_3_ = f32[8,256]{1,0:T(8,128)S(1)} collective-permute-done((f32[8,256]{1,0:T(8,128)S(1)}, f32[8,256]{1,0:T(8,128)S(1)}, u32[]{:S(2)}, u32[]{:S(2)}) %collective-permute-start.13) | collective-permute-done | bytes 8224 | tf_op jit(solution)/shard_map/ppermute | solution.py:72
  30.5 1.6 %collective-permute-done.12.refs_2_ = f32[8,256]{1,0:T(8,128)S(1)} collective-permute-done((f32[8,256]{1,0:T(8,128)S(1)}, f32[8,256]{1,0:T(8,128)S(1)}, u32[]{:S(2)}, u32[]{:S(2)}) %collective-permute-start.12) | collective-permute-done | bytes 8224 | tf_op jit(solution)/shard_map/ppermute | solution.py:72
  32.0 0.5 %collective-permute-done.11.refs_1_ = f32[8,256]{1,0:T(8,128)S(1)} collective-permute-done((f32[8,256]{1,0:T(8,128)S(1)}, f32[8,256]{1,0:T(8,128)S(1)}, u32[]{:S(2)}, u32[]{:S(2)}) %collective-permute-start.11) | collective-permute-done | bytes 8224 | tf_op jit(solution)/shard_map/ppermute | solution.py:72
  32.5 0.8 %shard_map.48 = f32[512,256]{1,0:T(8,128)} custom-call(f32[512,256]{1,0:T(8,128)S(1)} %get-tuple-element.41.squares_ref, f32[8,256]{1,0:T(8,128)S(1)} %get-tuple-element.42.refs_0_, f32[8,256]{1,0:T(8,128)S(1)} %collective-permute-done.11.refs_1_, f32[8,256]{1,0:T(8,128)S(1)} %collective-permute-done.12.refs_2_, f32[8,256]{1,0:T(8,128)S(1)} %collective-permute-done.13.refs_3_), custom_call_target="tpu_custom_call" | custom-call | flops 524288 | bytes 1048576 | tf_op jit(solution)/shard_map/pallas_call | solution.py:122
  (22 shorter events, 0.6 us)
Async XLA Ops:
  0.0 1.1 %copy-start.1 = (f32[512,256]{1,0:T(8,128)S(1)}, f32[512,256]{1,0:T(8,128)}, u32[]{:S(2)}) copy-start(f32[512,256]{1,0:T(8,128)} %param.4) | copy-start | bytes 1572868
  1.1 7.7 %copy-start.2 = (s32[4,2]{0,1:T(2,128)S(1)}, s32[4,2]{0,1:T(2,128)}, u32[]{:S(2)}) copy-start(s32[4,2]{0,1:T(2,128)} %param.6) | copy-start | bytes 100
  1.2 7.9 %copy-start = (s32[512,256]{1,0:T(8,128)S(1)}, s32[512,256]{1,0:T(8,128)}, u32[]{:S(2)}) copy-start(s32[512,256]{1,0:T(8,128)} %param.7) | copy-start | bytes 1572868
  1.2 10.8 %collective-permute-start.4 = (bf16[512,256]{1,0:T(8,128)(2,1)S(1)}, bf16[512,256]{1,0:T(8,128)(2,1)S(1)}, u32[]{:S(2)}, u32[]{:S(2)}) collective-permute-start(bf16[512,256]{1,0:T(8,128)(2,1)S(1)} %fusion.refs_0_.refs_4_), channel_id=1, source_target_pairs={{0,2},{3,1},{1,0},{2,3},{4,6},{7,5},{5,4},{6,7},{8,10},{11,9},{9,8... | collective-permute-start | bytes 786440 | tf_op jit(solution)/shard_map/ppermute | solution.py:93
  5.3 9.2 %collective-permute-start.3 = (bf16[512,256]{1,0:T(8,128)(2,1)S(1)}, bf16[512,256]{1,0:T(8,128)(2,1)S(1)}, u32[]{:S(2)}, u32[]{:S(2)}) collective-permute-start(bf16[512,256]{1,0:T(8,128)(2,1)S(1)} %fusion.refs_0_.refs_4_), channel_id=1, source_target_pairs={{0,8},{8,0},{16,24},{24,16},{1,9},{9,1},{17,25},{25,17},{2,10},{10... | collective-permute-start | bytes 786440 | tf_op jit(solution)/shard_map/ppermute | solution.py:72
  6.7 13.1 %collective-permute-start.2 = (bf16[512,256]{1,0:T(8,128)(2,1)S(1)}, bf16[512,256]{1,0:T(8,128)(2,1)S(1)}, u32[]{:S(2)}, u32[]{:S(2)}) collective-permute-start(bf16[512,256]{1,0:T(8,128)(2,1)S(1)} %fusion.refs_0_.refs_4_), channel_id=1, source_target_pairs={{0,16},{8,24},{16,0},{24,8},{1,17},{9,25},{17,1},{25,9},{2,18},{10... | collective-permute-start | bytes 786440 | tf_op jit(solution)/shard_map/ppermute | solution.py:72
  8.3 11.6 %collective-permute-start.1 = (bf16[512,256]{1,0:T(8,128)(2,1)S(1)}, bf16[512,256]{1,0:T(8,128)(2,1)S(1)}, u32[]{:S(2)}, u32[]{:S(2)}) collective-permute-start(bf16[512,256]{1,0:T(8,128)(2,1)S(1)} %fusion.refs_0_.refs_4_), channel_id=1, source_target_pairs={{0,24},{8,16},{16,8},{24,0},{1,25},{9,17},{17,9},{25,1},{2,26},{10... | collective-permute-start | bytes 786440 | tf_op jit(solution)/shard_map/ppermute | solution.py:72
  8.7 11.1 %collective-permute-start = (bf16[512,256]{1,0:T(8,128)(2,1)S(1)}, bf16[512,256]{1,0:T(8,128)(2,1)S(1)}, u32[]{:S(2)}, u32[]{:S(2)}) collective-permute-start(bf16[512,256]{1,0:T(8,128)(2,1)S(1)} %fusion.refs_0_.refs_4_), channel_id=1, source_target_pairs={{0,1},{3,2},{1,3},{2,0},{4,5},{7,6},{5,7},{6,4},{8,9},{11,10},{9,1... | collective-permute-start | bytes 786440 | tf_op jit(solution)/shard_map/ppermute | solution.py:94
  12.0 11.9 %collective-permute-start.6 = (bf16[512,256]{1,0:T(8,128)(2,1)S(1)}, bf16[512,256]{1,0:T(8,128)(2,1)S(1)}, u32[]{:S(2)}, u32[]{:S(2)}) collective-permute-start(bf16[512,256]{1,0:T(8,128)(2,1)S(1)} %collective-permute-done.4.refs_5_), channel_id=1, source_target_pairs={{1,0},{2,3},{5,4},{6,7},{9,8},{10,11},{13,12},{14,15},{17,16},{18,... | collective-permute-start | bytes 786440 | tf_op jit(solution)/shard_map/ppermute | solution.py:99
  14.5 9.4 %collective-permute-start.5 = (bf16[512,256]{1,0:T(8,128)(2,1)S(1)}, bf16[512,256]{1,0:T(8,128)(2,1)S(1)}, u32[]{:S(2)}, u32[]{:S(2)}) collective-permute-start(bf16[512,256]{1,0:T(8,128)(2,1)S(1)} %fusion.refs_0_.refs_4_), channel_id=1, source_target_pairs={{1,2},{2,1},{5,6},{6,5},{9,10},{10,9},{13,14},{14,13},{17,18},{18,... | collective-permute-start | bytes 786440 | tf_op jit(solution)/shard_map/ppermute | solution.py:98
  19.9 4.0 %collective-permute-start.7 = (bf16[512,256]{1,0:T(8,128)(2,1)S(1)}, bf16[512,256]{1,0:T(8,128)(2,1)S(1)}, u32[]{:S(2)}, u32[]{:S(2)}) collective-permute-start(bf16[512,256]{1,0:T(8,128)(2,1)S(1)} %fusion.refs_0_.refs_4_), channel_id=1, source_target_pairs={{0,4},{4,0},{1,5},{5,1},{2,6},{6,2},{3,7},{7,3},{8,12},{12,8},{9,1... | collective-permute-start | bytes 786440 | tf_op jit(solution)/shard_map/ppermute | solution.py:72
  19.9 4.0 %collective-permute-start.8 = (bf16[512,256]{1,0:T(8,128)(2,1)S(1)}, bf16[512,256]{1,0:T(8,128)(2,1)S(1)}, u32[]{:S(2)}, u32[]{:S(2)}) collective-permute-start(bf16[512,256]{1,0:T(8,128)(2,1)S(1)} %collective-permute-done.4.refs_5_), channel_id=1, source_target_pairs={{0,4},{4,0},{1,5},{5,1},{2,6},{6,2},{3,7},{7,3},{8,12},{12,8},{9,1... | collective-permute-start | bytes 786440 | tf_op jit(solution)/shard_map/ppermute | solution.py:72
  20.4 3.5 %collective-permute-start.9 = (bf16[512,256]{1,0:T(8,128)(2,1)S(1)}, bf16[512,256]{1,0:T(8,128)(2,1)S(1)}, u32[]{:S(2)}, u32[]{:S(2)}) collective-permute-start(bf16[512,256]{1,0:T(8,128)(2,1)S(1)} %collective-permute-done.refs_6_), channel_id=1, source_target_pairs={{0,4},{4,0},{1,5},{5,1},{2,6},{6,2},{3,7},{7,3},{8,12},{12,8},{9,1... | collective-permute-start | bytes 786440 | tf_op jit(solution)/shard_map/ppermute | solution.py:72
  24.0 1.6 %collective-permute-start.10 = (bf16[512,256]{1,0:T(8,128)(2,1)S(1)}, bf16[512,256]{1,0:T(8,128)(2,1)S(1)}, u32[]{:S(2)}, u32[]{:S(2)}) collective-permute-start(bf16[512,256]{1,0:T(8,128)(2,1)S(1)} %add.3.left_own_ref), channel_id=1, source_target_pairs={{0,4},{4,0},{1,5},{5,1},{2,6},{6,2},{3,7},{7,3},{8,12},{12,8},{9,1... | collective-permute-start | bytes 786440 | tf_op jit(solution)/shard_map/ppermute | solution.py:72
  25.9 4.6 %collective-permute-start.13 = (f32[8,256]{1,0:T(8,128)S(1)}, f32[8,256]{1,0:T(8,128)S(1)}, u32[]{:S(2)}, u32[]{:S(2)}) collective-permute-start(f32[8,256]{1,0:T(8,128)S(1)} %get-tuple-element.42.refs_0_), channel_id=1, source_target_pairs={{0,24},{8,16},{16,8},{24,0},{1,25},{9,17},{17,9},{25,1},{2,26},{10... | collective-permute-start | bytes 24584 | tf_op jit(solution)/shard_map/ppermute | solution.py:72
  28.4 3.7 %collective-permute-start.12 = (f32[8,256]{1,0:T(8,128)S(1)}, f32[8,256]{1,0:T(8,128)S(1)}, u32[]{:S(2)}, u32[]{:S(2)}) collective-permute-start(f32[8,256]{1,0:T(8,128)S(1)} %get-tuple-element.42.refs_0_), channel_id=1, source_target_pairs={{0,16},{8,24},{16,0},{24,8},{1,17},{9,25},{17,1},{25,9},{2,18},{10... | collective-permute-start | bytes 24584 | tf_op jit(solution)/shard_map/ppermute | solution.py:72
  28.9 3.7 %collective-permute-start.11 = (f32[8,256]{1,0:T(8,128)S(1)}, f32[8,256]{1,0:T(8,128)S(1)}, u32[]{:S(2)}, u32[]{:S(2)}) collective-permute-start(f32[8,256]{1,0:T(8,128)S(1)} %get-tuple-element.42.refs_0_), channel_id=1, source_target_pairs={{0,8},{8,0},{16,24},{24,16},{1,9},{9,1},{17,25},{25,17},{2,10},{10... | collective-permute-start | bytes 24584 | tf_op jit(solution)/shard_map/ppermute | solution.py:72

commit v5 on v4

--- a/solution.py
+++ b/solution.py
@@ -90,18 +90,17 @@
     full = jax.ShapeDtypeStruct((rows, cols), jnp.float32)
 
     own = times_tiles(values, a_pattern.astype(jnp.float32)).astype(jnp.bfloat16)
-    first = lax.ppermute(own, "layer", [(0, 2), (3, 1), (1, 0), (2, 3)])
-    second = lax.ppermute(own, "layer", [(0, 1), (3, 2), (1, 3), (2, 0)])
+    ring = [(0, 2), (2, 3), (3, 1), (1, 0)]
+    first = lax.ppermute(own, "layer", ring)
+    second = lax.ppermute(own, "layer", [(b, a) for a, b in ring])
     right = [own] + [swap(own, "row", 4, s) for s in (1, 2, 3)]
     weight = times_tiles(prune_mask.astype(jnp.float32), c_pattern.astype(jnp.float32))
     first, start, weight = lax.optimization_barrier((first, own, weight))
-    far = lax.ppermute(start, "layer", [(1, 2), (2, 1)])
-    ends = lax.ppermute(first, "layer", [(1, 0), (2, 3)])
+    far = lax.ppermute(first, "layer", ring)
     second, right[3], right[2], right[1], first, start = lax.optimization_barrier((second, right[3], right[2], right[1], first, start))
     here = [start, first, second]
     there = [swap(x, "col", 2, 1) for x in here]
-    far, ends, *there = lax.optimization_barrier((far, ends, *there))
-    far = ends + far
+    far, *there = lax.optimization_barrier((far, *there))
     far_other = swap(far, "col", 2, 1)
     total, last_own, last_other = call(
         most_kernel,

time: 33.6 us -> 33.1 us (0.985)
  waiting for transfers between devices: 16.1 us -> 14.3 us
  starting transfers between devices: 13.7 us -> 15.2 us
    ppermute x4 -> x3, starting transfers between devices: 6.04 us -> 7.47 us  [the longest x1 4.09 us: on_small_mesh(): first = lax.ppermute(own, 'layer', ring)]
    ppermute x10, waiting for transfers between devices: 9.88 us -> 8.46 us  [swap(): return lax.ppermute(x, axis, [(i, i ^ s) for i in range(size)])]
    ppermute x4 -> x3, waiting for transfers between devices: 6.25 us -> 5.87 us  [the longest x1 3.03 us: on_small_mesh(): far = lax.ppermute(first, 'layer', ring)]
  transfers between devices with their start and end apart: 14 -> 13, of which waited for: 8 -> 7; matrix products, arithmetic and copies ran while one was open for 1% -> 1% of each run, Pallas kernels for 2% -> 2%
where the time goes in v5:
time: 33.1 us; the launch traced here: 32.9 us
  starting transfers between devices  15.2 us (46%)
  waiting for transfers between devices  14.3 us (43%)
  Pallas kernels  1.81 us (5%)
  other arithmetic  0.89 us (3%)
  local copies, waits for them, and re-layouts  0.62 us (2%)
    ppermute x10, waiting for transfers between devices, swap(): return lax.ppermute(x, axis, [(i, i ^ s) for i in range(size)])  8.46 us
    ppermute x10, starting transfers between devices, swap(): return lax.ppermute(x, axis, [(i, i ^ s) for i in range(size)])  7.69 us
    ppermute x1, starting transfers between devices, on_small_mesh(): first = lax.ppermute(own, 'layer', ring)  4.09 us
    ppermute x1, starting transfers between devices, on_small_mesh(): far = lax.ppermute(first, 'layer', ring)  3.38 us
    ppermute x1, waiting for transfers between devices, on_small_mesh(): far = lax.ppermute(first, 'layer', ring)  3.03 us
    ppermute x1, waiting for transfers between devices, on_small_mesh(): first = lax.ppermute(own, 'layer', ring)  2.83 us
    pallas_call x1, Pallas kernels, on_small_mesh(): call(functools.partial(scale_kernel, total_rows), full, [VMEM] * 5, flops...  0.85 us
    convert_element_type x1, other arithmetic, on_small_mesh(): a_pattern.astype(jnp.float32)  0.74 us
  transfers between devices with their start and end apart: 13, of which 7 were waited for; matrix products, arithmetic and copies ran while one was open for 1% of the time, Pallas kernels for 2%

profile of v5, /device:TPU:0, one launch (start us, length us, event | category | flops | bytes accessed | tf_op | source)
XLA Modules:
  0.0 32.9 jit_solution(435311759365316733)
XLA Ops:
  0.0 0.7 %convert_element_type.12 = f32[4,2]{0,1:T(2,128)S(1)} convert(s32[4,2]{0,1:T(2,128)} %param.5) | non-fusion elementwise | flops 8 | bytes 64 | tf_op jit(solution)/shard_map/convert_element_type | solution.py:92
  0.7 0.1 copy.5
  0.8 0.2 mul.22
  1.2 4.1 %collective-permute-start.4 = (bf16[512,256]{1,0:T(8,128)(2,1)S(1)}, bf16[512,256]{1,0:T(8,128)(2,1)S(1)}, u32[]{:S(2)}, u32[]{:S(2)}) collective-permute-start(bf16[512,256]{1,0:T(8,128)(2,1)S(1)} %fusion.refs_0_.refs_4_), channel_id=1, source_target_pairs={{0,2},{2,3},{3,1},{1,0},{4,6},{6,7},{7,5},{5,4},{8,10},{10,11},{11... | collective-permute-start | bytes 786440 | tf_op jit(solution)/shard_map/ppermute | solution.py:94
  5.3 1.5 %collective-permute-start.3 = (bf16[512,256]{1,0:T(8,128)(2,1)S(1)}, bf16[512,256]{1,0:T(8,128)(2,1)S(1)}, u32[]{:S(2)}, u32[]{:S(2)}) collective-permute-start(bf16[512,256]{1,0:T(8,128)(2,1)S(1)} %fusion.refs_0_.refs_4_), channel_id=1, source_target_pairs={{0,8},{8,0},{16,24},{24,16},{1,9},{9,1},{17,25},{25,17},{2,10},{10... | collective-permute-start | bytes 786440 | tf_op jit(solution)/shard_map/ppermute | solution.py:72
  6.7 1.5 %collective-permute-start.2 = (bf16[512,256]{1,0:T(8,128)(2,1)S(1)}, bf16[512,256]{1,0:T(8,128)(2,1)S(1)}, u32[]{:S(2)}, u32[]{:S(2)}) collective-permute-start(bf16[512,256]{1,0:T(8,128)(2,1)S(1)} %fusion.refs_0_.refs_4_), channel_id=1, source_target_pairs={{0,16},{8,24},{16,0},{24,8},{1,17},{9,25},{17,1},{25,9},{2,18},{10... | collective-permute-start | bytes 786440 | tf_op jit(solution)/shard_map/ppermute | solution.py:72
  8.3 0.5 %collective-permute-start.1 = (bf16[512,256]{1,0:T(8,128)(2,1)S(1)}, bf16[512,256]{1,0:T(8,128)(2,1)S(1)}, u32[]{:S(2)}, u32[]{:S(2)}) collective-permute-start(bf16[512,256]{1,0:T(8,128)(2,1)S(1)} %fusion.refs_0_.refs_4_), channel_id=1, source_target_pairs={{0,24},{8,16},{16,8},{24,0},{1,25},{9,17},{17,9},{25,1},{2,26},{10... | collective-permute-start | bytes 786440 | tf_op jit(solution)/shard_map/ppermute | solution.py:72
  8.8 0.1 copy.6
  8.8 0.2 mul.25
  9.1 2.8 %collective-permute-done.4.refs_5_ = bf16[512,256]{1,0:T(8,128)(2,1)S(1)} collective-permute-done((bf16[512,256]{1,0:T(8,128)(2,1)S(1)}, bf16[512,256]{1,0:T(8,128)(2,1)S(1)}, u32[]{:S(2)}, u32[]{:S(2)}) %collective-permute-start.4) | collective-permute-done | bytes 262176 | tf_op jit(solution)/shard_map/ppermute | solution.py:94
  12.0 3.4 %collective-permute-start.5 = (bf16[512,256]{1,0:T(8,128)(2,1)S(1)}, bf16[512,256]{1,0:T(8,128)(2,1)S(1)}, u32[]{:S(2)}, u32[]{:S(2)}) collective-permute-start(bf16[512,256]{1,0:T(8,128)(2,1)S(1)} %collective-permute-done.4.refs_5_), channel_id=1, source_target_pairs={{0,2},{2,3},{3,1},{1,0},{4,6},{6,7},{7,5},{5,4},{8,10},{10,11},{11... | collective-permute-start | bytes 786440 | tf_op jit(solution)/shard_map/ppermute | solution.py:99
  15.4 4.5 %collective-permute-done.2.refs_2_ = bf16[512,256]{1,0:T(8,128)(2,1)S(1)} collective-permute-done((bf16[512,256]{1,0:T(8,128)(2,1)S(1)}, bf16[512,256]{1,0:T(8,128)(2,1)S(1)}, u32[]{:S(2)}, u32[]{:S(2)}) %collective-permute-start.2) | collective-permute-done | bytes 262176 | tf_op jit(solution)/shard_map/ppermute | solution.py:72
  19.9 0.5 %collective-permute-start.7 = (bf16[512,256]{1,0:T(8,128)(2,1)S(1)}, bf16[512,256]{1,0:T(8,128)(2,1)S(1)}, u32[]{:S(2)}, u32[]{:S(2)}) collective-permute-start(bf16[512,256]{1,0:T(8,128)(2,1)S(1)} %collective-permute-done.4.refs_5_), channel_id=1, source_target_pairs={{0,4},{4,0},{1,5},{5,1},{2,6},{6,2},{3,7},{7,3},{8,12},{12,8},{9,1... | collective-permute-start | bytes 786440 | tf_op jit(solution)/shard_map/ppermute | solution.py:72
  20.4 3.0 %collective-permute-done.5.left_own_ref = bf16[512,256]{1,0:T(8,128)(2,1)S(1)} collective-permute-done((bf16[512,256]{1,0:T(8,128)(2,1)S(1)}, bf16[512,256]{1,0:T(8,128)(2,1)S(1)}, u32[]{:S(2)}, u32[]{:S(2)}) %collective-permute-start.5) | collective-permute-done | bytes 262176 | tf_op jit(solution)/shard_map/ppermute | solution.py:99
  23.6 0.7 %shard_map.46 = (f32[512,256]{1,0:T(8,128)S(1)}, bf16[256,256]{1,0:T(8,128)(2,1)S(1)}, bf16[256,256]{1,0:T(8,128)(2,1)S(1)}) custom-call(bf16[512,256]{1,0:T(8,128)(2,1)S(1)} %fusion.refs_0_.refs_4_, bf16[512,256]{1,0:T(8,128)(2,1)S(1)} %collective-permute-done.3.refs_1_, bf16[512,256]{1,0:T(8,128)(2,1)S(1)} %collective-permute-done.2.refs_2_, ...), custom_call_target="tpu_custom_call" | custom-call | flops 402653184 | bytes 2621440 | tf_op jit(solution)/shard_map/pallas_call | solution.py:105
  24.2 0.8 %collective-permute-done.9.left_other_ref = bf16[512,256]{1,0:T(8,128)(2,1)S(1)} collective-permute-done((bf16[512,256]{1,0:T(8,128)(2,1)S(1)}, bf16[512,256]{1,0:T(8,128)(2,1)S(1)}, u32[]{:S(2)}, u32[]{:S(2)}) %collective-permute-start.9) | collective-permute-done | bytes 262176 | tf_op jit(solution)/shard_map/ppermute | solution.py:72
  25.1 0.3 shard_map.47
  25.4 2.5 %collective-permute-start.12 = (f32[8,256]{1,0:T(8,128)S(1)}, f32[8,256]{1,0:T(8,128)S(1)}, u32[]{:S(2)}, u32[]{:S(2)}) collective-permute-start(f32[8,256]{1,0:T(8,128)S(1)} %get-tuple-element.40.refs_0_), channel_id=1, source_target_pairs={{0,24},{8,16},{16,8},{24,0},{1,25},{9,17},{17,9},{25,1},{2,26},{10... | collective-permute-start | bytes 24584 | tf_op jit(solution)/shard_map/ppermute | solution.py:72
  27.9 0.5 %collective-permute-start.11 = (f32[8,256]{1,0:T(8,128)S(1)}, f32[8,256]{1,0:T(8,128)S(1)}, u32[]{:S(2)}, u32[]{:S(2)}) collective-permute-start(f32[8,256]{1,0:T(8,128)S(1)} %get-tuple-element.40.refs_0_), channel_id=1, source_target_pairs={{0,16},{8,24},{16,0},{24,8},{1,17},{9,25},{17,1},{25,9},{2,18},{10... | collective-permute-start | bytes 24584 | tf_op jit(solution)/shard_map/ppermute | solution.py:72
  28.4 0.5 %collective-permute-start.10 = (f32[8,256]{1,0:T(8,128)S(1)}, f32[8,256]{1,0:T(8,128)S(1)}, u32[]{:S(2)}, u32[]{:S(2)}) collective-permute-start(f32[8,256]{1,0:T(8,128)S(1)} %get-tuple-element.40.refs_0_), channel_id=1, source_target_pairs={{0,8},{8,0},{16,24},{24,16},{1,9},{9,1},{17,25},{25,17},{2,10},{10... | collective-permute-start | bytes 24584 | tf_op jit(solution)/shard_map/ppermute | solution.py:72
  28.9 1.1 %collective-permute-done.12.refs_3_ = f32[8,256]{1,0:T(8,128)S(1)} collective-permute-done((f32[8,256]{1,0:T(8,128)S(1)}, f32[8,256]{1,0:T(8,128)S(1)}, u32[]{:S(2)}, u32[]{:S(2)}) %collective-permute-start.12) | collective-permute-done | bytes 8224 | tf_op jit(solution)/shard_map/ppermute | solution.py:72
  30.0 1.5 %collective-permute-done.11.refs_2_ = f32[8,256]{1,0:T(8,128)S(1)} collective-permute-done((f32[8,256]{1,0:T(8,128)S(1)}, f32[8,256]{1,0:T(8,128)S(1)}, u32[]{:S(2)}, u32[]{:S(2)}) %collective-permute-start.11) | collective-permute-done | bytes 8224 | tf_op jit(solution)/shard_map/ppermute | solution.py:72
  31.6 0.5 %collective-permute-done.10.refs_1_ = f32[8,256]{1,0:T(8,128)S(1)} collective-permute-done((f32[8,256]{1,0:T(8,128)S(1)}, f32[8,256]{1,0:T(8,128)S(1)}, u32[]{:S(2)}, u32[]{:S(2)}) %collective-permute-start.10) | collective-permute-done | bytes 8224 | tf_op jit(solution)/shard_map/ppermute | solution.py:72
  32.1 0.8 %shard_map.48 = f32[512,256]{1,0:T(8,128)} custom-call(f32[512,256]{1,0:T(8,128)S(1)} %get-tuple-element.39.squares_ref, f32[8,256]{1,0:T(8,128)S(1)} %get-tuple-element.40.refs_0_, f32[8,256]{1,0:T(8,128)S(1)} %collective-permute-done.10.refs_1_, f32[8,256]{1,0:T(8,128)S(1)} %collective-permute-done.11.refs_2_, f32[8,256]{1,0:T(8,128)S(1)} %collective-permute-done.12.refs_3_), custom_call_target="tpu_custom_call" | custom-call | flops 524288 | bytes 1048576 | tf_op jit(solution)/shard_map/pallas_call | solution.py:121
  (19 shorter events, 0.3 us)
Async XLA Ops:
  0.0 1.1 %copy-start.1 = (f32[512,256]{1,0:T(8,128)S(1)}, f32[512,256]{1,0:T(8,128)}, u32[]{:S(2)}) copy-start(f32[512,256]{1,0:T(8,128)} %param.4) | copy-start | bytes 1572868
  1.1 7.7 %copy-start.2 = (s32[4,2]{0,1:T(2,128)S(1)}, s32[4,2]{0,1:T(2,128)}, u32[]{:S(2)}) copy-start(s32[4,2]{0,1:T(2,128)} %param.6) | copy-start | bytes 100
  1.2 7.9 %copy-start = (s32[512,256]{1,0:T(8,128)S(1)}, s32[512,256]{1,0:T(8,128)}, u32[]{:S(2)}) copy-start(s32[512,256]{1,0:T(8,128)} %param.7) | copy-start | bytes 1572868
  1.2 10.8 %collective-permute-start.4 = (bf16[512,256]{1,0:T(8,128)(2,1)S(1)}, bf16[512,256]{1,0:T(8,128)(2,1)S(1)}, u32[]{:S(2)}, u32[]{:S(2)}) collective-permute-start(bf16[512,256]{1,0:T(8,128)(2,1)S(1)} %fusion.refs_0_.refs_4_), channel_id=1, source_target_pairs={{0,2},{2,3},{3,1},{1,0},{4,6},{6,7},{7,5},{5,4},{8,10},{10,11},{11... | collective-permute-start | bytes 786440 | tf_op jit(solution)/shard_map/ppermute | solution.py:94
  5.3 10.1 %collective-permute-start.3 = (bf16[512,256]{1,0:T(8,128)(2,1)S(1)}, bf16[512,256]{1,0:T(8,128)(2,1)S(1)}, u32[]{:S(2)}, u32[]{:S(2)}) collective-permute-start(bf16[512,256]{1,0:T(8,128)(2,1)S(1)} %fusion.refs_0_.refs_4_), channel_id=1, source_target_pairs={{0,8},{8,0},{16,24},{24,16},{1,9},{9,1},{17,25},{25,17},{2,10},{10... | collective-permute-start | bytes 786440 | tf_op jit(solution)/shard_map/ppermute | solution.py:72
  6.7 13.1 %collective-permute-start.2 = (bf16[512,256]{1,0:T(8,128)(2,1)S(1)}, bf16[512,256]{1,0:T(8,128)(2,1)S(1)}, u32[]{:S(2)}, u32[]{:S(2)}) collective-permute-start(bf16[512,256]{1,0:T(8,128)(2,1)S(1)} %fusion.refs_0_.refs_4_), channel_id=1, source_target_pairs={{0,16},{8,24},{16,0},{24,8},{1,17},{9,25},{17,1},{25,9},{2,18},{10... | collective-permute-start | bytes 786440 | tf_op jit(solution)/shard_map/ppermute | solution.py:72
  8.3 11.6 %collective-permute-start.1 = (bf16[512,256]{1,0:T(8,128)(2,1)S(1)}, bf16[512,256]{1,0:T(8,128)(2,1)S(1)}, u32[]{:S(2)}, u32[]{:S(2)}) collective-permute-start(bf16[512,256]{1,0:T(8,128)(2,1)S(1)} %fusion.refs_0_.refs_4_), channel_id=1, source_target_pairs={{0,24},{8,16},{16,8},{24,0},{1,25},{9,17},{17,9},{25,1},{2,26},{10... | collective-permute-start | bytes 786440 | tf_op jit(solution)/shard_map/ppermute | solution.py:72
  8.7 11.1 %collective-permute-start = (bf16[512,256]{1,0:T(8,128)(2,1)S(1)}, bf16[512,256]{1,0:T(8,128)(2,1)S(1)}, u32[]{:S(2)}, u32[]{:S(2)}) collective-permute-start(bf16[512,256]{1,0:T(8,128)(2,1)S(1)} %fusion.refs_0_.refs_4_), channel_id=1, source_target_pairs={{2,0},{3,2},{1,3},{0,1},{6,4},{7,6},{5,7},{4,5},{10,8},{11,10},{9,... | collective-permute-start | bytes 786440 | tf_op jit(solution)/shard_map/ppermute | solution.py:95
  12.0 11.5 %collective-permute-start.5 = (bf16[512,256]{1,0:T(8,128)(2,1)S(1)}, bf16[512,256]{1,0:T(8,128)(2,1)S(1)}, u32[]{:S(2)}, u32[]{:S(2)}) collective-permute-start(bf16[512,256]{1,0:T(8,128)(2,1)S(1)} %collective-permute-done.4.refs_5_), channel_id=1, source_target_pairs={{0,2},{2,3},{3,1},{1,0},{4,6},{6,7},{7,5},{5,4},{8,10},{10,11},{11... | collective-permute-start | bytes 786440 | tf_op jit(solution)/shard_map/ppermute | solution.py:99
  19.9 3.6 %collective-permute-start.6 = (bf16[512,256]{1,0:T(8,128)(2,1)S(1)}, bf16[512,256]{1,0:T(8,128)(2,1)S(1)}, u32[]{:S(2)}, u32[]{:S(2)}) collective-permute-start(bf16[512,256]{1,0:T(8,128)(2,1)S(1)} %fusion.refs_0_.refs_4_), channel_id=1, source_target_pairs={{0,4},{4,0},{1,5},{5,1},{2,6},{6,2},{3,7},{7,3},{8,12},{12,8},{9,1... | collective-permute-start | bytes 786440 | tf_op jit(solution)/shard_map/ppermute | solution.py:72
  19.9 3.6 %collective-permute-start.7 = (bf16[512,256]{1,0:T(8,128)(2,1)S(1)}, bf16[512,256]{1,0:T(8,128)(2,1)S(1)}, u32[]{:S(2)}, u32[]{:S(2)}) collective-permute-start(bf16[512,256]{1,0:T(8,128)(2,1)S(1)} %collective-permute-done.4.refs_5_), channel_id=1, source_target_pairs={{0,4},{4,0},{1,5},{5,1},{2,6},{6,2},{3,7},{7,3},{8,12},{12,8},{9,1... | collective-permute-start | bytes 786440 | tf_op jit(solution)/shard_map/ppermute | solution.py:72
  20.4 3.1 %collective-permute-start.8 = (bf16[512,256]{1,0:T(8,128)(2,1)S(1)}, bf16[512,256]{1,0:T(8,128)(2,1)S(1)}, u32[]{:S(2)}, u32[]{:S(2)}) collective-permute-start(bf16[512,256]{1,0:T(8,128)(2,1)S(1)} %collective-permute-done.refs_6_), channel_id=1, source_target_pairs={{0,4},{4,0},{1,5},{5,1},{2,6},{6,2},{3,7},{7,3},{8,12},{12,8},{9,1... | collective-permute-start | bytes 786440 | tf_op jit(solution)/shard_map/ppermute | solution.py:72
  23.5 1.6 %collective-permute-start.9 = (bf16[512,256]{1,0:T(8,128)(2,1)S(1)}, bf16[512,256]{1,0:T(8,128)(2,1)S(1)}, u32[]{:S(2)}, u32[]{:S(2)}) collective-permute-start(bf16[512,256]{1,0:T(8,128)(2,1)S(1)} %collective-permute-done.5.left_own_ref), channel_id=1, source_target_pairs={{0,4},{4,0},{1,5},{5,1},{2,6},{6,2},{3,7},{7,3},{8,12},{12,8},{9,1... | collective-permute-start | bytes 786440 | tf_op jit(solution)/shard_map/ppermute | solution.py:72
  25.4 4.6 %collective-permute-start.12 = (f32[8,256]{1,0:T(8,128)S(1)}, f32[8,256]{1,0:T(8,128)S(1)}, u32[]{:S(2)}, u32[]{:S(2)}) collective-permute-start(f32[8,256]{1,0:T(8,128)S(1)} %get-tuple-element.40.refs_0_), channel_id=1, source_target_pairs={{0,24},{8,16},{16,8},{24,0},{1,25},{9,17},{17,9},{25,1},{2,26},{10... | collective-permute-start | bytes 24584 | tf_op jit(solution)/shard_map/ppermute | solution.py:72
  27.9 3.7 %collective-permute-start.11 = (f32[8,256]{1,0:T(8,128)S(1)}, f32[8,256]{1,0:T(8,128)S(1)}, u32[]{:S(2)}, u32[]{:S(2)}) collective-permute-start(f32[8,256]{1,0:T(8,128)S(1)} %get-tuple-element.40.refs_0_), channel_id=1, source_target_pairs={{0,16},{8,24},{16,0},{24,8},{1,17},{9,25},{17,1},{25,9},{2,18},{10... | collective-permute-start | bytes 24584 | tf_op jit(solution)/shard_map/ppermute | solution.py:72
  28.4 3.7 %collective-permute-start.10 = (f32[8,256]{1,0:T(8,128)S(1)}, f32[8,256]{1,0:T(8,128)S(1)}, u32[]{:S(2)}, u32[]{:S(2)}) collective-permute-start(f32[8,256]{1,0:T(8,128)S(1)} %get-tuple-element.40.refs_0_), channel_id=1, source_target_pairs={{0,8},{8,0},{16,24},{24,16},{1,9},{9,1},{17,25},{25,17},{2,10},{10... | collective-permute-start | bytes 24584 | tf_op jit(solution)/shard_map/ppermute | solution.py:72

commit v6 on v5

--- a/solution.py
+++ b/solution.py
@@ -30,8 +30,8 @@
 
 
 def most_kernel(*refs):
-    right, here, there = refs[:4], refs[4:7], refs[7:10]
-    total_ref, own_ref, other_ref, panel_ref = refs[10:]
+    right, here, there = refs[:4], refs[4:8], list(refs[8:11])
+    total_ref, other_ref, panel_ref = refs[11:]
     parity = lax.axis_index("col")
     layer = lax.axis_index("layer")
     lead = lax.axis_index("row") ^ layer
@@ -40,23 +40,21 @@
     for s in range(4):
         panel_ref[s ^ lead] = right[s][...]
     total = None
-    for s, distance in enumerate((0, 1 + middle, 2 - middle)):
-        for side, block in enumerate((here[s], there[s])):
+    for s, distance in enumerate((0, 1 + middle, 2 - middle, 3)):
+        for side, block in enumerate([here[s]] + there[s : s + 1]):
             rows = pl.ds(pl.multiple_of((parity ^ side) * half, half), half)
             part = jnp.dot(block[...], panel_ref[distance, rows, :], preferred_element_type=jnp.float32)
             total = part if total is None else total + part
     total_ref[...] = total
-    own_ref[...] = panel_ref[3, pl.ds(pl.multiple_of(parity * half, half), half), :]
     other_ref[...] = panel_ref[3, pl.ds(pl.multiple_of((1 - parity) * half, half), half), :]
 
 
-def squares_kernel(total_ref, left_own_ref, left_other_ref, own_ref, other_ref, weight_ref, squares_ref, sums_ref):
-    product = total_ref[...] + jnp.dot(left_own_ref[...], own_ref[...], preferred_element_type=jnp.float32)
-    product = product + jnp.dot(left_other_ref[...], other_ref[...], preferred_element_type=jnp.float32)
+def squares_kernel(total_ref, left_ref, right_ref, weight_ref, squares_ref, sums_ref):
+    product = total_ref[...] + jnp.dot(left_ref[...], right_ref[...], preferred_element_type=jnp.float32)
     squares = product * product * weight_ref[...]
     squares_ref[...] = squares
     rows, cols = squares.shape
-    sums_ref[...] = jnp.sum(squares.reshape(rows // 8, 8, cols), axis=0)
+    sums_ref[...] = jnp.sum(squares, axis=0, keepdims=True)
 
 
 def scale_kernel(total_rows, squares_ref, *refs):
@@ -64,7 +62,7 @@
     column = sums[0][...]
     for other in sums[1:]:
         column = column + other[...]
-    column = jnp.sum(column, axis=0, keepdims=True) + epsilon
+    column = column + epsilon
     out_ref[...] = total_rows * squares_ref[...] / column
 
 
@@ -102,21 +100,21 @@
     there = [swap(x, "col", 2, 1) for x in here]
     far, *there = lax.optimization_barrier((far, *there))
     far_other = swap(far, "col", 2, 1)
-    total, last_own, last_other = call(
+    total, last = call(
         most_kernel,
-        [full, jax.ShapeDtypeStruct((cols, cols), jnp.bfloat16), jax.ShapeDtypeStruct((cols, cols), jnp.bfloat16)],
-        [VMEM] * 10,
+        [full, jax.ShapeDtypeStruct((cols, cols), jnp.bfloat16)],
+        [VMEM] * 11,
         flops=2 * rows * cols * 3 * rows,
         size=2 * 10 * rows * cols,
         scratch_shapes=[pltpu.VMEM((4, rows, cols), jnp.bfloat16)],
-    )(*right, *here, *there)
+    )(*right, *here, far, *there)
     squares, sums = call(
         squares_kernel,
-        [full, jax.ShapeDtypeStruct((8, cols), jnp.float32)],
-        [VMEM] * 6,
+        [full, jax.ShapeDtypeStruct((1, cols), jnp.float32)],
+        [VMEM] * 4,
         flops=2 * rows * cols * rows,
         size=16 * rows * cols,
-    )(total, far, far_other, last_own, last_other, weight)
+    )(total, far_other, last, weight)
     others = [swap(sums, "row", 4, s) for s in (1, 2, 3)]
     return call(
         functools.partial(scale_kernel, total_rows), full, [VMEM] * 5, flops=4 * rows * cols, size=8 * rows * cols

time: 33.1 us -> 32.9 us (level)
  no operation moved by 1% of the time
where the time goes in v6:
time: 32.9 us; the launch traced here: 32.8 us
  starting transfers between devices  15.2 us (46%)
  waiting for transfers between devices  14.2 us (43%)
  Pallas kernels  1.84 us (6%)
  other arithmetic  0.89 us (3%)
  local copies, waits for them, and re-layouts  0.62 us (2%)
    ppermute x10, waiting for transfers between devices, swap(): return lax.ppermute(x, axis, [(i, i ^ s) for i in range(size)])  8.31 us
    ppermute x10, starting transfers between devices, swap(): return lax.ppermute(x, axis, [(i, i ^ s) for i in range(size)])  7.69 us
    ppermute x1, starting transfers between devices, on_small_mesh(): first = lax.ppermute(own, 'layer', ring)  4.09 us
    ppermute x1, starting transfers between devices, on_small_mesh(): far = lax.ppermute(first, 'layer', ring)  3.38 us
    ppermute x1, waiting for transfers between devices, on_small_mesh(): far = lax.ppermute(first, 'layer', ring)  3.03 us
    ppermute x1, waiting for transfers between devices, on_small_mesh(): first = lax.ppermute(own, 'layer', ring)  2.83 us
    pallas_call x1, Pallas kernels, on_small_mesh(): call(functools.partial(scale_kernel, total_rows), full, [VMEM] * 5, flops...  0.84 us
    convert_element_type x1, other arithmetic, on_small_mesh(): a_pattern.astype(jnp.float32)  0.74 us
  transfers between devices with their start and end apart: 13, of which 7 were waited for; matrix products, arithmetic and copies ran while one was open for 1% of the time, Pallas kernels for 2%

profile of v6, /device:TPU:0, one launch (start us, length us, event | category | flops | bytes accessed | tf_op | source)
XLA Modules:
  0.0 32.8 jit_solution(10666346866928179737)
XLA Ops:
  0.0 0.7 %convert_element_type.12 = f32[4,2]{0,1:T(2,128)S(1)} convert(s32[4,2]{0,1:T(2,128)} %param.5) | non-fusion elementwise | flops 8 | bytes 64 | tf_op jit(solution)/shard_map/convert_element_type | solution.py:90
  0.7 0.1 copy.5
  0.8 0.2 mul.22
  1.2 4.1 %collective-permute-start.4 = (bf16[512,256]{1,0:T(8,128)(2,1)S(1)}, bf16[512,256]{1,0:T(8,128)(2,1)S(1)}, u32[]{:S(2)}, u32[]{:S(2)}) collective-permute-start(bf16[512,256]{1,0:T(8,128)(2,1)S(1)} %fusion.refs_0_.refs_4_), channel_id=1, source_target_pairs={{0,2},{2,3},{3,1},{1,0},{4,6},{6,7},{7,5},{5,4},{8,10},{10,11},{11... | collective-permute-start | bytes 786440 | tf_op jit(solution)/shard_map/ppermute | solution.py:92
  5.3 1.5 %collective-permute-start.3 = (bf16[512,256]{1,0:T(8,128)(2,1)S(1)}, bf16[512,256]{1,0:T(8,128)(2,1)S(1)}, u32[]{:S(2)}, u32[]{:S(2)}) collective-permute-start(bf16[512,256]{1,0:T(8,128)(2,1)S(1)} %fusion.refs_0_.refs_4_), channel_id=1, source_target_pairs={{0,8},{8,0},{16,24},{24,16},{1,9},{9,1},{17,25},{25,17},{2,10},{10... | collective-permute-start | bytes 786440 | tf_op jit(solution)/shard_map/ppermute | solution.py:70
  6.7 1.5 %collective-permute-start.2 = (bf16[512,256]{1,0:T(8,128)(2,1)S(1)}, bf16[512,256]{1,0:T(8,128)(2,1)S(1)}, u32[]{:S(2)}, u32[]{:S(2)}) collective-permute-start(bf16[512,256]{1,0:T(8,128)(2,1)S(1)} %fusion.refs_0_.refs_4_), channel_id=1, source_target_pairs={{0,16},{8,24},{16,0},{24,8},{1,17},{9,25},{17,1},{25,9},{2,18},{10... | collective-permute-start | bytes 786440 | tf_op jit(solution)/shard_map/ppermute | solution.py:70
  8.3 0.5 %collective-permute-start.1 = (bf16[512,256]{1,0:T(8,128)(2,1)S(1)}, bf16[512,256]{1,0:T(8,128)(2,1)S(1)}, u32[]{:S(2)}, u32[]{:S(2)}) collective-permute-start(bf16[512,256]{1,0:T(8,128)(2,1)S(1)} %fusion.refs_0_.refs_4_), channel_id=1, source_target_pairs={{0,24},{8,16},{16,8},{24,0},{1,25},{9,17},{17,9},{25,1},{2,26},{10... | collective-permute-start | bytes 786440 | tf_op jit(solution)/shard_map/ppermute | solution.py:70
  8.8 0.1 copy.6
  8.8 0.2 mul.25
  9.1 2.8 %collective-permute-done.4.refs_5_ = bf16[512,256]{1,0:T(8,128)(2,1)S(1)} collective-permute-done((bf16[512,256]{1,0:T(8,128)(2,1)S(1)}, bf16[512,256]{1,0:T(8,128)(2,1)S(1)}, u32[]{:S(2)}, u32[]{:S(2)}) %collective-permute-start.4) | collective-permute-done | bytes 262176 | tf_op jit(solution)/shard_map/ppermute | solution.py:92
  12.0 3.4 %collective-permute-start.5 = (bf16[512,256]{1,0:T(8,128)(2,1)S(1)}, bf16[512,256]{1,0:T(8,128)(2,1)S(1)}, u32[]{:S(2)}, u32[]{:S(2)}) collective-permute-start(bf16[512,256]{1,0:T(8,128)(2,1)S(1)} %collective-permute-done.4.refs_5_), channel_id=1, source_target_pairs={{0,2},{2,3},{3,1},{1,0},{4,6},{6,7},{7,5},{5,4},{8,10},{10,11},{11... | collective-permute-start | bytes 786440 | tf_op jit(solution)/shard_map/ppermute | solution.py:97
  15.4 4.5 %collective-permute-done.2.refs_2_ = bf16[512,256]{1,0:T(8,128)(2,1)S(1)} collective-permute-done((bf16[512,256]{1,0:T(8,128)(2,1)S(1)}, bf16[512,256]{1,0:T(8,128)(2,1)S(1)}, u32[]{:S(2)}, u32[]{:S(2)}) %collective-permute-start.2) | collective-permute-done | bytes 262176 | tf_op jit(solution)/shard_map/ppermute | solution.py:70
  19.9 0.5 %collective-permute-start.7 = (bf16[512,256]{1,0:T(8,128)(2,1)S(1)}, bf16[512,256]{1,0:T(8,128)(2,1)S(1)}, u32[]{:S(2)}, u32[]{:S(2)}) collective-permute-start(bf16[512,256]{1,0:T(8,128)(2,1)S(1)} %collective-permute-done.4.refs_5_), channel_id=1, source_target_pairs={{0,4},{4,0},{1,5},{5,1},{2,6},{6,2},{3,7},{7,3},{8,12},{12,8},{9,1... | collective-permute-start | bytes 786440 | tf_op jit(solution)/shard_map/ppermute | solution.py:70
  20.4 3.0 %collective-permute-done.5.refs_7_ = bf16[512,256]{1,0:T(8,128)(2,1)S(1)} collective-permute-done((bf16[512,256]{1,0:T(8,128)(2,1)S(1)}, bf16[512,256]{1,0:T(8,128)(2,1)S(1)}, u32[]{:S(2)}, u32[]{:S(2)}) %collective-permute-start.5) | collective-permute-done | bytes 262176 | tf_op jit(solution)/shard_map/ppermute | solution.py:97
  23.6 0.7 %shard_map.46 = (f32[512,256]{1,0:T(8,128)S(1)}, bf16[256,256]{1,0:T(8,128)(2,1)S(1)}) custom-call(bf16[512,256]{1,0:T(8,128)(2,1)S(1)} %fusion.refs_0_.refs_4_, bf16[512,256]{1,0:T(8,128)(2,1)S(1)} %collective-permute-done.3.refs_1_, bf16[512,256]{1,0:T(8,128)(2,1)S(1)} %collective-permute-done.2.refs_2_, ...), custom_call_target="tpu_custom_call" | custom-call | flops 402653184 | bytes 2621440 | tf_op jit(solution)/shard_map/pallas_call | solution.py:103
  24.3 0.8 %collective-permute-done.9.left_ref = bf16[512,256]{1,0:T(8,128)(2,1)S(1)} collective-permute-done((bf16[512,256]{1,0:T(8,128)(2,1)S(1)}, bf16[512,256]{1,0:T(8,128)(2,1)S(1)}, u32[]{:S(2)}, u32[]{:S(2)}) %collective-permute-start.9) | collective-permute-done | bytes 262176 | tf_op jit(solution)/shard_map/ppermute | solution.py:70
  25.1 0.3 shard_map.47
  25.4 2.5 %collective-permute-start.12 = (f32[1,256]{1,0:T(1,128)S(1)}, f32[1,256]{1,0:T(1,128)S(1)}, u32[]{:S(2)}, u32[]{:S(2)}) collective-permute-start(f32[1,256]{1,0:T(1,128)S(1)} %get-tuple-element.38.refs_0_), channel_id=1, source_target_pairs={{0,24},{8,16},{16,8},{24,0},{1,25},{9,17},{17,9},{25,1},{2,26},{10... | collective-permute-start | bytes 3080 | tf_op jit(solution)/shard_map/ppermute | solution.py:70
  27.9 0.5 %collective-permute-start.11 = (f32[1,256]{1,0:T(1,128)S(1)}, f32[1,256]{1,0:T(1,128)S(1)}, u32[]{:S(2)}, u32[]{:S(2)}) collective-permute-start(f32[1,256]{1,0:T(1,128)S(1)} %get-tuple-element.38.refs_0_), channel_id=1, source_target_pairs={{0,16},{8,24},{16,0},{24,8},{1,17},{9,25},{17,1},{25,9},{2,18},{10... | collective-permute-start | bytes 3080 | tf_op jit(solution)/shard_map/ppermute | solution.py:70
  28.4 0.5 %collective-permute-start.10 = (f32[1,256]{1,0:T(1,128)S(1)}, f32[1,256]{1,0:T(1,128)S(1)}, u32[]{:S(2)}, u32[]{:S(2)}) collective-permute-start(f32[1,256]{1,0:T(1,128)S(1)} %get-tuple-element.38.refs_0_), channel_id=1, source_target_pairs={{0,8},{8,0},{16,24},{24,16},{1,9},{9,1},{17,25},{25,17},{2,10},{10... | collective-permute-start | bytes 3080 | tf_op jit(solution)/shard_map/ppermute | solution.py:70
  28.9 1.0 %collective-permute-done.12.refs_3_ = f32[1,256]{1,0:T(1,128)S(1)} collective-permute-done((f32[1,256]{1,0:T(1,128)S(1)}, f32[1,256]{1,0:T(1,128)S(1)}, u32[]{:S(2)}, u32[]{:S(2)}) %collective-permute-start.12) | collective-permute-done | bytes 1056 | tf_op jit(solution)/shard_map/ppermute | solution.py:70
  29.9 1.6 %collective-permute-done.11.refs_2_ = f32[1,256]{1,0:T(1,128)S(1)} collective-permute-done((f32[1,256]{1,0:T(1,128)S(1)}, f32[1,256]{1,0:T(1,128)S(1)}, u32[]{:S(2)}, u32[]{:S(2)}) %collective-permute-start.11) | collective-permute-done | bytes 1056 | tf_op jit(solution)/shard_map/ppermute | solution.py:70
  31.4 0.5 %collective-permute-done.10.refs_1_ = f32[1,256]{1,0:T(1,128)S(1)} collective-permute-done((f32[1,256]{1,0:T(1,128)S(1)}, f32[1,256]{1,0:T(1,128)S(1)}, u32[]{:S(2)}, u32[]{:S(2)}) %collective-permute-start.10) | collective-permute-done | bytes 1056 | tf_op jit(solution)/shard_map/ppermute | solution.py:70
  32.0 0.8 %shard_map.48 = f32[512,256]{1,0:T(8,128)} custom-call(f32[512,256]{1,0:T(8,128)S(1)} %get-tuple-element.37.squares_ref, f32[1,256]{1,0:T(1,128)S(1)} %get-tuple-element.38.refs_0_, f32[1,256]{1,0:T(1,128)S(1)} %collective-permute-done.10.refs_1_, f32[1,256]{1,0:T(1,128)S(1)} %collective-permute-done.11.refs_2_, f32[1,256]{1,0:T(1,128)S(1)} %collective-permute-done.12.refs_3_), custom_call_target="tpu_custom_call" | custom-call | flops 524288 | bytes 1048576 | tf_op jit(solution)/shard_map/pallas_call | solution.py:119
  (19 shorter events, 0.3 us)
Async XLA Ops:
  0.0 1.1 %copy-start.1 = (f32[512,256]{1,0:T(8,128)S(1)}, f32[512,256]{1,0:T(8,128)}, u32[]{:S(2)}) copy-start(f32[512,256]{1,0:T(8,128)} %param.4) | copy-start | bytes 1572868
  1.1 7.7 %copy-start.2 = (s32[4,2]{0,1:T(2,128)S(1)}, s32[4,2]{0,1:T(2,128)}, u32[]{:S(2)}) copy-start(s32[4,2]{0,1:T(2,128)} %param.6) | copy-start | bytes 100
  1.2 7.9 %copy-start = (s32[512,256]{1,0:T(8,128)S(1)}, s32[512,256]{1,0:T(8,128)}, u32[]{:S(2)}) copy-start(s32[512,256]{1,0:T(8,128)} %param.7) | copy-start | bytes 1572868
  1.2 10.8 %collective-permute-start.4 = (bf16[512,256]{1,0:T(8,128)(2,1)S(1)}, bf16[512,256]{1,0:T(8,128)(2,1)S(1)}, u32[]{:S(2)}, u32[]{:S(2)}) collective-permute-start(bf16[512,256]{1,0:T(8,128)(2,1)S(1)} %fusion.refs_0_.refs_4_), channel_id=1, source_target_pairs={{0,2},{2,3},{3,1},{1,0},{4,6},{6,7},{7,5},{5,4},{8,10},{10,11},{11... | collective-permute-start | bytes 786440 | tf_op jit(solution)/shard_map/ppermute | solution.py:92
  5.3 10.1 %collective-permute-start.3 = (bf16[512,256]{1,0:T(8,128)(2,1)S(1)}, bf16[512,256]{1,0:T(8,128)(2,1)S(1)}, u32[]{:S(2)}, u32[]{:S(2)}) collective-permute-start(bf16[512,256]{1,0:T(8,128)(2,1)S(1)} %fusion.refs_0_.refs_4_), channel_id=1, source_target_pairs={{0,8},{8,0},{16,24},{24,16},{1,9},{9,1},{17,25},{25,17},{2,10},{10... | collective-permute-start | bytes 786440 | tf_op jit(solution)/shard_map/ppermute | solution.py:70
  6.7 13.1 %collective-permute-start.2 = (bf16[512,256]{1,0:T(8,128)(2,1)S(1)}, bf16[512,256]{1,0:T(8,128)(2,1)S(1)}, u32[]{:S(2)}, u32[]{:S(2)}) collective-permute-start(bf16[512,256]{1,0:T(8,128)(2,1)S(1)} %fusion.refs_0_.refs_4_), channel_id=1, source_target_pairs={{0,16},{8,24},{16,0},{24,8},{1,17},{9,25},{17,1},{25,9},{2,18},{10... | collective-permute-start | bytes 786440 | tf_op jit(solution)/shard_map/ppermute | solution.py:70
  8.3 11.6 %collective-permute-start.1 = (bf16[512,256]{1,0:T(8,128)(2,1)S(1)}, bf16[512,256]{1,0:T(8,128)(2,1)S(1)}, u32[]{:S(2)}, u32[]{:S(2)}) collective-permute-start(bf16[512,256]{1,0:T(8,128)(2,1)S(1)} %fusion.refs_0_.refs_4_), channel_id=1, source_target_pairs={{0,24},{8,16},{16,8},{24,0},{1,25},{9,17},{17,9},{25,1},{2,26},{10... | collective-permute-start | bytes 786440 | tf_op jit(solution)/shard_map/ppermute | solution.py:70
  8.7 11.1 %collective-permute-start = (bf16[512,256]{1,0:T(8,128)(2,1)S(1)}, bf16[512,256]{1,0:T(8,128)(2,1)S(1)}, u32[]{:S(2)}, u32[]{:S(2)}) collective-permute-start(bf16[512,256]{1,0:T(8,128)(2,1)S(1)} %fusion.refs_0_.refs_4_), channel_id=1, source_target_pairs={{2,0},{3,2},{1,3},{0,1},{6,4},{7,6},{5,7},{4,5},{10,8},{11,10},{9,... | collective-permute-start | bytes 786440 | tf_op jit(solution)/shard_map/ppermute | solution.py:93
  12.0 11.5 %collective-permute-start.5 = (bf16[512,256]{1,0:T(8,128)(2,1)S(1)}, bf16[512,256]{1,0:T(8,128)(2,1)S(1)}, u32[]{:S(2)}, u32[]{:S(2)}) collective-permute-start(bf16[512,256]{1,0:T(8,128)(2,1)S(1)} %collective-permute-done.4.refs_5_), channel_id=1, source_target_pairs={{0,2},{2,3},{3,1},{1,0},{4,6},{6,7},{7,5},{5,4},{8,10},{10,11},{11... | collective-permute-start | bytes 786440 | tf_op jit(solution)/shard_map/ppermute | solution.py:97
  19.9 3.6 %collective-permute-start.6 = (bf16[512,256]{1,0:T(8,128)(2,1)S(1)}, bf16[512,256]{1,0:T(8,128)(2,1)S(1)}, u32[]{:S(2)}, u32[]{:S(2)}) collective-permute-start(bf16[512,256]{1,0:T(8,128)(2,1)S(1)} %fusion.refs_0_.refs_4_), channel_id=1, source_target_pairs={{0,4},{4,0},{1,5},{5,1},{2,6},{6,2},{3,7},{7,3},{8,12},{12,8},{9,1... | collective-permute-start | bytes 786440 | tf_op jit(solution)/shard_map/ppermute | solution.py:70
  19.9 3.6 %collective-permute-start.7 = (bf16[512,256]{1,0:T(8,128)(2,1)S(1)}, bf16[512,256]{1,0:T(8,128)(2,1)S(1)}, u32[]{:S(2)}, u32[]{:S(2)}) collective-permute-start(bf16[512,256]{1,0:T(8,128)(2,1)S(1)} %collective-permute-done.4.refs_5_), channel_id=1, source_target_pairs={{0,4},{4,0},{1,5},{5,1},{2,6},{6,2},{3,7},{7,3},{8,12},{12,8},{9,1... | collective-permute-start | bytes 786440 | tf_op jit(solution)/shard_map/ppermute | solution.py:70
  20.4 3.1 %collective-permute-start.8 = (bf16[512,256]{1,0:T(8,128)(2,1)S(1)}, bf16[512,256]{1,0:T(8,128)(2,1)S(1)}, u32[]{:S(2)}, u32[]{:S(2)}) collective-permute-start(bf16[512,256]{1,0:T(8,128)(2,1)S(1)} %collective-permute-done.refs_6_), channel_id=1, source_target_pairs={{0,4},{4,0},{1,5},{5,1},{2,6},{6,2},{3,7},{7,3},{8,12},{12,8},{9,1... | collective-permute-start | bytes 786440 | tf_op jit(solution)/shard_map/ppermute | solution.py:70
  23.5 1.6 %collective-permute-start.9 = (bf16[512,256]{1,0:T(8,128)(2,1)S(1)}, bf16[512,256]{1,0:T(8,128)(2,1)S(1)}, u32[]{:S(2)}, u32[]{:S(2)}) collective-permute-start(bf16[512,256]{1,0:T(8,128)(2,1)S(1)} %collective-permute-done.5.refs_7_), channel_id=1, source_target_pairs={{0,4},{4,0},{1,5},{5,1},{2,6},{6,2},{3,7},{7,3},{8,12},{12,8},{9,1... | collective-permute-start | bytes 786440 | tf_op jit(solution)/shard_map/ppermute | solution.py:70
  25.4 4.5 %collective-permute-start.12 = (f32[1,256]{1,0:T(1,128)S(1)}, f32[1,256]{1,0:T(1,128)S(1)}, u32[]{:S(2)}, u32[]{:S(2)}) collective-permute-start(f32[1,256]{1,0:T(1,128)S(1)} %get-tuple-element.38.refs_0_), channel_id=1, source_target_pairs={{0,24},{8,16},{16,8},{24,0},{1,25},{9,17},{17,9},{25,1},{2,26},{10... | collective-permute-start | bytes 3080 | tf_op jit(solution)/shard_map/ppermute | solution.py:70
  27.9 3.6 %collective-permute-start.11 = (f32[1,256]{1,0:T(1,128)S(1)}, f32[1,256]{1,0:T(1,128)S(1)}, u32[]{:S(2)}, u32[]{:S(2)}) collective-permute-start(f32[1,256]{1,0:T(1,128)S(1)} %get-tuple-element.38.refs_0_), channel_id=1, source_target_pairs={{0,16},{8,24},{16,0},{24,8},{1,17},{9,25},{17,1},{25,9},{2,18},{10... | collective-permute-start | bytes 3080 | tf_op jit(solution)/shard_map/ppermute | solution.py:70
  28.4 3.6 %collective-permute-start.10 = (f32[1,256]{1,0:T(1,128)S(1)}, f32[1,256]{1,0:T(1,128)S(1)}, u32[]{:S(2)}, u32[]{:S(2)}) collective-permute-start(f32[1,256]{1,0:T(1,128)S(1)} %get-tuple-element.38.refs_0_), channel_id=1, source_target_pairs={{0,8},{8,0},{16,24},{24,16},{1,9},{9,1},{17,25},{25,17},{2,10},{10... | collective-permute-start | bytes 3080 | tf_op jit(solution)/shard_map/ppermute | solution.py:70

commit v7 on v6

--- a/solution.py
+++ b/solution.py
@@ -90,12 +90,28 @@
     own = times_tiles(values, a_pattern.astype(jnp.float32)).astype(jnp.bfloat16)
     ring = [(0, 2), (2, 3), (3, 1), (1, 0)]
     first = lax.ppermute(own, "layer", ring)
-    second = lax.ppermute(own, "layer", [(b, a) for a, b in ring])
-    right = [own] + [swap(own, "row", 4, s) for s in (1, 2, 3)]
+    back = {a: b for b, a in ring}
+    mixed = [
+        lax.ppermute(
+            own,
+            ("row", "col", "layer"),
+            [
+                (8 * r + 4 * c + z, 8 * r + 4 * c + back[z] if c == core else 8 * (r ^ 1) + 4 * c + z)
+                for r in range(4)
+                for c in range(2)
+                for z in range(4)
+            ],
+        )
+        for core in range(2)
+    ]
+    right = [own, None] + [swap(own, "row", 4, s) for s in (2, 3)]
     weight = times_tiles(prune_mask.astype(jnp.float32), c_pattern.astype(jnp.float32))
     first, start, weight = lax.optimization_barrier((first, own, weight))
     far = lax.ppermute(first, "layer", ring)
-    second, right[3], right[2], right[1], first, start = lax.optimization_barrier((second, right[3], right[2], right[1], first, start))
+    right[3], right[2], mixed[1], mixed[0], first, start = lax.optimization_barrier((right[3], right[2], mixed[1], mixed[0], first, start))
+    first_core = lax.axis_index("col") == 0
+    second = jnp.where(first_core, mixed[0], mixed[1])
+    right[1] = jnp.where(first_core, mixed[1], mixed[0])
     here = [start, first, second]
     there = [swap(x, "col", 2, 1) for x in here]
     far, *there = lax.optimization_barrier((far, *there))

time: 32.9 us -> 32.9 us (level)
    ppermute x10 -> x9, waiting for transfers between devices: 8.31 us -> 4.24 us  [swap(): return lax.ppermute(x, axis, [(i, i ^ s) for i in range(size)])]
    ppermute x1 -> x2, waiting for transfers between devices: 0.01 us -> 4.05 us  [on_small_mesh(): lax.ppermute(own, ('row', 'col', 'layer'), [(8 * r + 4 * c + z, 8 * r + 4...]
    ppermute x1 -> x2, starting transfers between devices: 0.01 us -> 1.49 us  [on_small_mesh(): lax.ppermute(own, ('row', 'col', 'layer'), [(8 * r + 4 * c + z, 8 * r + 4...]
    ppermute x10 -> x9, starting transfers between devices: 7.69 us -> 6.27 us  [swap(): return lax.ppermute(x, axis, [(i, i ^ s) for i in range(size)])]
  transfers between devices with their start and end apart: 13 -> 13, of which waited for: 7 -> 8; matrix products, arithmetic and copies ran while one was open for 1% -> 1% of each run, Pallas kernels for 2% -> 2%
where the time goes in v7:
time: 32.9 us; the launch traced here: 32.8 us
  starting transfers between devices  15.2 us (46%)
  waiting for transfers between devices  14.1 us (43%)
  Pallas kernels  1.84 us (6%)
  other arithmetic  0.93 us (3%)
  local copies, waits for them, and re-layouts  0.63 us (2%)
    ppermute x9, starting transfers between devices, swap(): return lax.ppermute(x, axis, [(i, i ^ s) for i in range(size)])  6.27 us
    ppermute x9, waiting for transfers between devices, swap(): return lax.ppermute(x, axis, [(i, i ^ s) for i in range(size)])  4.24 us
    ppermute x1, starting transfers between devices, on_small_mesh(): first = lax.ppermute(own, 'layer', ring)  4.09 us
    ppermute x2, waiting for transfers between devices, on_small_mesh(): lax.ppermute(own, ('row', 'col', 'layer'), [(8 * r + 4 * c + z, 8 * r + 4...  4.05 us
    ppermute x1, starting transfers between devices, on_small_mesh(): far = lax.ppermute(first, 'layer', ring)  3.38 us
    ppermute x1, waiting for transfers between devices, on_small_mesh(): far = lax.ppermute(first, 'layer', ring)  2.92 us
    ppermute x1, waiting for transfers between devices, on_small_mesh(): first = lax.ppermute(own, 'layer', ring)  2.86 us
    ppermute x2, starting transfers between devices, on_small_mesh(): lax.ppermute(own, ('row', 'col', 'layer'), [(8 * r + 4 * c + z, 8 * r + 4...  1.49 us
  transfers between devices with their start and end apart: 13, of which 8 were waited for; matrix products, arithmetic and copies ran while one was open for 1% of the time, Pallas kernels for 2%

profile of v7, /device:TPU:0, one launch (start us, length us, event | category | flops | bytes accessed | tf_op | source)
XLA Modules:
  0.0 32.8 jit_solution(6425774715079038295)
XLA Ops:
  0.0 0.7 %convert_element_type.12 = f32[4,2]{0,1:T(2,128)S(1)} convert(s32[4,2]{0,1:T(2,128)} %param.5) | non-fusion elementwise | flops 8 | bytes 64 | tf_op jit(solution)/shard_map/convert_element_type | solution.py:90
  0.8 0.2 mul.22
  1.2 4.1 %collective-permute-start.4 = (bf16[512,256]{1,0:T(8,128)(2,1)S(1)}, bf16[512,256]{1,0:T(8,128)(2,1)S(1)}, u32[]{:S(2)}, u32[]{:S(2)}) collective-permute-start(bf16[512,256]{1,0:T(8,128)(2,1)S(1)} %fusion.refs_0_.refs_4_), channel_id=1, source_target_pairs={{0,2},{2,3},{3,1},{1,0},{4,6},{6,7},{7,5},{5,4},{8,10},{10,11},{11... | collective-permute-start | bytes 786440 | tf_op jit(solution)/shard_map/ppermute | solution.py:92
  5.3 1.5 %collective-permute-start.2 = (bf16[512,256]{1,0:T(8,128)(2,1)S(1)}, bf16[512,256]{1,0:T(8,128)(2,1)S(1)}, u32[]{:S(2)}, u32[]{:S(2)}) collective-permute-start(bf16[512,256]{1,0:T(8,128)(2,1)S(1)} %fusion.refs_0_.refs_4_), channel_id=1, source_target_pairs={{0,8},{1,9},{2,10},{3,11},{4,5},{5,7},{6,4},{7,6},{8,0},{9,1},{10,... | collective-permute-start | bytes 786440 | tf_op jit(solution)/shard_map/ppermute | solution.py:95
  6.7 1.5 %collective-permute-start.1 = (bf16[512,256]{1,0:T(8,128)(2,1)S(1)}, bf16[512,256]{1,0:T(8,128)(2,1)S(1)}, u32[]{:S(2)}, u32[]{:S(2)}) collective-permute-start(bf16[512,256]{1,0:T(8,128)(2,1)S(1)} %fusion.refs_0_.refs_4_), channel_id=1, source_target_pairs={{0,16},{8,24},{16,0},{24,8},{1,17},{9,25},{17,1},{25,9},{2,18},{10... | collective-permute-start | bytes 786440 | tf_op jit(solution)/shard_map/ppermute | solution.py:70
  8.3 0.5 %collective-permute-start = (bf16[512,256]{1,0:T(8,128)(2,1)S(1)}, bf16[512,256]{1,0:T(8,128)(2,1)S(1)}, u32[]{:S(2)}, u32[]{:S(2)}) collective-permute-start(bf16[512,256]{1,0:T(8,128)(2,1)S(1)} %fusion.refs_0_.refs_4_), channel_id=1, source_target_pairs={{0,24},{8,16},{16,8},{24,0},{1,25},{9,17},{17,9},{25,1},{2,26},{10... | collective-permute-start | bytes 786440 | tf_op jit(solution)/shard_map/ppermute | solution.py:70
  8.8 0.1 copy.6
  8.8 0.2 mul.25
  9.1 2.9 %collective-permute-done.4.refs_5_ = bf16[512,256]{1,0:T(8,128)(2,1)S(1)} collective-permute-done((bf16[512,256]{1,0:T(8,128)(2,1)S(1)}, bf16[512,256]{1,0:T(8,128)(2,1)S(1)}, u32[]{:S(2)}, u32[]{:S(2)}) %collective-permute-start.4) | collective-permute-done | bytes 262176 | tf_op jit(solution)/shard_map/ppermute | solution.py:92
  12.0 3.4 %collective-permute-start.5 = (bf16[512,256]{1,0:T(8,128)(2,1)S(1)}, bf16[512,256]{1,0:T(8,128)(2,1)S(1)}, u32[]{:S(2)}, u32[]{:S(2)}) collective-permute-start(bf16[512,256]{1,0:T(8,128)(2,1)S(1)} %collective-permute-done.4.refs_5_), channel_id=1, source_target_pairs={{0,2},{2,3},{3,1},{1,0},{4,6},{6,7},{7,5},{5,4},{8,10},{10,11},{11... | collective-permute-start | bytes 786440 | tf_op jit(solution)/shard_map/ppermute | solution.py:110
  15.4 4.0 %collective-permute-done.3 = bf16[512,256]{1,0:T(8,128)(2,1)S(1)} collective-permute-done((bf16[512,256]{1,0:T(8,128)(2,1)S(1)}, bf16[512,256]{1,0:T(8,128)(2,1)S(1)}, u32[]{:S(2)}, u32[]{:S(2)}) %collective-permute-start.3) | collective-permute-done | bytes 262176 | tf_op jit(solution)/shard_map/ppermute | solution.py:95
  19.4 0.4 %collective-permute-done.1.refs_2_ = bf16[512,256]{1,0:T(8,128)(2,1)S(1)} collective-permute-done((bf16[512,256]{1,0:T(8,128)(2,1)S(1)}, bf16[512,256]{1,0:T(8,128)(2,1)S(1)}, u32[]{:S(2)}, u32[]{:S(2)}) %collective-permute-start.1) | collective-permute-done | bytes 262176 | tf_op jit(solution)/shard_map/ppermute | solution.py:70
  20.0 0.5 %collective-permute-start.6 = (bf16[512,256]{1,0:T(8,128)(2,1)S(1)}, bf16[512,256]{1,0:T(8,128)(2,1)S(1)}, u32[]{:S(2)}, u32[]{:S(2)}) collective-permute-start(bf16[512,256]{1,0:T(8,128)(2,1)S(1)} %fusion.refs_0_.refs_4_), channel_id=1, source_target_pairs={{0,4},{4,0},{1,5},{5,1},{2,6},{6,2},{3,7},{7,3},{8,12},{12,8},{9,1... | collective-permute-start | bytes 786440 | tf_op jit(solution)/shard_map/ppermute | solution.py:70
  20.6 2.9 %collective-permute-done.5.refs_7_ = bf16[512,256]{1,0:T(8,128)(2,1)S(1)} collective-permute-done((bf16[512,256]{1,0:T(8,128)(2,1)S(1)}, bf16[512,256]{1,0:T(8,128)(2,1)S(1)}, u32[]{:S(2)}, u32[]{:S(2)}) %collective-permute-start.5) | collective-permute-done | bytes 262176 | tf_op jit(solution)/shard_map/ppermute | solution.py:110
  23.6 0.7 %shard_map.46 = (f32[512,256]{1,0:T(8,128)S(1)}, bf16[256,256]{1,0:T(8,128)(2,1)S(1)}) custom-call(bf16[512,256]{1,0:T(8,128)(2,1)S(1)} %fusion.refs_0_.refs_4_, bf16[512,256]{1,0:T(8,128)(2,1)S(1)} %get-tuple-element.40.refs_1_, bf16[512,256]{1,0:T(8,128)(2,1)S(1)} %collective-permute-done.1.refs_2_, bf16[512,256]{1,0:T(8,128)(2,1)S(1)} %collective-permute-done.refs_3_, ...), custom_call_target="tpu_custom_call" | custom-call | flops 402653184 | bytes 2621440 | tf_op jit(solution)/shard_map/pallas_call | solution.py:119
  24.3 0.8 %collective-permute-done.9.left_ref = bf16[512,256]{1,0:T(8,128)(2,1)S(1)} collective-permute-done((bf16[512,256]{1,0:T(8,128)(2,1)S(1)}, bf16[512,256]{1,0:T(8,128)(2,1)S(1)}, u32[]{:S(2)}, u32[]{:S(2)}) %collective-permute-start.9) | collective-permute-done | bytes 262176 | tf_op jit(solution)/shard_map/ppermute | solution.py:70
  25.1 0.3 shard_map.47
  25.4 2.5 %collective-permute-start.12 = (f32[1,256]{1,0:T(1,128)S(1)}, f32[1,256]{1,0:T(1,128)S(1)}, u32[]{:S(2)}, u32[]{:S(2)}) collective-permute-start(f32[1,256]{1,0:T(1,128)S(1)} %get-tuple-element.38.refs_0_), channel_id=1, source_target_pairs={{0,24},{8,16},{16,8},{24,0},{1,25},{9,17},{17,9},{25,1},{2,26},{10... | collective-permute-start | bytes 3080 | tf_op jit(solution)/shard_map/ppermute | solution.py:70
  27.9 0.5 %collective-permute-start.11 = (f32[1,256]{1,0:T(1,128)S(1)}, f32[1,256]{1,0:T(1,128)S(1)}, u32[]{:S(2)}, u32[]{:S(2)}) collective-permute-start(f32[1,256]{1,0:T(1,128)S(1)} %get-tuple-element.38.refs_0_), channel_id=1, source_target_pairs={{0,16},{8,24},{16,0},{24,8},{1,17},{9,25},{17,1},{25,9},{2,18},{10... | collective-permute-start | bytes 3080 | tf_op jit(solution)/shard_map/ppermute | solution.py:70
  28.4 0.5 %collective-permute-start.10 = (f32[1,256]{1,0:T(1,128)S(1)}, f32[1,256]{1,0:T(1,128)S(1)}, u32[]{:S(2)}, u32[]{:S(2)}) collective-permute-start(f32[1,256]{1,0:T(1,128)S(1)} %get-tuple-element.38.refs_0_), channel_id=1, source_target_pairs={{0,8},{8,0},{16,24},{24,16},{1,9},{9,1},{17,25},{25,17},{2,10},{10... | collective-permute-start | bytes 3080 | tf_op jit(solution)/shard_map/ppermute | solution.py:70
  28.9 1.0 %collective-permute-done.12.refs_3_ = f32[1,256]{1,0:T(1,128)S(1)} collective-permute-done((f32[1,256]{1,0:T(1,128)S(1)}, f32[1,256]{1,0:T(1,128)S(1)}, u32[]{:S(2)}, u32[]{:S(2)}) %collective-permute-start.12) | collective-permute-done | bytes 1056 | tf_op jit(solution)/shard_map/ppermute | solution.py:70
  29.9 1.6 %collective-permute-done.11.refs_2_ = f32[1,256]{1,0:T(1,128)S(1)} collective-permute-done((f32[1,256]{1,0:T(1,128)S(1)}, f32[1,256]{1,0:T(1,128)S(1)}, u32[]{:S(2)}, u32[]{:S(2)}) %collective-permute-start.11) | collective-permute-done | bytes 1056 | tf_op jit(solution)/shard_map/ppermute | solution.py:70
  31.4 0.5 %collective-permute-done.10.refs_1_ = f32[1,256]{1,0:T(1,128)S(1)} collective-permute-done((f32[1,256]{1,0:T(1,128)S(1)}, f32[1,256]{1,0:T(1,128)S(1)}, u32[]{:S(2)}, u32[]{:S(2)}) %collective-permute-start.10) | collective-permute-done | bytes 1056 | tf_op jit(solution)/shard_map/ppermute | solution.py:70
  31.9 0.8 %shard_map.48 = f32[512,256]{1,0:T(8,128)} custom-call(f32[512,256]{1,0:T(8,128)S(1)} %get-tuple-element.37.squares_ref, f32[1,256]{1,0:T(1,128)S(1)} %get-tuple-element.38.refs_0_, f32[1,256]{1,0:T(1,128)S(1)} %collective-permute-done.10.refs_1_, f32[1,256]{1,0:T(1,128)S(1)} %collective-permute-done.11.refs_2_, f32[1,256]{1,0:T(1,128)S(1)} %collective-permute-done.12.refs_3_), custom_call_target="tpu_custom_call" | custom-call | flops 524288 | bytes 1048576 | tf_op jit(solution)/shard_map/pallas_call | solution.py:135
  (20 shorter events, 0.5 us)
Async XLA Ops:
  0.0 1.1 %copy-start.1 = (f32[512,256]{1,0:T(8,128)S(1)}, f32[512,256]{1,0:T(8,128)}, u32[]{:S(2)}) copy-start(f32[512,256]{1,0:T(8,128)} %param.4) | copy-start | bytes 1572868
  1.1 7.7 %copy-start.2 = (s32[4,2]{0,1:T(2,128)S(1)}, s32[4,2]{0,1:T(2,128)}, u32[]{:S(2)}) copy-start(s32[4,2]{0,1:T(2,128)} %param.6) | copy-start | bytes 100
  1.2 7.9 %copy-start = (s32[512,256]{1,0:T(8,128)S(1)}, s32[512,256]{1,0:T(8,128)}, u32[]{:S(2)}) copy-start(s32[512,256]{1,0:T(8,128)} %param.7) | copy-start | bytes 1572868
  1.2 10.8 %collective-permute-start.4 = (bf16[512,256]{1,0:T(8,128)(2,1)S(1)}, bf16[512,256]{1,0:T(8,128)(2,1)S(1)}, u32[]{:S(2)}, u32[]{:S(2)}) collective-permute-start(bf16[512,256]{1,0:T(8,128)(2,1)S(1)} %fusion.refs_0_.refs_4_), channel_id=1, source_target_pairs={{0,2},{2,3},{3,1},{1,0},{4,6},{6,7},{7,5},{5,4},{8,10},{10,11},{11... | collective-permute-start | bytes 786440 | tf_op jit(solution)/shard_map/ppermute | solution.py:92
  5.3 14.2 %collective-permute-start.3 = (bf16[512,256]{1,0:T(8,128)(2,1)S(1)}, bf16[512,256]{1,0:T(8,128)(2,1)S(1)}, u32[]{:S(2)}, u32[]{:S(2)}) collective-permute-start(bf16[512,256]{1,0:T(8,128)(2,1)S(1)} %fusion.refs_0_.refs_4_), channel_id=1, source_target_pairs={{0,1},{1,3},{2,0},{3,2},{4,12},{5,13},{6,14},{7,15},{8,9},{9,11},{... | collective-permute-start | bytes 786440 | tf_op jit(solution)/shard_map/ppermute | solution.py:95
  5.3 14.2 %collective-permute-start.2 = (bf16[512,256]{1,0:T(8,128)(2,1)S(1)}, bf16[512,256]{1,0:T(8,128)(2,1)S(1)}, u32[]{:S(2)}, u32[]{:S(2)}) collective-permute-start(bf16[512,256]{1,0:T(8,128)(2,1)S(1)} %fusion.refs_0_.refs_4_), channel_id=1, source_target_pairs={{0,8},{1,9},{2,10},{3,11},{4,5},{5,7},{6,4},{7,6},{8,0},{9,1},{10,... | collective-permute-start | bytes 786440 | tf_op jit(solution)/shard_map/ppermute | solution.py:95
  6.7 13.1 %collective-permute-start.1 = (bf16[512,256]{1,0:T(8,128)(2,1)S(1)}, bf16[512,256]{1,0:T(8,128)(2,1)S(1)}, u32[]{:S(2)}, u32[]{:S(2)}) collective-permute-start(bf16[512,256]{1,0:T(8,128)(2,1)S(1)} %fusion.refs_0_.refs_4_), channel_id=1, source_target_pairs={{0,16},{8,24},{16,0},{24,8},{1,17},{9,25},{17,1},{25,9},{2,18},{10... | collective-permute-start | bytes 786440 | tf_op jit(solution)/shard_map/ppermute | solution.py:70
  8.3 11.6 %collective-permute-start = (bf16[512,256]{1,0:T(8,128)(2,1)S(1)}, bf16[512,256]{1,0:T(8,128)(2,1)S(1)}, u32[]{:S(2)}, u32[]{:S(2)}) collective-permute-start(bf16[512,256]{1,0:T(8,128)(2,1)S(1)} %fusion.refs_0_.refs_4_), channel_id=1, source_target_pairs={{0,24},{8,16},{16,8},{24,0},{1,25},{9,17},{17,9},{25,1},{2,26},{10... | collective-permute-start | bytes 786440 | tf_op jit(solution)/shard_map/ppermute | solution.py:70
  12.0 11.5 %collective-permute-start.5 = (bf16[512,256]{1,0:T(8,128)(2,1)S(1)}, bf16[512,256]{1,0:T(8,128)(2,1)S(1)}, u32[]{:S(2)}, u32[]{:S(2)}) collective-permute-start(bf16[512,256]{1,0:T(8,128)(2,1)S(1)} %collective-permute-done.4.refs_5_), channel_id=1, source_target_pairs={{0,2},{2,3},{3,1},{1,0},{4,6},{6,7},{7,5},{5,4},{8,10},{10,11},{11... | collective-permute-start | bytes 786440 | tf_op jit(solution)/shard_map/ppermute | solution.py:110
  19.9 3.6 %collective-permute-start.8 = (bf16[512,256]{1,0:T(8,128)(2,1)S(1)}, bf16[512,256]{1,0:T(8,128)(2,1)S(1)}, u32[]{:S(2)}, u32[]{:S(2)}) collective-permute-start(bf16[512,256]{1,0:T(8,128)(2,1)S(1)} %get-tuple-element.39.refs_6_), channel_id=1, source_target_pairs={{0,4},{4,0},{1,5},{5,1},{2,6},{6,2},{3,7},{7,3},{8,12},{12,8},{9,1... | collective-permute-start | bytes 786440 | tf_op jit(solution)/shard_map/ppermute | solution.py:70
  20.0 3.5 %collective-permute-start.6 = (bf16[512,256]{1,0:T(8,128)(2,1)S(1)}, bf16[512,256]{1,0:T(8,128)(2,1)S(1)}, u32[]{:S(2)}, u32[]{:S(2)}) collective-permute-start(bf16[512,256]{1,0:T(8,128)(2,1)S(1)} %fusion.refs_0_.refs_4_), channel_id=1, source_target_pairs={{0,4},{4,0},{1,5},{5,1},{2,6},{6,2},{3,7},{7,3},{8,12},{12,8},{9,1... | collective-permute-start | bytes 786440 | tf_op jit(solution)/shard_map/ppermute | solution.py:70
  20.5 3.0 %collective-permute-start.7 = (bf16[512,256]{1,0:T(8,128)(2,1)S(1)}, bf16[512,256]{1,0:T(8,128)(2,1)S(1)}, u32[]{:S(2)}, u32[]{:S(2)}) collective-permute-start(bf16[512,256]{1,0:T(8,128)(2,1)S(1)} %collective-permute-done.4.refs_5_), channel_id=1, source_target_pairs={{0,4},{4,0},{1,5},{5,1},{2,6},{6,2},{3,7},{7,3},{8,12},{12,8},{9,1... | collective-permute-start | bytes 786440 | tf_op jit(solution)/shard_map/ppermute | solution.py:70
  23.5 1.6 %collective-permute-start.9 = (bf16[512,256]{1,0:T(8,128)(2,1)S(1)}, bf16[512,256]{1,0:T(8,128)(2,1)S(1)}, u32[]{:S(2)}, u32[]{:S(2)}) collective-permute-start(bf16[512,256]{1,0:T(8,128)(2,1)S(1)} %collective-permute-done.5.refs_7_), channel_id=1, source_target_pairs={{0,4},{4,0},{1,5},{5,1},{2,6},{6,2},{3,7},{7,3},{8,12},{12,8},{9,1... | collective-permute-start | bytes 786440 | tf_op jit(solution)/shard_map/ppermute | solution.py:70
  25.4 4.5 %collective-permute-start.12 = (f32[1,256]{1,0:T(1,128)S(1)}, f32[1,256]{1,0:T(1,128)S(1)}, u32[]{:S(2)}, u32[]{:S(2)}) collective-permute-start(f32[1,256]{1,0:T(1,128)S(1)} %get-tuple-element.38.refs_0_), channel_id=1, source_target_pairs={{0,24},{8,16},{16,8},{24,0},{1,25},{9,17},{17,9},{25,1},{2,26},{10... | collective-permute-start | bytes 3080 | tf_op jit(solution)/shard_map/ppermute | solution.py:70
  27.9 3.6 %collective-permute-start.11 = (f32[1,256]{1,0:T(1,128)S(1)}, f32[1,256]{1,0:T(1,128)S(1)}, u32[]{:S(2)}, u32[]{:S(2)}) collective-permute-start(f32[1,256]{1,0:T(1,128)S(1)} %get-tuple-element.38.refs_0_), channel_id=1, source_target_pairs={{0,16},{8,24},{16,0},{24,8},{1,17},{9,25},{17,1},{25,9},{2,18},{10... | collective-permute-start | bytes 3080 | tf_op jit(solution)/shard_map/ppermute | solution.py:70
  28.4 3.6 %collective-permute-start.10 = (f32[1,256]{1,0:T(1,128)S(1)}, f32[1,256]{1,0:T(1,128)S(1)}, u32[]{:S(2)}, u32[]{:S(2)}) collective-permute-start(f32[1,256]{1,0:T(1,128)S(1)} %get-tuple-element.38.refs_0_), channel_id=1, source_target_pairs={{0,8},{8,0},{16,24},{24,16},{1,9},{9,1},{17,25},{25,17},{2,10},{10... | collective-permute-start | bytes 3080 | tf_op jit(solution)/shard_map/ppermute | solution.py:70

commit v8 on v7

--- a/solution.py
+++ b/solution.py
@@ -131,7 +131,10 @@
         flops=2 * rows * cols * rows,
         size=16 * rows * cols,
     )(total, far_other, last, weight)
-    others = [swap(sums, "row", 4, s) for s in (1, 2, 3)]
+    others = [
+        lax.ppermute(sums, ("row", "col"), [(2 * r + c, 2 * (r ^ steps[c]) + c) for r in range(4) for c in range(2)])
+        for steps in ((1, 3), (2, 1), (3, 2))
+    ]
     return call(
         functools.partial(scale_kernel, total_rows), full, [VMEM] * 5, flops=4 * rows * cols, size=8 * rows * cols
     )(squares, sums, *others)

time: 32.9 us -> 32.9 us (level)
    ppermute x9 -> x6, starting transfers between devices: 6.27 us -> 2.71 us  [swap(): return lax.ppermute(x, axis, [(i, i ^ s) for i in range(size)])]
    ppermute x0 -> x3, starting transfers between devices: none -> 3.55 us  [on_small_mesh(): lax.ppermute(sums, ('row', 'col'), [(2 * r + c, 2 * (r ^ steps[c]) + c) f...]
    ppermute x0 -> x3, waiting for transfers between devices: none -> 3.04 us  [on_small_mesh(): lax.ppermute(sums, ('row', 'col'), [(2 * r + c, 2 * (r ^ steps[c]) + c) f...]
    ppermute x9 -> x6, waiting for transfers between devices: 4.24 us -> 1.2 us  [swap(): return lax.ppermute(x, axis, [(i, i ^ s) for i in range(size)])]
where the time goes in v8:
time: 32.9 us; the launch traced here: 32.8 us
  starting transfers between devices  15.2 us (46%)
  waiting for transfers between devices  14.1 us (43%)
  Pallas kernels  1.84 us (6%)
  other arithmetic  0.93 us (3%)
  local copies, waits for them, and re-layouts  0.63 us (2%)
    ppermute x1, starting transfers between devices, on_small_mesh(): first = lax.ppermute(own, 'layer', ring)  4.09 us
    ppermute x2, waiting for transfers between devices, on_small_mesh(): lax.ppermute(own, ('row', 'col', 'layer'), [(8 * r + 4 * c + z, 8 * r + 4...  4.05 us
    ppermute x3, starting transfers between devices, on_small_mesh(): lax.ppermute(sums, ('row', 'col'), [(2 * r + c, 2 * (r ^ steps[c]) + c) f...  3.55 us
    ppermute x1, starting transfers between devices, on_small_mesh(): far = lax.ppermute(first, 'layer', ring)  3.38 us
    ppermute x3, waiting for transfers between devices, on_small_mesh(): lax.ppermute(sums, ('row', 'col'), [(2 * r + c, 2 * (r ^ steps[c]) + c) f...  3.04 us
    ppermute x1, waiting for transfers between devices, on_small_mesh(): far = lax.ppermute(first, 'layer', ring)  2.92 us
    ppermute x1, waiting for transfers between devices, on_small_mesh(): first = lax.ppermute(own, 'layer', ring)  2.86 us
    ppermute x6, starting transfers between devices, swap(): return lax.ppermute(x, axis, [(i, i ^ s) for i in range(size)])  2.71 us
  transfers between devices with their start and end apart: 13, of which 8 were waited for; matrix products, arithmetic and copies ran while one was open for 1% of the time, Pallas kernels for 2%

profile of v8, /device:TPU:0, one launch (start us, length us, event | category | flops | bytes accessed | tf_op | source)
XLA Modules:
  0.0 32.8 jit_solution(12788258934580250549)
XLA Ops:
  0.0 0.7 %convert_element_type.12 = f32[4,2]{0,1:T(2,128)S(1)} convert(s32[4,2]{0,1:T(2,128)} %param.5) | non-fusion elementwise | flops 8 | bytes 64 | tf_op jit(solution)/shard_map/convert_element_type | solution.py:90
  0.8 0.2 mul.22
  1.2 4.1 %collective-permute-start.4 = (bf16[512,256]{1,0:T(8,128)(2,1)S(1)}, bf16[512,256]{1,0:T(8,128)(2,1)S(1)}, u32[]{:S(2)}, u32[]{:S(2)}) collective-permute-start(bf16[512,256]{1,0:T(8,128)(2,1)S(1)} %fusion.refs_0_.refs_4_), channel_id=1, source_target_pairs={{0,2},{2,3},{3,1},{1,0},{4,6},{6,7},{7,5},{5,4},{8,10},{10,11},{11... | collective-permute-start | bytes 786440 | tf_op jit(solution)/shard_map/ppermute | solution.py:92
  5.3 1.5 %collective-permute-start.2 = (bf16[512,256]{1,0:T(8,128)(2,1)S(1)}, bf16[512,256]{1,0:T(8,128)(2,1)S(1)}, u32[]{:S(2)}, u32[]{:S(2)}) collective-permute-start(bf16[512,256]{1,0:T(8,128)(2,1)S(1)} %fusion.refs_0_.refs_4_), channel_id=1, source_target_pairs={{0,8},{1,9},{2,10},{3,11},{4,5},{5,7},{6,4},{7,6},{8,0},{9,1},{10,... | collective-permute-start | bytes 786440 | tf_op jit(solution)/shard_map/ppermute | solution.py:95
  6.7 1.5 %collective-permute-start.1 = (bf16[512,256]{1,0:T(8,128)(2,1)S(1)}, bf16[512,256]{1,0:T(8,128)(2,1)S(1)}, u32[]{:S(2)}, u32[]{:S(2)}) collective-permute-start(bf16[512,256]{1,0:T(8,128)(2,1)S(1)} %fusion.refs_0_.refs_4_), channel_id=1, source_target_pairs={{0,16},{8,24},{16,0},{24,8},{1,17},{9,25},{17,1},{25,9},{2,18},{10... | collective-permute-start | bytes 786440 | tf_op jit(solution)/shard_map/ppermute | solution.py:70
  8.3 0.5 %collective-permute-start = (bf16[512,256]{1,0:T(8,128)(2,1)S(1)}, bf16[512,256]{1,0:T(8,128)(2,1)S(1)}, u32[]{:S(2)}, u32[]{:S(2)}) collective-permute-start(bf16[512,256]{1,0:T(8,128)(2,1)S(1)} %fusion.refs_0_.refs_4_), channel_id=1, source_target_pairs={{0,24},{8,16},{16,8},{24,0},{1,25},{9,17},{17,9},{25,1},{2,26},{10... | collective-permute-start | bytes 786440 | tf_op jit(solution)/shard_map/ppermute | solution.py:70
  8.8 0.1 copy.6
  8.8 0.2 mul.25
  9.1 2.9 %collective-permute-done.4.refs_5_ = bf16[512,256]{1,0:T(8,128)(2,1)S(1)} collective-permute-done((bf16[512,256]{1,0:T(8,128)(2,1)S(1)}, bf16[512,256]{1,0:T(8,128)(2,1)S(1)}, u32[]{:S(2)}, u32[]{:S(2)}) %collective-permute-start.4) | collective-permute-done | bytes 262176 | tf_op jit(solution)/shard_map/ppermute | solution.py:92
  12.0 3.4 %collective-permute-start.5 = (bf16[512,256]{1,0:T(8,128)(2,1)S(1)}, bf16[512,256]{1,0:T(8,128)(2,1)S(1)}, u32[]{:S(2)}, u32[]{:S(2)}) collective-permute-start(bf16[512,256]{1,0:T(8,128)(2,1)S(1)} %collective-permute-done.4.refs_5_), channel_id=1, source_target_pairs={{0,2},{2,3},{3,1},{1,0},{4,6},{6,7},{7,5},{5,4},{8,10},{10,11},{11... | collective-permute-start | bytes 786440 | tf_op jit(solution)/shard_map/ppermute | solution.py:110
  15.4 4.0 %collective-permute-done.3 = bf16[512,256]{1,0:T(8,128)(2,1)S(1)} collective-permute-done((bf16[512,256]{1,0:T(8,128)(2,1)S(1)}, bf16[512,256]{1,0:T(8,128)(2,1)S(1)}, u32[]{:S(2)}, u32[]{:S(2)}) %collective-permute-start.3) | collective-permute-done | bytes 262176 | tf_op jit(solution)/shard_map/ppermute | solution.py:95
  19.4 0.4 %collective-permute-done.1.refs_2_ = bf16[512,256]{1,0:T(8,128)(2,1)S(1)} collective-permute-done((bf16[512,256]{1,0:T(8,128)(2,1)S(1)}, bf16[512,256]{1,0:T(8,128)(2,1)S(1)}, u32[]{:S(2)}, u32[]{:S(2)}) %collective-permute-start.1) | collective-permute-done | bytes 262176 | tf_op jit(solution)/shard_map/ppermute | solution.py:70
  20.0 0.5 %collective-permute-start.6 = (bf16[512,256]{1,0:T(8,128)(2,1)S(1)}, bf16[512,256]{1,0:T(8,128)(2,1)S(1)}, u32[]{:S(2)}, u32[]{:S(2)}) collective-permute-start(bf16[512,256]{1,0:T(8,128)(2,1)S(1)} %fusion.refs_0_.refs_4_), channel_id=1, source_target_pairs={{0,4},{4,0},{1,5},{5,1},{2,6},{6,2},{3,7},{7,3},{8,12},{12,8},{9,1... | collective-permute-start | bytes 786440 | tf_op jit(solution)/shard_map/ppermute | solution.py:70
  20.6 2.9 %collective-permute-done.5.refs_7_ = bf16[512,256]{1,0:T(8,128)(2,1)S(1)} collective-permute-done((bf16[512,256]{1,0:T(8,128)(2,1)S(1)}, bf16[512,256]{1,0:T(8,128)(2,1)S(1)}, u32[]{:S(2)}, u32[]{:S(2)}) %collective-permute-start.5) | collective-permute-done | bytes 262176 | tf_op jit(solution)/shard_map/ppermute | solution.py:110
  23.6 0.7 %shard_map.46 = (f32[512,256]{1,0:T(8,128)S(1)}, bf16[256,256]{1,0:T(8,128)(2,1)S(1)}) custom-call(bf16[512,256]{1,0:T(8,128)(2,1)S(1)} %fusion.refs_0_.refs_4_, bf16[512,256]{1,0:T(8,128)(2,1)S(1)} %get-tuple-element.40.refs_1_, bf16[512,256]{1,0:T(8,128)(2,1)S(1)} %collective-permute-done.1.refs_2_, bf16[512,256]{1,0:T(8,128)(2,1)S(1)} %collective-permute-done.refs_3_, ...), custom_call_target="tpu_custom_call" | custom-call | flops 402653184 | bytes 2621440 | tf_op jit(solution)/shard_map/pallas_call | solution.py:119
  24.3 0.8 %collective-permute-done.9.left_ref = bf16[512,256]{1,0:T(8,128)(2,1)S(1)} collective-permute-done((bf16[512,256]{1,0:T(8,128)(2,1)S(1)}, bf16[512,256]{1,0:T(8,128)(2,1)S(1)}, u32[]{:S(2)}, u32[]{:S(2)}) %collective-permute-start.9) | collective-permute-done | bytes 262176 | tf_op jit(solution)/shard_map/ppermute | solution.py:70
  25.1 0.3 shard_map.47
  25.4 2.5 %collective-permute-start.12 = (f32[1,256]{1,0:T(1,128)S(1)}, f32[1,256]{1,0:T(1,128)S(1)}, u32[]{:S(2)}, u32[]{:S(2)}) collective-permute-start(f32[1,256]{1,0:T(1,128)S(1)} %get-tuple-element.38.refs_0_), channel_id=1, source_target_pairs={{0,24},{4,20},{8,16},{12,28},{16,8},{20,4},{24,0},{28,12},{1,25},{... | collective-permute-start | bytes 3080 | tf_op jit(solution)/shard_map/ppermute | solution.py:135
  27.9 0.5 %collective-permute-start.11 = (f32[1,256]{1,0:T(1,128)S(1)}, f32[1,256]{1,0:T(1,128)S(1)}, u32[]{:S(2)}, u32[]{:S(2)}) collective-permute-start(f32[1,256]{1,0:T(1,128)S(1)} %get-tuple-element.38.refs_0_), channel_id=1, source_target_pairs={{0,16},{4,12},{8,24},{12,4},{16,0},{20,28},{24,8},{28,20},{1,17},{... | collective-permute-start | bytes 3080 | tf_op jit(solution)/shard_map/ppermute | solution.py:135
  28.4 0.5 %collective-permute-start.10 = (f32[1,256]{1,0:T(1,128)S(1)}, f32[1,256]{1,0:T(1,128)S(1)}, u32[]{:S(2)}, u32[]{:S(2)}) collective-permute-start(f32[1,256]{1,0:T(1,128)S(1)} %get-tuple-element.38.refs_0_), channel_id=1, source_target_pairs={{0,8},{4,28},{8,0},{12,20},{16,24},{20,12},{24,16},{28,4},{1,9},{5... | collective-permute-start | bytes 3080 | tf_op jit(solution)/shard_map/ppermute | solution.py:135
  28.9 1.0 %collective-permute-done.12.refs_3_ = f32[1,256]{1,0:T(1,128)S(1)} collective-permute-done((f32[1,256]{1,0:T(1,128)S(1)}, f32[1,256]{1,0:T(1,128)S(1)}, u32[]{:S(2)}, u32[]{:S(2)}) %collective-permute-start.12) | collective-permute-done | bytes 1056 | tf_op jit(solution)/shard_map/ppermute | solution.py:135
  29.9 1.6 %collective-permute-done.11.refs_2_ = f32[1,256]{1,0:T(1,128)S(1)} collective-permute-done((f32[1,256]{1,0:T(1,128)S(1)}, f32[1,256]{1,0:T(1,128)S(1)}, u32[]{:S(2)}, u32[]{:S(2)}) %collective-permute-start.11) | collective-permute-done | bytes 1056 | tf_op jit(solution)/shard_map/ppermute | solution.py:135
  31.4 0.5 %collective-permute-done.10.refs_1_ = f32[1,256]{1,0:T(1,128)S(1)} collective-permute-done((f32[1,256]{1,0:T(1,128)S(1)}, f32[1,256]{1,0:T(1,128)S(1)}, u32[]{:S(2)}, u32[]{:S(2)}) %collective-permute-start.10) | collective-permute-done | bytes 1056 | tf_op jit(solution)/shard_map/ppermute | solution.py:135
  31.9 0.8 %shard_map.48 = f32[512,256]{1,0:T(8,128)} custom-call(f32[512,256]{1,0:T(8,128)S(1)} %get-tuple-element.37.squares_ref, f32[1,256]{1,0:T(1,128)S(1)} %get-tuple-element.38.refs_0_, f32[1,256]{1,0:T(1,128)S(1)} %collective-permute-done.10.refs_1_, f32[1,256]{1,0:T(1,128)S(1)} %collective-permute-done.11.refs_2_, f32[1,256]{1,0:T(1,128)S(1)} %collective-permute-done.12.refs_3_), custom_call_target="tpu_custom_call" | custom-call | flops 524288 | bytes 1048576 | tf_op jit(solution)/shard_map/pallas_call | solution.py:138
  (20 shorter events, 0.5 us)
Async XLA Ops:
  0.0 1.1 %copy-start.1 = (f32[512,256]{1,0:T(8,128)S(1)}, f32[512,256]{1,0:T(8,128)}, u32[]{:S(2)}) copy-start(f32[512,256]{1,0:T(8,128)} %param.4) | copy-start | bytes 1572868
  1.1 7.7 %copy-start.2 = (s32[4,2]{0,1:T(2,128)S(1)}, s32[4,2]{0,1:T(2,128)}, u32[]{:S(2)}) copy-start(s32[4,2]{0,1:T(2,128)} %param.6) | copy-start | bytes 100
  1.2 7.9 %copy-start = (s32[512,256]{1,0:T(8,128)S(1)}, s32[512,256]{1,0:T(8,128)}, u32[]{:S(2)}) copy-start(s32[512,256]{1,0:T(8,128)} %param.7) | copy-start | bytes 1572868
  1.2 10.8 %collective-permute-start.4 = (bf16[512,256]{1,0:T(8,128)(2,1)S(1)}, bf16[512,256]{1,0:T(8,128)(2,1)S(1)}, u32[]{:S(2)}, u32[]{:S(2)}) collective-permute-start(bf16[512,256]{1,0:T(8,128)(2,1)S(1)} %fusion.refs_0_.refs_4_), channel_id=1, source_target_pairs={{0,2},{2,3},{3,1},{1,0},{4,6},{6,7},{7,5},{5,4},{8,10},{10,11},{11... | collective-permute-start | bytes 786440 | tf_op jit(solution)/shard_map/ppermute | solution.py:92
  5.3 14.2 %collective-permute-start.3 = (bf16[512,256]{1,0:T(8,128)(2,1)S(1)}, bf16[512,256]{1,0:T(8,128)(2,1)S(1)}, u32[]{:S(2)}, u32[]{:S(2)}) collective-permute-start(bf16[512,256]{1,0:T(8,128)(2,1)S(1)} %fusion.refs_0_.refs_4_), channel_id=1, source_target_pairs={{0,1},{1,3},{2,0},{3,2},{4,12},{5,13},{6,14},{7,15},{8,9},{9,11},{... | collective-permute-start | bytes 786440 | tf_op jit(solution)/shard_map/ppermute | solution.py:95
  5.3 14.2 %collective-permute-start.2 = (bf16[512,256]{1,0:T(8,128)(2,1)S(1)}, bf16[512,256]{1,0:T(8,128)(2,1)S(1)}, u32[]{:S(2)}, u32[]{:S(2)}) collective-permute-start(bf16[512,256]{1,0:T(8,128)(2,1)S(1)} %fusion.refs_0_.refs_4_), channel_id=1, source_target_pairs={{0,8},{1,9},{2,10},{3,11},{4,5},{5,7},{6,4},{7,6},{8,0},{9,1},{10,... | collective-permute-start | bytes 786440 | tf_op jit(solution)/shard_map/ppermute | solution.py:95
  6.7 13.1 %collective-permute-start.1 = (bf16[512,256]{1,0:T(8,128)(2,1)S(1)}, bf16[512,256]{1,0:T(8,128)(2,1)S(1)}, u32[]{:S(2)}, u32[]{:S(2)}) collective-permute-start(bf16[512,256]{1,0:T(8,128)(2,1)S(1)} %fusion.refs_0_.refs_4_), channel_id=1, source_target_pairs={{0,16},{8,24},{16,0},{24,8},{1,17},{9,25},{17,1},{25,9},{2,18},{10... | collective-permute-start | bytes 786440 | tf_op jit(solution)/shard_map/ppermute | solution.py:70
  8.3 11.6 %collective-permute-start = (bf16[512,256]{1,0:T(8,128)(2,1)S(1)}, bf16[512,256]{1,0:T(8,128)(2,1)S(1)}, u32[]{:S(2)}, u32[]{:S(2)}) collective-permute-start(bf16[512,256]{1,0:T(8,128)(2,1)S(1)} %fusion.refs_0_.refs_4_), channel_id=1, source_target_pairs={{0,24},{8,16},{16,8},{24,0},{1,25},{9,17},{17,9},{25,1},{2,26},{10... | collective-permute-start | bytes 786440 | tf_op jit(solution)/shard_map/ppermute | solution.py:70
  12.0 11.5 %collective-permute-start.5 = (bf16[512,256]{1,0:T(8,128)(2,1)S(1)}, bf16[512,256]{1,0:T(8,128)(2,1)S(1)}, u32[]{:S(2)}, u32[]{:S(2)}) collective-permute-start(bf16[512,256]{1,0:T(8,128)(2,1)S(1)} %collective-permute-done.4.refs_5_), channel_id=1, source_target_pairs={{0,2},{2,3},{3,1},{1,0},{4,6},{6,7},{7,5},{5,4},{8,10},{10,11},{11... | collective-permute-start | bytes 786440 | tf_op jit(solution)/shard_map/ppermute | solution.py:110
  19.9 3.6 %collective-permute-start.8 = (bf16[512,256]{1,0:T(8,128)(2,1)S(1)}, bf16[512,256]{1,0:T(8,128)(2,1)S(1)}, u32[]{:S(2)}, u32[]{:S(2)}) collective-permute-start(bf16[512,256]{1,0:T(8,128)(2,1)S(1)} %get-tuple-element.39.refs_6_), channel_id=1, source_target_pairs={{0,4},{4,0},{1,5},{5,1},{2,6},{6,2},{3,7},{7,3},{8,12},{12,8},{9,1... | collective-permute-start | bytes 786440 | tf_op jit(solution)/shard_map/ppermute | solution.py:70
  20.0 3.5 %collective-permute-start.6 = (bf16[512,256]{1,0:T(8,128)(2,1)S(1)}, bf16[512,256]{1,0:T(8,128)(2,1)S(1)}, u32[]{:S(2)}, u32[]{:S(2)}) collective-permute-start(bf16[512,256]{1,0:T(8,128)(2,1)S(1)} %fusion.refs_0_.refs_4_), channel_id=1, source_target_pairs={{0,4},{4,0},{1,5},{5,1},{2,6},{6,2},{3,7},{7,3},{8,12},{12,8},{9,1... | collective-permute-start | bytes 786440 | tf_op jit(solution)/shard_map/ppermute | solution.py:70
  20.5 3.0 %collective-permute-start.7 = (bf16[512,256]{1,0:T(8,128)(2,1)S(1)}, bf16[512,256]{1,0:T(8,128)(2,1)S(1)}, u32[]{:S(2)}, u32[]{:S(2)}) collective-permute-start(bf16[512,256]{1,0:T(8,128)(2,1)S(1)} %collective-permute-done.4.refs_5_), channel_id=1, source_target_pairs={{0,4},{4,0},{1,5},{5,1},{2,6},{6,2},{3,7},{7,3},{8,12},{12,8},{9,1... | collective-permute-start | bytes 786440 | tf_op jit(solution)/shard_map/ppermute | solution.py:70
  23.5 1.6 %collective-permute-start.9 = (bf16[512,256]{1,0:T(8,128)(2,1)S(1)}, bf16[512,256]{1,0:T(8,128)(2,1)S(1)}, u32[]{:S(2)}, u32[]{:S(2)}) collective-permute-start(bf16[512,256]{1,0:T(8,128)(2,1)S(1)} %collective-permute-done.5.refs_7_), channel_id=1, source_target_pairs={{0,4},{4,0},{1,5},{5,1},{2,6},{6,2},{3,7},{7,3},{8,12},{12,8},{9,1... | collective-permute-start | bytes 786440 | tf_op jit(solution)/shard_map/ppermute | solution.py:70
  25.4 4.5 %collective-permute-start.12 = (f32[1,256]{1,0:T(1,128)S(1)}, f32[1,256]{1,0:T(1,128)S(1)}, u32[]{:S(2)}, u32[]{:S(2)}) collective-permute-start(f32[1,256]{1,0:T(1,128)S(1)} %get-tuple-element.38.refs_0_), channel_id=1, source_target_pairs={{0,24},{4,20},{8,16},{12,28},{16,8},{20,4},{24,0},{28,12},{1,25},{... | collective-permute-start | bytes 3080 | tf_op jit(solution)/shard_map/ppermute | solution.py:135
  27.9 3.6 %collective-permute-start.11 = (f32[1,256]{1,0:T(1,128)S(1)}, f32[1,256]{1,0:T(1,128)S(1)}, u32[]{:S(2)}, u32[]{:S(2)}) collective-permute-start(f32[1,256]{1,0:T(1,128)S(1)} %get-tuple-element.38.refs_0_), channel_id=1, source_target_pairs={{0,16},{4,12},{8,24},{12,4},{16,0},{20,28},{24,8},{28,20},{1,17},{... | collective-permute-start | bytes 3080 | tf_op jit(solution)/shard_map/ppermute | solution.py:135
  28.4 3.6 %collective-permute-start.10 = (f32[1,256]{1,0:T(1,128)S(1)}, f32[1,256]{1,0:T(1,128)S(1)}, u32[]{:S(2)}, u32[]{:S(2)}) collective-permute-start(f32[1,256]{1,0:T(1,128)S(1)} %get-tuple-element.38.refs_0_), channel_id=1, source_target_pairs={{0,8},{4,28},{8,0},{12,20},{16,24},{20,12},{24,16},{28,4},{1,9},{5... | collective-permute-start | bytes 3080 | tf_op jit(solution)/shard_map/ppermute | solution.py:135

commit v9 on v7

--- a/solution.py
+++ b/solution.py
@@ -50,11 +50,15 @@
 
 
 def squares_kernel(total_ref, left_ref, right_ref, weight_ref, squares_ref, sums_ref):
-    product = total_ref[...] + jnp.dot(left_ref[...], right_ref[...], preferred_element_type=jnp.float32)
-    squares = product * product * weight_ref[...]
-    squares_ref[...] = squares
-    rows, cols = squares.shape
-    sums_ref[...] = jnp.sum(squares, axis=0, keepdims=True)
+    sums = None
+    for i in range(total_ref.shape[0] // TILE):
+        at = slice(i * TILE, (i + 1) * TILE)
+        product = total_ref[at] + jnp.dot(left_ref[at], right_ref[...], preferred_element_type=jnp.float32)
+        squares = product * product * weight_ref[at]
+        squares_ref[at] = squares
+        part = jnp.sum(squares.reshape(TILE // 8, 8, squares.shape[1]), axis=0)
+        sums = part if sums is None else sums + part
+    sums_ref[...] = jnp.sum(sums, axis=0, keepdims=True)
 
 
 def scale_kernel(total_rows, squares_ref, *refs):

time: 32.9 us -> 32.9 us (level)
  no operation moved by 1% of the time
where the time goes in v9:
time: 32.9 us; the launch traced here: 32.8 us
  starting transfers between devices  15.2 us (46%)
  waiting for transfers between devices  14.1 us (43%)
  Pallas kernels  1.83 us (6%)
  other arithmetic  0.93 us (3%)
  local copies, waits for them, and re-layouts  0.63 us (2%)
    ppermute x9, starting transfers between devices, swap(): return lax.ppermute(x, axis, [(i, i ^ s) for i in range(size)])  6.27 us
    ppermute x9, waiting for transfers between devices, swap(): return lax.ppermute(x, axis, [(i, i ^ s) for i in range(size)])  4.24 us
    ppermute x1, starting transfers between devices, on_small_mesh(): first = lax.ppermute(own, 'layer', ring)  4.09 us
    ppermute x2, waiting for transfers between devices, on_small_mesh(): lax.ppermute(own, ('row', 'col', 'layer'), [(8 * r + 4 * c + z, 8 * r + 4...  4.05 us
    ppermute x1, starting transfers between devices, on_small_mesh(): far = lax.ppermute(first, 'layer', ring)  3.38 us
    ppermute x1, waiting for transfers between devices, on_small_mesh(): far = lax.ppermute(first, 'layer', ring)  2.92 us
    ppermute x1, waiting for transfers between devices, on_small_mesh(): first = lax.ppermute(own, 'layer', ring)  2.86 us
    ppermute x2, starting transfers between devices, on_small_mesh(): lax.ppermute(own, ('row', 'col', 'layer'), [(8 * r + 4 * c + z, 8 * r + 4...  1.49 us
  transfers between devices with their start and end apart: 13, of which 8 were waited for; matrix products, arithmetic and copies ran while one was open for 1% of the time, Pallas kernels for 2%

profile of v9, /device:TPU:0, one launch (start us, length us, event | category | flops | bytes accessed | tf_op | source)
XLA Modules:
  0.0 32.8 jit_solution(12496217492213654147)
XLA Ops:
  0.0 0.7 %convert_element_type.12 = f32[4,2]{0,1:T(2,128)S(1)} convert(s32[4,2]{0,1:T(2,128)} %param.5) | non-fusion elementwise | flops 8 | bytes 64 | tf_op jit(solution)/shard_map/convert_element_type | solution.py:94
  0.8 0.2 mul.22
  1.2 4.1 %collective-permute-start.4 = (bf16[512,256]{1,0:T(8,128)(2,1)S(1)}, bf16[512,256]{1,0:T(8,128)(2,1)S(1)}, u32[]{:S(2)}, u32[]{:S(2)}) collective-permute-start(bf16[512,256]{1,0:T(8,128)(2,1)S(1)} %fusion.refs_0_.refs_4_), channel_id=1, source_target_pairs={{0,2},{2,3},{3,1},{1,0},{4,6},{6,7},{7,5},{5,4},{8,10},{10,11},{11... | collective-permute-start | bytes 786440 | tf_op jit(solution)/shard_map/ppermute | solution.py:96
  5.3 1.5 %collective-permute-start.2 = (bf16[512,256]{1,0:T(8,128)(2,1)S(1)}, bf16[512,256]{1,0:T(8,128)(2,1)S(1)}, u32[]{:S(2)}, u32[]{:S(2)}) collective-permute-start(bf16[512,256]{1,0:T(8,128)(2,1)S(1)} %fusion.refs_0_.refs_4_), channel_id=1, source_target_pairs={{0,8},{1,9},{2,10},{3,11},{4,5},{5,7},{6,4},{7,6},{8,0},{9,1},{10,... | collective-permute-start | bytes 786440 | tf_op jit(solution)/shard_map/ppermute | solution.py:99
  6.7 1.5 %collective-permute-start.1 = (bf16[512,256]{1,0:T(8,128)(2,1)S(1)}, bf16[512,256]{1,0:T(8,128)(2,1)S(1)}, u32[]{:S(2)}, u32[]{:S(2)}) collective-permute-start(bf16[512,256]{1,0:T(8,128)(2,1)S(1)} %fusion.refs_0_.refs_4_), channel_id=1, source_target_pairs={{0,16},{8,24},{16,0},{24,8},{1,17},{9,25},{17,1},{25,9},{2,18},{10... | collective-permute-start | bytes 786440 | tf_op jit(solution)/shard_map/ppermute | solution.py:74
  8.3 0.5 %collective-permute-start = (bf16[512,256]{1,0:T(8,128)(2,1)S(1)}, bf16[512,256]{1,0:T(8,128)(2,1)S(1)}, u32[]{:S(2)}, u32[]{:S(2)}) collective-permute-start(bf16[512,256]{1,0:T(8,128)(2,1)S(1)} %fusion.refs_0_.refs_4_), channel_id=1, source_target_pairs={{0,24},{8,16},{16,8},{24,0},{1,25},{9,17},{17,9},{25,1},{2,26},{10... | collective-permute-start | bytes 786440 | tf_op jit(solution)/shard_map/ppermute | solution.py:74
  8.8 0.1 copy.6
  8.8 0.2 mul.25
  9.1 2.9 %collective-permute-done.4.refs_5_ = bf16[512,256]{1,0:T(8,128)(2,1)S(1)} collective-permute-done((bf16[512,256]{1,0:T(8,128)(2,1)S(1)}, bf16[512,256]{1,0:T(8,128)(2,1)S(1)}, u32[]{:S(2)}, u32[]{:S(2)}) %collective-permute-start.4) | collective-permute-done | bytes 262176 | tf_op jit(solution)/shard_map/ppermute | solution.py:96
  12.0 3.4 %collective-permute-start.5 = (bf16[512,256]{1,0:T(8,128)(2,1)S(1)}, bf16[512,256]{1,0:T(8,128)(2,1)S(1)}, u32[]{:S(2)}, u32[]{:S(2)}) collective-permute-start(bf16[512,256]{1,0:T(8,128)(2,1)S(1)} %collective-permute-done.4.refs_5_), channel_id=1, source_target_pairs={{0,2},{2,3},{3,1},{1,0},{4,6},{6,7},{7,5},{5,4},{8,10},{10,11},{11... | collective-permute-start | bytes 786440 | tf_op jit(solution)/shard_map/ppermute | solution.py:114
  15.4 4.0 %collective-permute-done.3 = bf16[512,256]{1,0:T(8,128)(2,1)S(1)} collective-permute-done((bf16[512,256]{1,0:T(8,128)(2,1)S(1)}, bf16[512,256]{1,0:T(8,128)(2,1)S(1)}, u32[]{:S(2)}, u32[]{:S(2)}) %collective-permute-start.3) | collective-permute-done | bytes 262176 | tf_op jit(solution)/shard_map/ppermute | solution.py:99
  19.4 0.4 %collective-permute-done.1.refs_2_ = bf16[512,256]{1,0:T(8,128)(2,1)S(1)} collective-permute-done((bf16[512,256]{1,0:T(8,128)(2,1)S(1)}, bf16[512,256]{1,0:T(8,128)(2,1)S(1)}, u32[]{:S(2)}, u32[]{:S(2)}) %collective-permute-start.1) | collective-permute-done | bytes 262176 | tf_op jit(solution)/shard_map/ppermute | solution.py:74
  20.0 0.5 %collective-permute-start.6 = (bf16[512,256]{1,0:T(8,128)(2,1)S(1)}, bf16[512,256]{1,0:T(8,128)(2,1)S(1)}, u32[]{:S(2)}, u32[]{:S(2)}) collective-permute-start(bf16[512,256]{1,0:T(8,128)(2,1)S(1)} %fusion.refs_0_.refs_4_), channel_id=1, source_target_pairs={{0,4},{4,0},{1,5},{5,1},{2,6},{6,2},{3,7},{7,3},{8,12},{12,8},{9,1... | collective-permute-start | bytes 786440 | tf_op jit(solution)/shard_map/ppermute | solution.py:74
  20.6 2.9 %collective-permute-done.5.refs_7_ = bf16[512,256]{1,0:T(8,128)(2,1)S(1)} collective-permute-done((bf16[512,256]{1,0:T(8,128)(2,1)S(1)}, bf16[512,256]{1,0:T(8,128)(2,1)S(1)}, u32[]{:S(2)}, u32[]{:S(2)}) %collective-permute-start.5) | collective-permute-done | bytes 262176 | tf_op jit(solution)/shard_map/ppermute | solution.py:114
  23.6 0.7 %shard_map.46 = (f32[512,256]{1,0:T(8,128)S(1)}, bf16[256,256]{1,0:T(8,128)(2,1)S(1)}) custom-call(bf16[512,256]{1,0:T(8,128)(2,1)S(1)} %fusion.refs_0_.refs_4_, bf16[512,256]{1,0:T(8,128)(2,1)S(1)} %get-tuple-element.40.refs_1_, bf16[512,256]{1,0:T(8,128)(2,1)S(1)} %collective-permute-done.1.refs_2_, bf16[512,256]{1,0:T(8,128)(2,1)S(1)} %collective-permute-done.refs_3_, ...), custom_call_target="tpu_custom_call" | custom-call | flops 402653184 | bytes 2621440 | tf_op jit(solution)/shard_map/pallas_call | solution.py:123
  24.3 0.8 %collective-permute-done.9.left_ref = bf16[512,256]{1,0:T(8,128)(2,1)S(1)} collective-permute-done((bf16[512,256]{1,0:T(8,128)(2,1)S(1)}, bf16[512,256]{1,0:T(8,128)(2,1)S(1)}, u32[]{:S(2)}, u32[]{:S(2)}) %collective-permute-start.9) | collective-permute-done | bytes 262176 | tf_op jit(solution)/shard_map/ppermute | solution.py:74
  25.1 0.2 shard_map.47
  25.3 2.5 %collective-permute-start.12 = (f32[1,256]{1,0:T(1,128)S(1)}, f32[1,256]{1,0:T(1,128)S(1)}, u32[]{:S(2)}, u32[]{:S(2)}) collective-permute-start(f32[1,256]{1,0:T(1,128)S(1)} %get-tuple-element.38.refs_0_), channel_id=1, source_target_pairs={{0,24},{8,16},{16,8},{24,0},{1,25},{9,17},{17,9},{25,1},{2,26},{10... | collective-permute-start | bytes 3080 | tf_op jit(solution)/shard_map/ppermute | solution.py:74
  27.9 0.5 %collective-permute-start.11 = (f32[1,256]{1,0:T(1,128)S(1)}, f32[1,256]{1,0:T(1,128)S(1)}, u32[]{:S(2)}, u32[]{:S(2)}) collective-permute-start(f32[1,256]{1,0:T(1,128)S(1)} %get-tuple-element.38.refs_0_), channel_id=1, source_target_pairs={{0,16},{8,24},{16,0},{24,8},{1,17},{9,25},{17,1},{25,9},{2,18},{10... | collective-permute-start | bytes 3080 | tf_op jit(solution)/shard_map/ppermute | solution.py:74
  28.4 0.5 %collective-permute-start.10 = (f32[1,256]{1,0:T(1,128)S(1)}, f32[1,256]{1,0:T(1,128)S(1)}, u32[]{:S(2)}, u32[]{:S(2)}) collective-permute-start(f32[1,256]{1,0:T(1,128)S(1)} %get-tuple-element.38.refs_0_), channel_id=1, source_target_pairs={{0,8},{8,0},{16,24},{24,16},{1,9},{9,1},{17,25},{25,17},{2,10},{10... | collective-permute-start | bytes 3080 | tf_op jit(solution)/shard_map/ppermute | solution.py:74
  28.9 1.0 %collective-permute-done.12.refs_3_ = f32[1,256]{1,0:T(1,128)S(1)} collective-permute-done((f32[1,256]{1,0:T(1,128)S(1)}, f32[1,256]{1,0:T(1,128)S(1)}, u32[]{:S(2)}, u32[]{:S(2)}) %collective-permute-start.12) | collective-permute-done | bytes 1056 | tf_op jit(solution)/shard_map/ppermute | solution.py:74
  29.9 1.5 %collective-permute-done.11.refs_2_ = f32[1,256]{1,0:T(1,128)S(1)} collective-permute-done((f32[1,256]{1,0:T(1,128)S(1)}, f32[1,256]{1,0:T(1,128)S(1)}, u32[]{:S(2)}, u32[]{:S(2)}) %collective-permute-start.11) | collective-permute-done | bytes 1056 | tf_op jit(solution)/shard_map/ppermute | solution.py:74
  31.4 0.5 %collective-permute-done.10.refs_1_ = f32[1,256]{1,0:T(1,128)S(1)} collective-permute-done((f32[1,256]{1,0:T(1,128)S(1)}, f32[1,256]{1,0:T(1,128)S(1)}, u32[]{:S(2)}, u32[]{:S(2)}) %collective-permute-start.10) | collective-permute-done | bytes 1056 | tf_op jit(solution)/shard_map/ppermute | solution.py:74
  31.9 0.8 %shard_map.48 = f32[512,256]{1,0:T(8,128)} custom-call(f32[512,256]{1,0:T(8,128)S(1)} %get-tuple-element.37.squares_ref, f32[1,256]{1,0:T(1,128)S(1)} %get-tuple-element.38.refs_0_, f32[1,256]{1,0:T(1,128)S(1)} %collective-permute-done.10.refs_1_, f32[1,256]{1,0:T(1,128)S(1)} %collective-permute-done.11.refs_2_, f32[1,256]{1,0:T(1,128)S(1)} %collective-permute-done.12.refs_3_), custom_call_target="tpu_custom_call" | custom-call | flops 524288 | bytes 1048576 | tf_op jit(solution)/shard_map/pallas_call | solution.py:139
  (20 shorter events, 0.5 us)
Async XLA Ops:
  0.0 1.1 %copy-start.1 = (f32[512,256]{1,0:T(8,128)S(1)}, f32[512,256]{1,0:T(8,128)}, u32[]{:S(2)}) copy-start(f32[512,256]{1,0:T(8,128)} %param.4) | copy-start | bytes 1572868
  1.1 7.7 %copy-start.2 = (s32[4,2]{0,1:T(2,128)S(1)}, s32[4,2]{0,1:T(2,128)}, u32[]{:S(2)}) copy-start(s32[4,2]{0,1:T(2,128)} %param.6) | copy-start | bytes 100
  1.2 7.9 %copy-start = (s32[512,256]{1,0:T(8,128)S(1)}, s32[512,256]{1,0:T(8,128)}, u32[]{:S(2)}) copy-start(s32[512,256]{1,0:T(8,128)} %param.7) | copy-start | bytes 1572868
  1.2 10.8 %collective-permute-start.4 = (bf16[512,256]{1,0:T(8,128)(2,1)S(1)}, bf16[512,256]{1,0:T(8,128)(2,1)S(1)}, u32[]{:S(2)}, u32[]{:S(2)}) collective-permute-start(bf16[512,256]{1,0:T(8,128)(2,1)S(1)} %fusion.refs_0_.refs_4_), channel_id=1, source_target_pairs={{0,2},{2,3},{3,1},{1,0},{4,6},{6,7},{7,5},{5,4},{8,10},{10,11},{11... | collective-permute-start | bytes 786440 | tf_op jit(solution)/shard_map/ppermute | solution.py:96
  5.3 14.2 %collective-permute-start.3 = (bf16[512,256]{1,0:T(8,128)(2,1)S(1)}, bf16[512,256]{1,0:T(8,128)(2,1)S(1)}, u32[]{:S(2)}, u32[]{:S(2)}) collective-permute-start(bf16[512,256]{1,0:T(8,128)(2,1)S(1)} %fusion.refs_0_.refs_4_), channel_id=1, source_target_pairs={{0,1},{1,3},{2,0},{3,2},{4,12},{5,13},{6,14},{7,15},{8,9},{9,11},{... | collective-permute-start | bytes 786440 | tf_op jit(solution)/shard_map/ppermute | solution.py:99
  5.3 14.2 %collective-permute-start.2 = (bf16[512,256]{1,0:T(8,128)(2,1)S(1)}, bf16[512,256]{1,0:T(8,128)(2,1)S(1)}, u32[]{:S(2)}, u32[]{:S(2)}) collective-permute-start(bf16[512,256]{1,0:T(8,128)(2,1)S(1)} %fusion.refs_0_.refs_4_), channel_id=1, source_target_pairs={{0,8},{1,9},{2,10},{3,11},{4,5},{5,7},{6,4},{7,6},{8,0},{9,1},{10,... | collective-permute-start | bytes 786440 | tf_op jit(solution)/shard_map/ppermute | solution.py:99
  6.7 13.1 %collective-permute-start.1 = (bf16[512,256]{1,0:T(8,128)(2,1)S(1)}, bf16[512,256]{1,0:T(8,128)(2,1)S(1)}, u32[]{:S(2)}, u32[]{:S(2)}) collective-permute-start(bf16[512,256]{1,0:T(8,128)(2,1)S(1)} %fusion.refs_0_.refs_4_), channel_id=1, source_target_pairs={{0,16},{8,24},{16,0},{24,8},{1,17},{9,25},{17,1},{25,9},{2,18},{10... | collective-permute-start | bytes 786440 | tf_op jit(solution)/shard_map/ppermute | solution.py:74
  8.3 11.6 %collective-permute-start = (bf16[512,256]{1,0:T(8,128)(2,1)S(1)}, bf16[512,256]{1,0:T(8,128)(2,1)S(1)}, u32[]{:S(2)}, u32[]{:S(2)}) collective-permute-start(bf16[512,256]{1,0:T(8,128)(2,1)S(1)} %fusion.refs_0_.refs_4_), channel_id=1, source_target_pairs={{0,24},{8,16},{16,8},{24,0},{1,25},{9,17},{17,9},{25,1},{2,26},{10... | collective-permute-start | bytes 786440 | tf_op jit(solution)/shard_map/ppermute | solution.py:74
  12.0 11.5 %collective-permute-start.5 = (bf16[512,256]{1,0:T(8,128)(2,1)S(1)}, bf16[512,256]{1,0:T(8,128)(2,1)S(1)}, u32[]{:S(2)}, u32[]{:S(2)}) collective-permute-start(bf16[512,256]{1,0:T(8,128)(2,1)S(1)} %collective-permute-done.4.refs_5_), channel_id=1, source_target_pairs={{0,2},{2,3},{3,1},{1,0},{4,6},{6,7},{7,5},{5,4},{8,10},{10,11},{11... | collective-permute-start | bytes 786440 | tf_op jit(solution)/shard_map/ppermute | solution.py:114
  19.9 3.6 %collective-permute-start.8 = (bf16[512,256]{1,0:T(8,128)(2,1)S(1)}, bf16[512,256]{1,0:T(8,128)(2,1)S(1)}, u32[]{:S(2)}, u32[]{:S(2)}) collective-permute-start(bf16[512,256]{1,0:T(8,128)(2,1)S(1)} %get-tuple-element.39.refs_6_), channel_id=1, source_target_pairs={{0,4},{4,0},{1,5},{5,1},{2,6},{6,2},{3,7},{7,3},{8,12},{12,8},{9,1... | collective-permute-start | bytes 786440 | tf_op jit(solution)/shard_map/ppermute | solution.py:74
  20.0 3.5 %collective-permute-start.6 = (bf16[512,256]{1,0:T(8,128)(2,1)S(1)}, bf16[512,256]{1,0:T(8,128)(2,1)S(1)}, u32[]{:S(2)}, u32[]{:S(2)}) collective-permute-start(bf16[512,256]{1,0:T(8,128)(2,1)S(1)} %fusion.refs_0_.refs_4_), channel_id=1, source_target_pairs={{0,4},{4,0},{1,5},{5,1},{2,6},{6,2},{3,7},{7,3},{8,12},{12,8},{9,1... | collective-permute-start | bytes 786440 | tf_op jit(solution)/shard_map/ppermute | solution.py:74
  20.5 3.0 %collective-permute-start.7 = (bf16[512,256]{1,0:T(8,128)(2,1)S(1)}, bf16[512,256]{1,0:T(8,128)(2,1)S(1)}, u32[]{:S(2)}, u32[]{:S(2)}) collective-permute-start(bf16[512,256]{1,0:T(8,128)(2,1)S(1)} %collective-permute-done.4.refs_5_), channel_id=1, source_target_pairs={{0,4},{4,0},{1,5},{5,1},{2,6},{6,2},{3,7},{7,3},{8,12},{12,8},{9,1... | collective-permute-start | bytes 786440 | tf_op jit(solution)/shard_map/ppermute | solution.py:74
  23.5 1.6 %collective-permute-start.9 = (bf16[512,256]{1,0:T(8,128)(2,1)S(1)}, bf16[512,256]{1,0:T(8,128)(2,1)S(1)}, u32[]{:S(2)}, u32[]{:S(2)}) collective-permute-start(bf16[512,256]{1,0:T(8,128)(2,1)S(1)} %collective-permute-done.5.refs_7_), channel_id=1, source_target_pairs={{0,4},{4,0},{1,5},{5,1},{2,6},{6,2},{3,7},{7,3},{8,12},{12,8},{9,1... | collective-permute-start | bytes 786440 | tf_op jit(solution)/shard_map/ppermute | solution.py:74
  25.3 4.5 %collective-permute-start.12 = (f32[1,256]{1,0:T(1,128)S(1)}, f32[1,256]{1,0:T(1,128)S(1)}, u32[]{:S(2)}, u32[]{:S(2)}) collective-permute-start(f32[1,256]{1,0:T(1,128)S(1)} %get-tuple-element.38.refs_0_), channel_id=1, source_target_pairs={{0,24},{8,16},{16,8},{24,0},{1,25},{9,17},{17,9},{25,1},{2,26},{10... | collective-permute-start | bytes 3080 | tf_op jit(solution)/shard_map/ppermute | solution.py:74
  27.9 3.6 %collective-permute-start.11 = (f32[1,256]{1,0:T(1,128)S(1)}, f32[1,256]{1,0:T(1,128)S(1)}, u32[]{:S(2)}, u32[]{:S(2)}) collective-permute-start(f32[1,256]{1,0:T(1,128)S(1)} %get-tuple-element.38.refs_0_), channel_id=1, source_target_pairs={{0,16},{8,24},{16,0},{24,8},{1,17},{9,25},{17,1},{25,9},{2,18},{10... | collective-permute-start | bytes 3080 | tf_op jit(solution)/shard_map/ppermute | solution.py:74
  28.4 3.6 %collective-permute-start.10 = (f32[1,256]{1,0:T(1,128)S(1)}, f32[1,256]{1,0:T(1,128)S(1)}, u32[]{:S(2)}, u32[]{:S(2)}) collective-permute-start(f32[1,256]{1,0:T(1,128)S(1)} %get-tuple-element.38.refs_0_), channel_id=1, source_target_pairs={{0,8},{8,0},{16,24},{24,16},{1,9},{9,1},{17,25},{25,17},{2,10},{10... | collective-permute-start | bytes 3080 | tf_op jit(solution)/shard_map/ppermute | solution.py:74
